TPU v7x, 512 devices: a whole 4x4x16 slice. The times are simulated.
512 devices in a mesh: sec: 32 (over z, core), bond: 16 (over y, x).
Axes of the slice: x: 4, y: 4, z: 16, core: 2. Of those that a mesh axis runs over, the one named last changes fastest.
Arguments:
- left_env: bfloat16 [32, 512, 8, 512], P('sec', 'bond'), may hold values from -6 to 6
- site: bfloat16 [32, 512, 4, 512], P('sec', 'bond'), may hold values from -0.125 to 0.125
- psi: bfloat16 [32, 512, 4, 4, 512], P('sec', 'bond'), may hold values from -0.25 to 0.25
- right_env: bfloat16 [32, 8, 512, 512], P('sec'), may hold values from -0.09375 to 0.09375
- mpo: bfloat16 [8, 8, 4, 4], replicated, may hold values from -1 to 1
Outputs:
- new_left: bfloat16 [32, 512, 8, 512], P('sec', 'bond')
- product: bfloat16 [32, 512, 4, 4, 512], P('sec', 'bond')
All inputs are finite; a program needn't handle non-finite values.
Results may differ from a plain program's by a relative error of at most 0.0095.
Values may be sent and summed in bfloat16 or wider, within the bound.
No kernel may reach another device: no remote copies, remote signals or barrier semaphores. Data moves between devices by JAX's collectives and lax.ppermute only.
A program may use at most 64 MiB of HBM per device.

v0:
```python
import jax
import jax.numpy as jnp
from jax import lax
from jax.sharding import PartitionSpec as P


def shifted(block, axis, distance):
    devices = range(lax.axis_size(axis))
    route = [((i - distance) % len(devices), i) for i in devices]
    return lax.ppermute(block, axis, route)


def shards(left_env, site, psi, right_env, mpo):
    left = left_env[0]
    tensor = site[0]
    rows = tensor.shape[0]
    phys = tensor.shape[1]
    chi = tensor.shape[2]
    width = left.shape[1]
    pair_source = shifted(psi[0], "sec", 1)
    offset = lax.axis_index("bond") * rows
    whole_left, whole_site = (
        lax.all_gather(left, "bond", axis=0, tiled=True),
        lax.all_gather(tensor, "bond", axis=0, tiled=True),
    )
    own_cols = lax.dynamic_slice_in_dim(whole_site, offset, rows, 2)
    first = jnp.dot(
        whole_left.reshape(chi * width, chi),
        own_cols.reshape(chi, phys * rows),
        preferred_element_type=jnp.float32,
    )
    first = first.astype(jnp.bfloat16).reshape(chi, width, phys, rows)
    second = jnp.einsum("pmsb,mnsu->punb", first, mpo, preferred_element_type=jnp.float32).astype(
        jnp.bfloat16
    )
    fresh = lax.dot_general(
        whole_site.reshape(chi * phys, chi),
        second.reshape(chi * phys, width * rows),
        (((0,), (0,)), ((), ())),
        preferred_element_type=jnp.float32,
    )
    fresh = fresh.astype(jnp.bfloat16).reshape(chi, width, rows)
    new_left = lax.all_to_all(fresh, "bond", split_axis=0, concat_axis=2, tiled=True)
    left_source = shifted(new_left, "sec", 1)
    source_flat = left_source.reshape(rows * width, chi)
    pair = pair_source.reshape(rows, phys * phys * chi)
    mixed = jnp.dot(
        source_flat,
        lax.all_gather(pair, "bond", axis=0, tiled=True),
        preferred_element_type=jnp.float32,
    )
    mixed = mixed.astype(jnp.bfloat16).reshape(rows, width * phys * phys, chi)
    two_site = jnp.einsum("mnsu,nkvw->msvuwk", mpo, mpo, preferred_element_type=jnp.float32)
    two_site = two_site.astype(jnp.bfloat16).reshape(width * phys * phys, phys * phys * width)
    projected = jnp.einsum(
        "pqc,qr->prc", mixed, two_site, preferred_element_type=jnp.float32
    ).astype(jnp.bfloat16)
    env_right = right_env[0].reshape(width * chi, chi)
    result = jnp.dot(
        projected.reshape(rows * phys * phys, width * chi),
        env_right,
        preferred_element_type=jnp.float32,
    ).astype(jnp.bfloat16)
    return (new_left[None], result.reshape(1, rows, phys, phys, chi))


def solution(mesh):
    in_specs = (
        P("sec", "bond", None, None),
        P("sec", "bond", None, None),
        P("sec", "bond", None, None, None),
        P("sec", None, None, None),
        P(),
    )
    out_specs = (P("sec", "bond", None, None), P("sec", "bond", None, None, None))
    return jax.shard_map(shards, mesh=mesh, in_specs=in_specs, out_specs=out_specs, check_vma=False)
```

profile of v0, /device:TPU:1, one launch (start us, length us, event | category | flops | bytes accessed | tf_op | source)
XLA Modules:
  0.0 276.7 jit_solution(3635646627741291133)
XLA Ops:
  7.2 0.7 all-gather.8.cloned.1.call-update
  7.9 0.7 all-gather.10.cloned.1.call-update
  8.7 3.0 %collective-permute-start.1 = (bf16[32,4,4,512]{3,2,1,0:T(4,128)(2,1)}, bf16[32,4,4,512]{3,2,1,0:T(4,128)(2,1)S(1)}, u32[]{:S(2)}, u32[]{:S(2)}) collective-permute-start(bf16[32,4,4,512]{3,2,1,0:T(4,128)(2,1)} %bitcast.69), channel_id=1, source_target_pairs={{496,0},{0,16},{16,32},{32,48},{48,64},{64,80},{80,96},{96,112},{1... | collective-permute-start | bytes 1572872 | tf_op jit(solution)/shard_map/ppermute | solution.py:10
  11.7 6.4 %collective-permute-done.1 = bf16[32,4,4,512]{3,2,1,0:T(4,128)(2,1)S(1)} collective-permute-done((bf16[32,4,4,512]{3,2,1,0:T(4,128)(2,1)}, bf16[32,4,4,512]{3,2,1,0:T(4,128)(2,1)S(1)}, u32[]{:S(2)}, u32[]{:S(2)}) %collective-permute-start.1) | collective-permute-done | bytes 524320 | tf_op jit(solution)/shard_map/ppermute | solution.py:10
  18.2 1.2 reshape.49
  19.4 0.9 copy.51
  20.2 55.5 %all-gather.8.cloned.1.call-done = bf16[1,512,4,512]{3,2,0,1:T(4,128)(2,1)} async-done(((bf16[1,32,4,512]{3,2,0,1:T(4,128)(2,1)}), bf16[1,512,4,512]{3,2,0,1:T(4,128)(2,1)}) %all-gather.8.cloned.1.call-update) | async-done | bytes 2097168 | tf_op jit(solution)/shard_map/all_gather | solution.py:24
  75.8 1.4 constant_dynamic-slice_fusion
  77.4 4.0 %reshape.45 = bf16[2048,512]{1,0:T(8,128)(2,1)} reshape(bf16[1,512,4,512]{3,2,0,1:T(4,128)(2,1)} %all-gather.8.cloned.1.call-done) | data formatting | bytes 4194304 | tf_op jit(solution)/shard_map/reshape | solution.py:37
  81.4 64.5 %all-gather.10.cloned.1.call-done = bf16[1,512,8,512]{3,2,0,1:T(8,128)(2,1)} async-done(((bf16[1,32,8,512]{3,2,0,1:T(8,128)(2,1)}), bf16[1,512,8,512]{3,2,0,1:T(8,128)(2,1)}) %all-gather.10.cloned.1.call-update) | async-done | bytes 4194320 | tf_op jit(solution)/shard_map/all_gather | solution.py:23
  145.9 3.7 %fusion = bf16[4096,128]{0,1:T(8,128)(2,1)S(1)} fusion(bf16[512,128]{0,1:T(8,128)(2,1)S(1)} %bitcast.63, bf16[1,512,8,512]{3,2,0,1:T(8,128)(2,1)} %all-gather.10.cloned.1.call-done), kind=kOutput, calls=%fused_computation.2 | convolution fusion | flops 537395200 | bytes 5373952 | tf_op jit(solution)/shard_map/dot_general | solution.py:27
  149.6 0.7 copy.49
  150.3 3.3 %reshape.43 = bf16[512,8,4,32]{3,2,1,0:T(4,128)(2,1)} reshape(bf16[4096,128]{1,0:T(8,128)(2,1)S(1)} %copy.49) | data formatting | bytes 2097152 | tf_op jit(solution)/shard_map/reshape | solution.py:32
  153.6 6.8 %copy.59 = bf16[512,8,4,32,1]{0,1,2,4,3:T(8,128)(2,1)S(1)} copy(bf16[512,8,4,32,1]{3,2,1,0,4:T(4,128)(2,1)} %bitcast.59) | data formatting | bytes 2097152 | tf_op jit(solution)/shard_map/reshape | solution.py:32
  160.9 6.8 %copy.52 = bf16[512,4,8,32]{3,2,1,0:T(8,128)(2,1)} copy(bf16[512,4,8,32]{0,2,1,3:T(8,128)(2,1)S(1)} %fusion.2) | data formatting | bytes 2097152 | tf_op jit(solution)/shard_map/convert_element_type | solution.py:33
  167.7 5.4 %reshape.44 = bf16[2048,256]{1,0:T(8,128)(2,1)S(1)} reshape(bf16[512,4,8,32]{3,2,1,0:T(8,128)(2,1)} %copy.52) | data formatting | bytes 2097152 | tf_op jit(solution)/shard_map/reshape | solution.py:38
  173.2 0.7 convolution_convert_fusion.4
  173.9 0.8 copy.53
  174.7 1.0 reshape.65
  175.7 12.4 %all_to_all.18 = bf16[16,2,4096]{2,1,0:T(2,128)(2,1)S(1)} all-to-all(bf16[16,2,4096]{2,1,0:T(2,128)(2,1)S(1)} %reshape.65), channel_id=1, replica_groups=mesh['sec'=32,'bond'=16] {'bond'}, dimensions={0} | all-to-all | bytes 524288 | tf_op jit(solution)/shard_map/all_to_all | solution.py:43
  188.6 1.2 copy.77
  189.8 1.0 all_to_all.16
  190.8 3.3 %collective-permute-start = (bf16[32,8,512]{2,1,0:T(8,128)(2,1)S(1)}, bf16[32,8,512]{2,1,0:T(8,128)(2,1)S(1)}, u32[]{:S(2)}, u32[]{:S(2)}) collective-permute-start(bf16[32,8,512]{2,1,0:T(8,128)(2,1)S(1)} %all_to_all.16), channel_id=1, source_target_pairs={{496,0},{0,16},{16,32},{32,48},{48,64},{64,80},{80,96},{96,112},{1... | collective-permute-start | bytes 786440 | tf_op jit(solution)/shard_map/ppermute | solution.py:10
  194.4 0.9 copy.57
  195.9 1.7 broadcast_in_dim.3
  197.6 38.0 %all-gather.6.cloned.1.call-done = bf16[512,8192]{1,0:T(8,128)(2,1)} async-done(((bf16[32,8192]{1,0:T(8,128)(2,1)}), bf16[512,8192]{1,0:T(8,128)(2,1)}) %all-gather.6.cloned.1.call-update) | async-done | bytes 8388624 | tf_op jit(solution)/shard_map/all_gather | solution.py:49
  235.6 7.7 %convolution_convert_fusion = bf16[256,8192]{1,0:T(8,128)(2,1)} fusion(bf16[512,8192]{1,0:T(8,128)(2,1)} %all-gather.6.cloned.1.call-done, bf16[32,8,512]{2,1,0:T(8,128)(2,1)S(1)} %collective-permute-done), kind=kOutput, calls=%fused_computation | convolution fusion | flops 2149580800 | bytes 12845056 | tf_op jit(solution)/shard_map/dot_general | solution.py:47
  243.3 7.4 %reshape.50 = bf16[32,128,512]{2,1,0:T(8,128)(2,1)} reshape(bf16[256,8192]{1,0:T(8,128)(2,1)} %convolution_convert_fusion) | data formatting | bytes 8388608 | tf_op jit(solution)/shard_map/reshape | solution.py:52
  250.7 5.4 %convert_bitcast_fusion = bf16[32,128,512]{2,1,0:T(8,128)(2,1)} fusion(bf16[32,128,512]{2,1,0:T(8,128)(2,1)} %reshape.50, bf16[128,128]{1,0:T(8,128)(2,1)S(1)} %reshape.47), kind=kOutput, calls=%fused_computation.4 | convolution fusion | flops 538968064 | bytes 8421376 | tf_op jit(solution)/shard_map/pqc,qr->prc/dot_general | solution.py:55
  256.1 7.4 %reshape.51 = bf16[512,4096]{1,0:T(8,128)(2,1)} reshape(bf16[32,128,512]{2,1,0:T(8,128)(2,1)} %convert_bitcast_fusion) | data formatting | bytes 8388608 | tf_op jit(solution)/shard_map/reshape | solution.py:60
  263.5 5.8 %convolution_convert_fusion.2 = bf16[512,512]{1,0:T(8,128)(2,1)S(1)} fusion(bf16[512,4096]{1,0:T(8,128)(2,1)} %reshape.51, bf16[4096,512]{1,0:T(8,128)(2,1)} %bitcast.68), kind=kOutput, calls=%fused_computation.7 | convolution fusion | flops 2147745792 | bytes 8912896 | tf_op jit(solution)/shard_map/dot_general | solution.py:59
  269.3 0.9 reshape.52
  (14 shorter events, 2.3 us)
Async XLA Ops:
  7.2 68.6 %all-gather.8.cloned.1.call-start = ((), (), s32[]{:S(2)}) async-start(), calls=%async_computation.2 | async-start | bytes 2228224 | tf_op jit(solution)/shard_map/all_gather | solution.py:24
  7.9 138.0 %all-gather.10.cloned.1.call-start = ((), (), s32[]{:S(2)}) async-start(), calls=%async_computation.3 | async-start | bytes 4456448 | tf_op jit(solution)/shard_map/all_gather | solution.py:23
  8.6 226.9 %all-gather.6.cloned.1.call-start = ((), (), s32[]{:S(2)}) async-start(), calls=%async_computation.1 | async-start | bytes 8912896 | tf_op jit(solution)/shard_map/all_gather | solution.py:49
  8.7 9.5 %collective-permute-start.1 = (bf16[32,4,4,512]{3,2,1,0:T(4,128)(2,1)}, bf16[32,4,4,512]{3,2,1,0:T(4,128)(2,1)S(1)}, u32[]{:S(2)}, u32[]{:S(2)}) collective-permute-start(bf16[32,4,4,512]{3,2,1,0:T(4,128)(2,1)} %bitcast.69), channel_id=1, source_target_pairs={{496,0},{0,16},{16,32},{32,48},{48,64},{64,80},{80,96},{96,112},{1... | collective-permute-start | bytes 1572872 | tf_op jit(solution)/shard_map/ppermute | solution.py:10
  160.9 12.3 %copy-start = (bf16[2048,512]{1,0:T(8,128)(2,1)S(1)}, bf16[2048,512]{1,0:T(8,128)(2,1)}, u32[]{:S(2)}) copy-start(bf16[2048,512]{1,0:T(8,128)(2,1)} %reshape.45) | copy-start | bytes 6291460
  173.9 20.2 %copy-start.1 = (bf16[8,8,4,4]{1,3,2,0:T(4,128)(2,1)S(1)}, bf16[8,8,4,4]{1,3,2,0:T(4,128)(2,1)}, u32[]{:S(2)}) copy-start(bf16[8,8,4,4]{1,3,2,0:T(4,128)(2,1)} %param.9) | copy-start | bytes 6148
  190.8 6.8 %collective-permute-start = (bf16[32,8,512]{2,1,0:T(8,128)(2,1)S(1)}, bf16[32,8,512]{2,1,0:T(8,128)(2,1)S(1)}, u32[]{:S(2)}, u32[]{:S(2)}) collective-permute-start(bf16[32,8,512]{2,1,0:T(8,128)(2,1)S(1)} %all_to_all.16), channel_id=1, source_target_pairs={{496,0},{0,16},{16,32},{32,48},{48,64},{64,80},{80,96},{96,112},{1... | collective-permute-start | bytes 786440 | tf_op jit(solution)/shard_map/ppermute | solution.py:10
Sparse Core Ops, SparseCore 0:
  11.0 64.6 all-gather.7
  78.8 67.1 all-gather.9
  149.5 86.0 all-gather.5
where the time goes:
time: 278 us; the launch traced here: 277 us
  waiting for transfers between devices  166 us (60%)
  local copies, waits for them, and re-layouts  54.1 us (19%)
  matrix products  24.1 us (9%)
  between operations  13.9 us (5%)
  blocking collectives  12.4 us (4%)
  starting transfers between devices  6.43 us (2%)
    all_gather x1, waiting for transfers between devices, shards(): lax.all_gather(left, 'bond', axis=0, tiled=True)  64.5 us
    all_gather x1, waiting for transfers between devices, shards(): lax.all_gather(tensor, 'bond', axis=0, tiled=True)  55.5 us
    all_gather x1, waiting for transfers between devices, shards(): lax.all_gather(pair, 'bond', axis=0, tiled=True)  38 us
    all_to_all x1, blocking collectives, shards(): lax.all_to_all(fresh, 'bond', split_axis=0, concat_axis=2, tiled=True)  12.4 us
    reshape x2, local copies, waits for them, and re-layouts, shards(): first = first.astype(jnp.bfloat16).reshape(chi, width, phys, rows)  10.1 us
    dot_general x1, matrix products, shards(): jnp.dot(source_flat, lax.all_gather(pair, 'bond', axis=0, tiled=True), pr...  7.69 us
    reshape x1, local copies, waits for them, and re-layouts, shards(): projected.reshape(rows * phys * phys, width * chi)  7.38 us
    reshape x1, local copies, waits for them, and re-layouts, shards(): mixed = mixed.astype(jnp.bfloat16).reshape(rows, width * phys * phys, chi)  7.38 us
  transfers between devices with their start and end apart: 5, of which 4 were waited for; matrix products, arithmetic and copies ran while one was open for 15% of the time, Pallas kernels for 0%

commit v1 on v0

v1 whole, which is shorter than its diff:
```python
import jax
import jax.numpy as jnp
from jax import lax
from jax.experimental import pallas as pl
from jax.experimental.pallas import tpu as pltpu
from jax.sharding import PartitionSpec as P

BF = jnp.bfloat16
F32 = jnp.float32
VM = pl.BlockSpec(memory_space=pltpu.VMEM)


def shifted(block, axis, distance):
    devices = range(lax.axis_size(axis))
    route = [((i - distance) % len(devices), i) for i in devices]
    return lax.ppermute(block, axis, route)


def front(left_a, left_b, cols, kron, site_a, site_b, out, first, second):
    for g, left in enumerate((left_a, left_b)):
        rows = left[...]
        for h in range(2):
            part = []
            for s in (2 * h, 2 * h + 1):
                f = jnp.dot(rows, cols[:, s].reshape(512, 256), preferred_element_type=F32)
                part.append(f.reshape(32, 8, 256))
            first[32 * g : 32 * g + 32, 16 * h : 16 * h + 16, :] = jnp.concatenate(part, axis=1).astype(BF)
    for blk in range(8):
        f = first[8 * blk : 8 * blk + 8].reshape(256, 256)
        o = jnp.dot(kron[...], f, preferred_element_type=F32)
        second[:, 32 * blk : 32 * blk + 32, :] = o.astype(BF).reshape(8, 32, 256)
    site = jnp.concatenate([site_a[...], site_b[...]], axis=0)
    for n in range(8):
        o = lax.dot_general(site, second[n], (((0,), (0,)), ((), ())), preferred_element_type=F32)
        out[:, n] = o.astype(BF).reshape(16, 32, 256)


def back(left, pair, mix, right, out, mixed, proj):
    j = pl.program_id(0)
    m = jnp.dot(left[...], pair[...], preferred_element_type=F32)
    m = jnp.concatenate([m[:, :512].reshape(32, 8, 512), m[:, 512:].reshape(32, 8, 512)], axis=1)
    mixed[:, pl.ds(pl.multiple_of(16 * j, 16), 16), :] = m.astype(BF)

    @pl.when(j == 7)
    def _():
        for p in range(32):
            o = jnp.dot(mix[...], mixed[p], preferred_element_type=F32).astype(BF)
            proj[:, 16 * p : 16 * p + 16, :] = o.reshape(8, 16, 512)
        acc = jnp.dot(proj[0], right[0], preferred_element_type=F32)
        for k in range(1, 8):
            acc += jnp.dot(proj[k], right[k], preferred_element_type=F32)
        out[...] = acc.astype(BF)


def shards(left_env, site, psi, right_env, mpo):
    chi = site.shape[-1]
    pair = shifted(psi[0].reshape(32, 16 * chi), "sec", 1)
    pair = lax.all_gather(pair, "bond", axis=0, tiled=True)
    left = left_env[0].reshape(256, chi)
    tensor = site[0].reshape(128, chi)
    swap = [(i, i ^ 1) for i in range(16)]
    left_b = lax.ppermute(left, "bond", swap)
    tensor_b = lax.ppermute(tensor, "bond", swap)
    halves = site[0].reshape(32, 4, 2, 256).transpose(2, 1, 0, 3)
    send = jnp.broadcast_to(halves[None], (8, 2, 4, 32, 256)).reshape(16, 4, 32, 256)
    cols = lax.all_to_all(send, "bond", 0, 0, tiled=True)
    eye = jnp.eye(8, dtype=BF)
    kron = jnp.einsum("pq,mnsu->npuqsm", eye, mpo).reshape(256, 256)
    fresh = pl.pallas_call(
        front,
        out_shape=jax.ShapeDtypeStruct((16, 8, 32, 256), BF),
        in_specs=[VM] * 6,
        out_specs=VM,
        scratch_shapes=[pltpu.VMEM((64, 32, 256), BF), pltpu.VMEM((8, 256, 256), BF)],
        compiler_params=pltpu.CompilerParams(vmem_limit_bytes=40 << 20),
        cost_estimate=pl.CostEstimate(flops=2_000_000_000, bytes_accessed=5_000_000, transcendentals=0),
        name="front",
    )(left, left_b, cols, kron, tensor, tensor_b)
    fresh = lax.all_to_all(fresh, "bond", 0, 0, tiled=True)
    fresh = jnp.sum(fresh.reshape(8, 2, 8, 32, 256).astype(F32), axis=0).astype(BF)
    new_left = fresh.transpose(2, 1, 0, 3).reshape(32, 8, chi)
    source = shifted(new_left.reshape(256, chi), "sec", 1)
    two_site = jnp.einsum("mnsu,nkvw->kuwsvm", mpo, mpo, preferred_element_type=F32)
    two_site = two_site.astype(BF).reshape(128, 128)
    result = pl.pallas_call(
        back,
        grid=(8,),
        out_shape=jax.ShapeDtypeStruct((512, chi), BF),
        in_specs=[
            pl.BlockSpec((256, 512), lambda j: (0, 0)),
            pl.BlockSpec((512, 1024), lambda j: (0, j)),
            pl.BlockSpec((128, 128), lambda j: (0, 0)),
            pl.BlockSpec((8, 512, 512), lambda j: (0, 0, 0)),
        ],
        out_specs=pl.BlockSpec((512, 512), lambda j: (0, 0)),
        scratch_shapes=[pltpu.VMEM((32, 128, 512), BF), pltpu.VMEM((8, 512, 512), BF)],
        compiler_params=pltpu.CompilerParams(vmem_limit_bytes=48 << 20),
        cost_estimate=pl.CostEstimate(flops=5_000_000_000, bytes_accessed=14_000_000, transcendentals=0),
        name="back",
    )(source, pair, two_site, right_env[0])
    return (new_left[None], result.reshape(1, 32, 4, 4, chi))


def solution(mesh):
    in_specs = (
        P("sec", "bond", None, None),
        P("sec", "bond", None, None),
        P("sec", "bond", None, None, None),
        P("sec", None, None, None),
        P(),
    )
    out_specs = (P("sec", "bond", None, None), P("sec", "bond", None, None, None))
    return jax.shard_map(shards, mesh=mesh, in_specs=in_specs, out_specs=out_specs, check_vma=False)
```

time: 278 us -> 150 us (0.54)
  the two profiles are of different devices: /device:TPU:1 before, /device:TPU:97 now
where the time goes in v1:
time: 150 us; the launch traced here: 149 us
  blocking collectives  48.5 us (32%)
  waiting for transfers between devices  42 us (28%)
  starting transfers between devices  15.5 us (10%)
  between operations  14.2 us (9%)
  local copies, waits for them, and re-layouts  13.8 us (9%)
  Pallas kernels  12.4 us (8%)
  other arithmetic  2.55 us (2%)
    all_to_all x1, blocking collectives, shards(): fresh = lax.all_to_all(fresh, 'bond', 0, 0, tiled=True)  48.5 us
    ppermute x1, waiting for transfers between devices, shards(): tensor_b = lax.ppermute(tensor, 'bond', swap)  19.3 us
    all_gather x1, waiting for transfers between devices, shards(): pair = lax.all_gather(pair, 'bond', axis=0, tiled=True)  12.6 us
    pallas_call x1, Pallas kernels, shards(): pl.pallas_call(back, grid=(8,), out_shape=jax.ShapeDtypeStruct((512, chi)...  10.8 us
    ppermute x2, waiting for transfers between devices, shifted(): return lax.ppermute(block, axis, route)  10.1 us
    all_to_all x1, starting transfers between devices, shards(): cols = lax.all_to_all(send, 'bond', 0, 0, tiled=True)  6.75 us
    reshape x1, local copies, waits for them, and re-layouts, shards(): kron = jnp.einsum('pq,mnsu->npuqsm', eye, mpo).reshape(256, 256)  4.05 us
    ppermute x2, starting transfers between devices, shifted(): return lax.ppermute(block, axis, route)  3.44 us
  transfers between devices with their start and end apart: 6, of which 4 were waited for; matrix products, arithmetic and copies ran while one was open for 8% of the time, Pallas kernels for 1%

profile of v1, /device:TPU:97, one launch (start us, length us, event | category | flops | bytes accessed | tf_op | source)
XLA Modules:
  0.0 149.4 jit_solution(17565583851107167998)
XLA Ops:
  7.2 0.0 all-gather.2.cloned.1.call-start
  7.2 1.4 reshape_squeeze.15
  8.6 3.4 %collective-permute-start.3 = (bf16[32,8192]{1,0:T(8,128)(2,1)S(1)}, bf16[32,8192]{1,0:T(8,128)(2,1)S(1)}, u32[]{:S(2)}, u32[]{:S(2)}) collective-permute-start(bf16[32,8192]{1,0:T(8,128)(2,1)S(1)} %reshape_squeeze.15), channel_id=1, source_target_pairs={{496,0},{0,16},{16,32},{32,48},{48,64},{64,80},{80,96},{96,112},{1... | collective-permute-start | bytes 1572872 | tf_op jit(solution)/shard_map/ppermute | solution.py:16
  12.0 6.1 %collective-permute-done.3 = bf16[32,8192]{1,0:T(8,128)(2,1)S(1)} collective-permute-done((bf16[32,8192]{1,0:T(8,128)(2,1)S(1)}, bf16[32,8192]{1,0:T(8,128)(2,1)S(1)}, u32[]{:S(2)}, u32[]{:S(2)}) %collective-permute-start.3) | collective-permute-done | bytes 524320 | tf_op jit(solution)/shard_map/ppermute | solution.py:16
  18.2 0.8 copy-done.2
  19.0 0.0 all-gather.2.cloned.1.call-update
  19.0 0.0 copy-start.4
  19.0 1.0 reshape_squeeze.13
  20.0 1.1 broadcast_in_dim.2
  21.1 6.8 %all-to-all-start = ((bf16[16,4,32,256]{3,2,1,0:T(8,128)(2,1)}), bf16[16,4,32,256]{3,2,1,0:T(8,128)(2,1)S(1)}, u32[]{:S(2)}, u32[]{:S(2)}) async-start(bf16[16,4,32,256]{3,2,1,0:T(8,128)(2,1)} %bitcast.2), calls=%async_computation | async-start | bytes 2097152 | tf_op jit(solution)/shard_map/all_to_all | solution.py:66
  27.9 3.3 %collective-permute-start = (bf16[256,512]{1,0:T(8,128)(2,1)S(1)}, bf16[256,512]{1,0:T(8,128)(2,1)S(1)}, u32[]{:S(2)}, u32[]{:S(2)}) collective-permute-start(bf16[256,512]{1,0:T(8,128)(2,1)S(1)} %bitcast.17), channel_id=1, source_target_pairs={{0,1},{1,0},{2,3},{3,2},{4,5},{5,4},{6,7},{7,6},{8,9},{9,8},{10,11... | collective-permute-start | bytes 786440 | tf_op jit(solution)/shard_map/ppermute | solution.py:62
  31.2 2.0 %collective-permute-start.1 = (bf16[128,512]{1,0:T(8,128)(2,1)S(1)}, bf16[128,512]{1,0:T(8,128)(2,1)S(1)}, u32[]{:S(2)}, u32[]{:S(2)}) collective-permute-start(bf16[128,512]{1,0:T(8,128)(2,1)S(1)} %reshape_squeeze.14.site_a), channel_id=1, source_target_pairs={{0,1},{1,0},{2,3},{3,2},{4,5},{5,4},{6,7},{7,6},{8,9},{9,8},{10,11... | collective-permute-start | bytes 393224 | tf_op jit(solution)/shard_map/ppermute | solution.py:63
  33.2 0.1 copy.19
  33.4 2.2 %multiply_bitcast_fusion = bf16[8,8,4,8,4,8]{5,4,3,2,1,0:T(4,128)(2,1)} fusion(bf16[8,8,4,4]{0,2,3,1:T(4,128)(2,1)S(1)} %copy.19, bf16[8,8]{1,0:T(8,128)(2,1)S(1)} %fusion.3), kind=kLoop, calls=%fused_computation | loop fusion | flops 65536 | bytes 133248 | tf_op jit(solution)/shard_map/pq,mnsu->npuqsm/transpose | solution.py:68
  35.6 4.1 %reshape.21.kron = bf16[256,256]{1,0:T(8,128)(2,1)S(1)} reshape(bf16[8,8,4,8,4,8]{5,4,3,2,1,0:T(4,128)(2,1)} %multiply_bitcast_fusion) | data formatting | bytes 262144 | tf_op jit(solution)/shard_map/reshape | solution.py:68
  39.6 19.3 %collective-permute-done.1.site_b = bf16[128,512]{1,0:T(8,128)(2,1)S(1)} collective-permute-done((bf16[128,512]{1,0:T(8,128)(2,1)S(1)}, bf16[128,512]{1,0:T(8,128)(2,1)S(1)}, u32[]{:S(2)}, u32[]{:S(2)}) %collective-permute-start.1) | collective-permute-done | bytes 131104 | tf_op jit(solution)/shard_map/ppermute | solution.py:63
  58.9 0.0 collective-permute-done.left_b
  58.9 1.6 %front.1 = bf16[16,8,32,256]{3,2,1,0:T(8,128)(2,1)S(1)} custom-call(bf16[256,512]{1,0:T(8,128)(2,1)S(1)} %bitcast.18, bf16[256,512]{1,0:T(8,128)(2,1)S(1)} %collective-permute-done.left_b, bf16[16,4,32,256]{3,2,1,0:T(8,128)(2,1)S(1)} %all-to-all-done.cols, bf16[256,256]{1,0:T(8,128)(2,1)S(1)} %reshape.21.kron, bf16[128,512]{1,0:T(8,128)(2,1)S(1)} %reshape_squeeze.14.site_a, ...), custom_call_target="tpu_custom_call" | custom-call | flops 2000000000 | bytes 5000000 | tf_op jit(solution)/shard_map/front/pallas_call | solution.py:69
  60.5 48.5 %all_to_all.10 = bf16[16,8,32,256]{3,2,1,0:T(8,128)(2,1)S(1)} all-to-all(bf16[16,8,32,256]{3,2,1,0:T(8,128)(2,1)S(1)} %front.1), channel_id=1, replica_groups=mesh['sec'=32,'bond'=16] {'bond'}, dimensions={0} | all-to-all | bytes 4194304 | tf_op jit(solution)/shard_map/all_to_all | solution.py:79
  109.1 0.4 reduce_sum.12
  109.4 0.2 copy.21
  109.6 0.0 collective-permute-start.2
  109.6 0.3 fusion
  110.0 0.4 copy.24
  110.4 0.5 reshape.23.mix
  110.9 0.3 copy.20
  111.2 0.9 broadcast_in_dim_reshape.3
  112.0 4.0 %collective-permute-done.2.left = bf16[256,512]{1,0:T(8,128)(2,1)S(1)} collective-permute-done((bf16[256,512]{1,0:T(8,128)(2,1)S(1)}, bf16[256,512]{1,0:T(8,128)(2,1)S(1)}, u32[]{:S(2)}, u32[]{:S(2)}) %collective-permute-start.2) | collective-permute-done | bytes 262176 | tf_op jit(solution)/shard_map/ppermute | solution.py:16
  116.1 12.6 %all-gather.2.cloned.1.call-done.pair = bf16[512,8192]{1,0:T(8,128)(2,1)} async-done(((bf16[32,8192]{1,0:T(8,128)(2,1)}), bf16[512,8192]{1,0:T(8,128)(2,1)}) %all-gather.2.cloned.1.call-update) | async-done | bytes 8388624 | tf_op jit(solution)/shard_map/all_gather | solution.py:58
  128.6 2.2 %copy-done = bf16[1,8,512,512]{3,2,1,0:T(8,128)(2,1)S(1)} copy-done((bf16[1,8,512,512]{3,2,1,0:T(8,128)(2,1)S(1)}, bf16[1,8,512,512]{3,2,1,0:T(8,128)(2,1)}, u32[]{:S(2)}) %copy-start) | copy-done | bytes 4194328
  130.8 10.8 %back.1 = bf16[512,512]{1,0:T(8,128)(2,1)S(1)} custom-call(bf16[256,512]{1,0:T(8,128)(2,1)S(1)} %collective-permute-done.2.left, bf16[512,8192]{1,0:T(8,128)(2,1)} %all-gather.2.cloned.1.call-done.pair, bf16[128,128]{1,0:T(8,128)(2,1)S(1)} %reshape.23.mix, bf16[8,512,512]{2,1,0:T(8,128)(2,1)S(1)} %bitcast.16), custom_call_target="tpu_custom_call" | custom-call | flops 5000000000 | bytes 14000000 | tf_op jit(solution)/shard_map/back/pallas_call | solution.py:85
  141.6 0.9 reshape.24
  (11 shorter events, 0.1 us)
Async XLA Ops:
  7.2 121.5 %all-gather.2.cloned.1.call-start = ((), (), s32[]{:S(2)}) async-start(), calls=%async_computation.2 | async-start | bytes 8912896 | tf_op jit(solution)/shard_map/all_gather | solution.py:58
  8.6 9.5 %collective-permute-start.3 = (bf16[32,8192]{1,0:T(8,128)(2,1)S(1)}, bf16[32,8192]{1,0:T(8,128)(2,1)S(1)}, u32[]{:S(2)}, u32[]{:S(2)}) collective-permute-start(bf16[32,8192]{1,0:T(8,128)(2,1)S(1)} %reshape_squeeze.15), channel_id=1, source_target_pairs={{496,0},{0,16},{16,32},{32,48},{48,64},{64,80},{80,96},{96,112},{1... | collective-permute-start | bytes 1572872 | tf_op jit(solution)/shard_map/ppermute | solution.py:16
  18.2 0.8 copy-start.2
  18.2 9.7 %copy-start.1 = (bf16[1,32,8,512]{3,2,1,0:T(8,128)(2,1)S(1)}, bf16[1,32,8,512]{3,2,1,0:T(8,128)(2,1)}, u32[]{:S(2)}) copy-start(bf16[1,32,8,512]{3,2,1,0:T(8,128)(2,1)} %param.5) | copy-start | bytes 786436
  18.2 13.0 %copy-start.3 = (bf16[1,32,4,512]{3,2,1,0:T(4,128)(2,1)S(1)}, bf16[1,32,4,512]{3,2,1,0:T(4,128)(2,1)}, u32[]{:S(2)}) copy-start(bf16[1,32,4,512]{3,2,1,0:T(4,128)(2,1)} %param.6) | copy-start | bytes 393220
  19.0 14.2 %copy-start.4 = (bf16[8,8,4,4]{1,3,2,0:T(4,128)(2,1)S(1)}, bf16[8,8,4,4]{1,3,2,0:T(4,128)(2,1)}, u32[]{:S(2)}) copy-start(bf16[8,8,4,4]{1,3,2,0:T(4,128)(2,1)} %param.9) | copy-start | bytes 6148
  21.1 37.8 %all-to-all-start = ((bf16[16,4,32,256]{3,2,1,0:T(8,128)(2,1)}), bf16[16,4,32,256]{3,2,1,0:T(8,128)(2,1)S(1)}, u32[]{:S(2)}, u32[]{:S(2)}) async-start(bf16[16,4,32,256]{3,2,1,0:T(8,128)(2,1)} %bitcast.2), calls=%async_computation | async-start | bytes 2097152 | tf_op jit(solution)/shard_map/all_to_all | solution.py:66
  27.9 31.0 %collective-permute-start = (bf16[256,512]{1,0:T(8,128)(2,1)S(1)}, bf16[256,512]{1,0:T(8,128)(2,1)S(1)}, u32[]{:S(2)}, u32[]{:S(2)}) collective-permute-start(bf16[256,512]{1,0:T(8,128)(2,1)S(1)} %bitcast.17), channel_id=1, source_target_pairs={{0,1},{1,0},{2,3},{3,2},{4,5},{5,4},{6,7},{7,6},{8,9},{9,8},{10,11... | collective-permute-start | bytes 786440 | tf_op jit(solution)/shard_map/ppermute | solution.py:62
  31.2 27.7 %collective-permute-start.1 = (bf16[128,512]{1,0:T(8,128)(2,1)S(1)}, bf16[128,512]{1,0:T(8,128)(2,1)S(1)}, u32[]{:S(2)}, u32[]{:S(2)}) collective-permute-start(bf16[128,512]{1,0:T(8,128)(2,1)S(1)} %reshape_squeeze.14.site_a), channel_id=1, source_target_pairs={{0,1},{1,0},{2,3},{3,2},{4,5},{5,4},{6,7},{7,6},{8,9},{9,8},{10,11... | collective-permute-start | bytes 393224 | tf_op jit(solution)/shard_map/ppermute | solution.py:63
  109.6 6.5 %collective-permute-start.2 = (bf16[256,512]{1,0:T(8,128)(2,1)S(1)}, bf16[256,512]{1,0:T(8,128)(2,1)S(1)}, u32[]{:S(2)}, u32[]{:S(2)}) collective-permute-start(bf16[256,512]{1,0:T(8,128)(2,1)S(1)} %bitcast.24), channel_id=1, source_target_pairs={{496,0},{0,16},{16,32},{32,48},{48,64},{64,80},{80,96},{96,112},{1... | collective-permute-start | bytes 786440 | tf_op jit(solution)/shard_map/ppermute | solution.py:16
  128.6 2.2 %copy-start = (bf16[1,8,512,512]{3,2,1,0:T(8,128)(2,1)S(1)}, bf16[1,8,512,512]{3,2,1,0:T(8,128)(2,1)}, u32[]{:S(2)}) copy-start(bf16[1,8,512,512]{3,2,1,0:T(8,128)(2,1)} %param.8) | copy-start | bytes 12582916
Sparse Core Ops, SparseCore 0:
  19.1 109.4 all-gather.1

commit v2 on v1

v2 whole, which is shorter than its diff:
```python
import jax
import jax.numpy as jnp
from jax import lax
from jax.experimental import pallas as pl
from jax.experimental.pallas import tpu as pltpu
from jax.sharding import PartitionSpec as P

BF = jnp.bfloat16
F32 = jnp.float32
VM = pl.BlockSpec(memory_space=pltpu.VMEM)


def shifted(block, axis, distance):
    devices = range(lax.axis_size(axis))
    route = [((i - distance) % len(devices), i) for i in devices]
    return lax.ppermute(block, axis, route)


def front(gathered, cols, kron, out, first, second):
    ket = jnp.concatenate([cols[:, s].reshape(512, 128) for s in range(4)], axis=1)
    for g in range(4):
        f = jnp.dot(gathered[g, :256, :], ket, preferred_element_type=F32)
        for h in range(2):
            part = [f[:, 128 * s : 128 * s + 128].reshape(32, 8, 128) for s in (2 * h, 2 * h + 1)]
            first[32 * g : 32 * g + 32, 16 * h : 16 * h + 16, :] = jnp.concatenate(part, axis=1).astype(BF)
    for blk in range(0, 16, 2):
        f = [first[8 * i : 8 * i + 8].reshape(256, 128) for i in (blk, blk + 1)]
        o = jnp.dot(kron[...], jnp.concatenate(f, axis=1), preferred_element_type=F32).astype(BF)
        for i in range(2):
            second[:, 32 * (blk + i) : 32 * (blk + i) + 32, :] = o[:, 128 * i : 128 * i + 128].reshape(8, 32, 128)
    site = gathered[:, 256:, :].reshape(512, 512)
    for n in range(0, 8, 2):
        f = jnp.concatenate([second[n], second[n + 1]], axis=1)
        o = lax.dot_general(site, f, (((0,), (0,)), ((), ())), preferred_element_type=F32).astype(BF)
        for i in range(2):
            out[:, n + i] = o[:, 128 * i : 128 * i + 128].reshape(16, 32, 128)


def back(left, pair, mix, right, out, mixed, proj, env, sem):
    j = pl.program_id(0)
    fetch = pltpu.make_async_copy(right, env, sem)

    @pl.when(j == 0)
    def _():
        fetch.start()

    m = jnp.dot(left[...], pair[...], preferred_element_type=F32)
    m = jnp.concatenate([m[:, :512].reshape(32, 8, 512), m[:, 512:].reshape(32, 8, 512)], axis=1)
    mixed[:, pl.ds(pl.multiple_of(16 * j, 16), 16), :] = m.astype(BF)

    @pl.when(j == 7)
    def _():
        for p in range(32):
            o = jnp.dot(mix[...], mixed[p], preferred_element_type=F32).astype(BF)
            for k in range(8):
                proj[16 * p : 16 * p + 16, 512 * k : 512 * k + 512] = o[16 * k : 16 * k + 16, :]
        fetch.wait()
        out[...] = jnp.dot(proj[...], env[...], preferred_element_type=F32).astype(BF)


def shards(left_env, site, psi, right_env, mpo):
    chi = site.shape[-1]
    pair = shifted(psi[0], "sec", 1).reshape(32, 16 * chi)
    pair = lax.all_gather(pair, "bond", axis=0, tiled=True)
    own = jnp.concatenate([left_env[0].reshape(256, chi), site[0].reshape(128, chi)], axis=0)
    lines = [[4 * y + x for x in range(4)] for y in range(4)]
    gathered = lax.all_to_all(
        jnp.broadcast_to(own[None], (4, 384, chi)), "bond", 0, 0, axis_index_groups=lines, tiled=True
    )
    quarters = site[0].reshape(32, 4, 4, 128).transpose(2, 1, 0, 3)
    send = jnp.broadcast_to(quarters[None], (4, 4, 4, 32, 128)).reshape(16, 4, 32, 128)
    cols = lax.all_to_all(send, "bond", 0, 0, tiled=True)
    eye = jnp.eye(8, dtype=BF)
    kron = jnp.einsum("pq,mnsu->npuqsm", eye, mpo).reshape(256, 256)
    fresh = pl.pallas_call(
        front,
        out_shape=jax.ShapeDtypeStruct((16, 8, 32, 128), BF),
        in_specs=[VM] * 3,
        out_specs=VM,
        scratch_shapes=[pltpu.VMEM((128, 32, 128), BF), pltpu.VMEM((8, 512, 128), BF)],
        compiler_params=pltpu.CompilerParams(vmem_limit_bytes=40 << 20),
        cost_estimate=pl.CostEstimate(flops=2_000_000_000, bytes_accessed=4_000_000, transcendentals=0),
        name="front",
    )(gathered, cols, kron)
    fresh = lax.all_to_all(fresh, "bond", 0, 0, tiled=True).reshape(4, 4, 8, 32, 128).astype(F32)
    fresh = ((fresh[0] + fresh[1]) + (fresh[2] + fresh[3])).astype(BF)
    new_left = fresh.transpose(2, 1, 0, 3).reshape(32, 8, chi)
    source = shifted(new_left.reshape(256, chi), "sec", 1)
    two_site = jnp.einsum("mnsu,nkvw->kuwsvm", mpo, mpo, preferred_element_type=F32)
    two_site = two_site.astype(BF).reshape(128, 128)
    result = pl.pallas_call(
        back,
        grid=(8,),
        out_shape=jax.ShapeDtypeStruct((512, chi), BF),
        in_specs=[
            pl.BlockSpec((256, 512), lambda j: (0, 0)),
            pl.BlockSpec((512, 1024), lambda j: (0, j)),
            pl.BlockSpec((128, 128), lambda j: (0, 0)),
            pl.BlockSpec(memory_space=pl.ANY),
        ],
        out_specs=pl.BlockSpec((512, 512), lambda j: (0, 0)),
        scratch_shapes=[
            pltpu.VMEM((32, 128, 512), BF),
            pltpu.VMEM((512, 4096), BF),
            pltpu.VMEM((4096, 512), BF),
            pltpu.SemaphoreType.DMA,
        ],
        compiler_params=pltpu.CompilerParams(vmem_limit_bytes=58 << 20),
        cost_estimate=pl.CostEstimate(flops=5_000_000_000, bytes_accessed=14_000_000, transcendentals=0),
        name="back",
    )(source, pair, two_site, right_env[0].reshape(8 * chi, chi))
    return (new_left[None], result.reshape(1, 32, 4, 4, chi))


def solution(mesh):
    in_specs = (
        P("sec", "bond", None, None),
        P("sec", "bond", None, None),
        P("sec", "bond", None, None, None),
        P("sec", None, None, None),
        P(),
    )
    out_specs = (P("sec", "bond", None, None), P("sec", "bond", None, None, None))
    return jax.shard_map(shards, mesh=mesh, in_specs=in_specs, out_specs=out_specs, check_vma=False)
```

time: 150 us -> 146 us (0.973)
  blocking collectives: 48.5 us -> 32.4 us
  waiting for transfers between devices: 42 us -> 54.9 us
  Pallas kernels: 12.4 us -> 14.2 us
  local copies, waits for them, and re-layouts: 13.8 us -> 12.2 us
    ppermute x2 -> x0, waiting for transfers between devices: 19.3 us -> none  [the longest x1 19.3 us: shards(): tensor_b = lax.ppermute(tensor, 'bond', swap)]
    all_to_all x0 -> x1, waiting for transfers between devices: none -> 19.1 us  [shards(): lax.all_to_all(jnp.broadcast_to(own[None], (4, 384, chi)), 'bond', 0, 0,...]
    all_to_all x1, blocking collectives: 48.5 us -> 32.4 us  [shards(): lax.all_to_all(fresh, 'bond', 0, 0, tiled=True).reshape(4, 4, 8, 32, 128)]
    all_to_all x1, waiting for transfers between devices: 0.01 us -> 11.7 us  [shards(): cols = lax.all_to_all(send, 'bond', 0, 0, tiled=True)]
    ppermute x2 -> x0, starting transfers between devices: 5.28 us -> none  [the longest x1 3.27 us: shards(): left_b = lax.ppermute(left, 'bond', swap)]
    all_gather x1, waiting for transfers between devices: 12.6 us -> 16.2 us  [shards(): pair = lax.all_gather(pair, 'bond', axis=0, tiled=True)]
    all_to_all x0 -> x1, starting transfers between devices: none -> 3.56 us  [shards(): lax.all_to_all(jnp.broadcast_to(own[None], (4, 384, chi)), 'bond', 0, 0,...]
    unnamed x11, local copies, waits for them, and re-layouts: 3.11 us -> 0.15 us
  transfers between devices with their start and end apart: 6 -> 5, of which waited for: 4 -> 5; matrix products, arithmetic and copies ran while one was open for 8% -> 8% of each run, Pallas kernels for 1% -> 1%
where the time goes in v2:
time: 146 us
  waiting for transfers between devices  54.9 us (38%)
  blocking collectives  32.4 us (22%)
  starting transfers between devices  14.9 us (10%)
  Pallas kernels  14.2 us (10%)
  between operations  14.2 us (10%)
  local copies, waits for them, and re-layouts  12.2 us (8%)
  other arithmetic  2.7 us (2%)
    all_to_all x1, blocking collectives, shards(): lax.all_to_all(fresh, 'bond', 0, 0, tiled=True).reshape(4, 4, 8, 32, 128)  32.4 us
    all_to_all x1, waiting for transfers between devices, shards(): lax.all_to_all(jnp.broadcast_to(own[None], (4, 384, chi)), 'bond', 0, 0,...  19.1 us
    all_gather x1, waiting for transfers between devices, shards(): pair = lax.all_gather(pair, 'bond', axis=0, tiled=True)  16.2 us
    pallas_call x1, Pallas kernels, shards(): pl.pallas_call(back, grid=(8,), out_shape=jax.ShapeDtypeStruct((512, chi)...  12.7 us
    all_to_all x1, waiting for transfers between devices, shards(): cols = lax.all_to_all(send, 'bond', 0, 0, tiled=True)  11.7 us
    ppermute x2, waiting for transfers between devices, shifted(): return lax.ppermute(block, axis, route)  7.88 us
    all_to_all x1, starting transfers between devices, shards(): cols = lax.all_to_all(send, 'bond', 0, 0, tiled=True)  6.75 us
    ppermute x2, starting transfers between devices, shifted(): return lax.ppermute(block, axis, route)  4.53 us
  transfers between devices with their start and end apart: 5, of which 5 were waited for; matrix products, arithmetic and copies ran while one was open for 8% of the time, Pallas kernels for 1%

profile of v2, /device:TPU:97, one launch (start us, length us, event | category | flops | bytes accessed | tf_op | source)
XLA Modules:
  0.0 145.8 jit_solution(7384354382396109588)
XLA Ops:
  7.2 0.0 copy-start
  7.2 0.0 all-gather.2.cloned.1.call-start
  7.2 3.4 %collective-permute-start.1 = (bf16[32,4,4,512]{3,2,1,0:T(4,128)(2,1)}, bf16[32,4,4,512]{3,2,1,0:T(4,128)(2,1)S(1)}, u32[]{:S(2)}, u32[]{:S(2)}) collective-permute-start(bf16[32,4,4,512]{3,2,1,0:T(4,128)(2,1)} %bitcast.27), channel_id=1, source_target_pairs={{496,0},{0,16},{16,32},{32,48},{48,64},{64,80},{80,96},{96,112},{1... | collective-permute-start | bytes 1572872 | tf_op jit(solution)/shard_map/ppermute | solution.py:16
  10.7 6.4 %collective-permute-done.1 = bf16[32,4,4,512]{3,2,1,0:T(4,128)(2,1)S(1)} collective-permute-done((bf16[32,4,4,512]{3,2,1,0:T(4,128)(2,1)}, bf16[32,4,4,512]{3,2,1,0:T(4,128)(2,1)S(1)}, u32[]{:S(2)}, u32[]{:S(2)}) %collective-permute-start.1) | collective-permute-done | bytes 524320 | tf_op jit(solution)/shard_map/ppermute | solution.py:16
  17.1 1.2 reshape.38
  18.3 0.0 all-gather.2.cloned.1.call-update
  18.3 1.0 reshape_squeeze.14
  19.3 0.9 broadcast_in_dim.5
  20.2 6.8 %all-to-all-start.1 = ((bf16[16,4,32,128]{3,2,1,0:T(8,128)(2,1)}), bf16[16,4,32,128]{3,2,1,0:T(8,128)(2,1)S(1)}, u32[]{:S(2)}, u32[]{:S(2)}) async-start(bf16[16,4,32,128]{3,2,1,0:T(8,128)(2,1)} %bitcast.2), calls=%async_computation.1 | async-start | bytes 1048576 | tf_op jit(solution)/shard_map/all_to_all | solution.py:72
  27.0 0.0 copy-done
  27.1 0.0 copy-start.1
  27.1 11.7 %all-to-all-done.1.cols = bf16[16,4,32,128]{3,2,1,0:T(8,128)(2,1)S(1)} async-done(((bf16[16,4,32,128]{3,2,1,0:T(8,128)(2,1)}), bf16[16,4,32,128]{3,2,1,0:T(8,128)(2,1)S(1)}, u32[]{:S(2)}, u32[]{:S(2)}) %all-to-all-start.1) | async-done | bytes 524320 | tf_op jit(solution)/shard_map/all_to_all | solution.py:72
  38.8 1.3 broadcast_in_dim.4
  40.0 3.6 %all-to-all-start = ((bf16[4,384,512]{2,1,0:T(8,128)(2,1)}), bf16[4,384,512]{2,1,0:T(8,128)(2,1)S(1)}, u32[]{:S(2)}, u32[]{:S(2)}) async-start(bf16[4,384,512]{2,1,0:T(8,128)(2,1)} %broadcast_in_dim.4), calls=%async_computation | async-start | bytes 3145728 | tf_op jit(solution)/shard_map/all_to_all | solution.py:67
  43.6 0.1 copy.14
  43.8 2.2 %multiply_bitcast_fusion = bf16[8,8,4,8,4,8]{5,4,3,2,1,0:T(4,128)(2,1)} fusion(bf16[8,8,4,4]{0,2,3,1:T(4,128)(2,1)S(1)} %copy.14, bf16[8,8]{1,0:T(8,128)(2,1)S(1)} %fusion.6), kind=kLoop, calls=%fused_computation | loop fusion | flops 65536 | bytes 133248 | tf_op jit(solution)/shard_map/pq,mnsu->npuqsm/transpose | solution.py:74
  45.9 4.1 %reshape.37.kron = bf16[256,256]{1,0:T(8,128)(2,1)S(1)} reshape(bf16[8,8,4,8,4,8]{5,4,3,2,1,0:T(4,128)(2,1)} %multiply_bitcast_fusion) | data formatting | bytes 262144 | tf_op jit(solution)/shard_map/reshape | solution.py:74
  50.0 19.1 %all-to-all-done.gathered = bf16[4,384,512]{2,1,0:T(8,128)(2,1)S(1)} async-done(((bf16[4,384,512]{2,1,0:T(8,128)(2,1)}), bf16[4,384,512]{2,1,0:T(8,128)(2,1)S(1)}, u32[]{:S(2)}, u32[]{:S(2)}) %all-to-all-start) | async-done | bytes 1572896 | tf_op jit(solution)/shard_map/all_to_all | solution.py:67
  69.1 1.5 %front.1 = bf16[16,8,32,128]{3,2,1,0:T(8,128)(2,1)S(1)} custom-call(bf16[4,384,512]{2,1,0:T(8,128)(2,1)S(1)} %all-to-all-done.gathered, bf16[16,4,32,128]{3,2,1,0:T(8,128)(2,1)S(1)} %all-to-all-done.1.cols, bf16[256,256]{1,0:T(8,128)(2,1)S(1)} %reshape.37.kron), custom_call_target="tpu_custom_call" | custom-call | flops 2000000000 | bytes 4000000 | tf_op jit(solution)/shard_map/front/pallas_call | solution.py:75
  70.7 32.4 %all_to_all.15 = bf16[16,8,32,128]{3,2,1,0:T(8,128)(2,1)S(1)} all-to-all(bf16[16,8,32,128]{3,2,1,0:T(8,128)(2,1)S(1)} %front.1), channel_id=1, replica_groups=mesh['sec'=32,'bond'=16] {'bond'}, dimensions={0} | all-to-all | bytes 2097152 | tf_op jit(solution)/shard_map/all_to_all | solution.py:85
  103.1 0.3 convert_element_type.16
  103.4 0.2 fusion.3
  103.6 0.1 copy.32
  103.7 0.0 copy-start.3
  103.7 1.1 collective-permute-start
  104.8 0.3 fusion
  105.2 0.4 copy.19
  105.6 1.1 reshape.39.mix
  106.7 1.4 collective-permute-done.left
  108.2 16.2 %all-gather.2.cloned.1.call-done.pair = bf16[512,8192]{1,0:T(8,128)(2,1)} async-done(((bf16[32,8192]{1,0:T(8,128)(2,1)}), bf16[512,8192]{1,0:T(8,128)(2,1)}) %all-gather.2.cloned.1.call-update) | async-done | bytes 8388624 | tf_op jit(solution)/shard_map/all_gather | solution.py:64
  124.3 12.7 %back.1 = bf16[512,512]{1,0:T(8,128)(2,1)} custom-call(bf16[256,512]{1,0:T(8,128)(2,1)} %copy-done.4, bf16[512,8192]{1,0:T(8,128)(2,1)} %all-gather.2.cloned.1.call-done.pair, bf16[128,128]{1,0:T(8,128)(2,1)} %reshape.39.mix, bf16[4096,512]{1,0:T(8,128)(2,1)} %bitcast.26), custom_call_target="tpu_custom_call" | custom-call | flops 5000000000 | bytes 14000000 | tf_op jit(solution)/shard_map/back/pallas_call | solution.py:91
  137.0 2.0 %reshape.40 = bf16[1,32,4,4,512]{4,3,2,1,0:T(4,128)(2,1)} reshape(bf16[512,512]{1,0:T(8,128)(2,1)} %back.1) | data formatting | bytes 1048576 | tf_op jit(solution)/shard_map/reshape | solution.py:112
  (10 shorter events, 0.1 us)
Async XLA Ops:
  7.2 19.8 %copy-start = (bf16[1,32,4,512]{3,2,1,0:T(4,128)(2,1)S(1)}, bf16[1,32,4,512]{3,2,1,0:T(4,128)(2,1)}, u32[]{:S(2)}) copy-start(bf16[1,32,4,512]{3,2,1,0:T(4,128)(2,1)} %param.6) | copy-start | bytes 393220
  7.2 19.8 %copy-start.2 = (bf16[1,32,8,512]{3,2,1,0:T(8,128)(2,1)S(1)}, bf16[1,32,8,512]{3,2,1,0:T(8,128)(2,1)}, u32[]{:S(2)}) copy-start(bf16[1,32,8,512]{3,2,1,0:T(8,128)(2,1)} %param.5) | copy-start | bytes 786436
  7.2 117.2 %all-gather.2.cloned.1.call-start = ((), (), s32[]{:S(2)}) async-start(), calls=%async_computation.3 | async-start | bytes 8912896 | tf_op jit(solution)/shard_map/all_gather | solution.py:64
  7.2 9.9 %collective-permute-start.1 = (bf16[32,4,4,512]{3,2,1,0:T(4,128)(2,1)}, bf16[32,4,4,512]{3,2,1,0:T(4,128)(2,1)S(1)}, u32[]{:S(2)}, u32[]{:S(2)}) collective-permute-start(bf16[32,4,4,512]{3,2,1,0:T(4,128)(2,1)} %bitcast.27), channel_id=1, source_target_pairs={{496,0},{0,16},{16,32},{32,48},{48,64},{64,80},{80,96},{96,112},{1... | collective-permute-start | bytes 1572872 | tf_op jit(solution)/shard_map/ppermute | solution.py:16
  20.2 18.6 %all-to-all-start.1 = ((bf16[16,4,32,128]{3,2,1,0:T(8,128)(2,1)}), bf16[16,4,32,128]{3,2,1,0:T(8,128)(2,1)S(1)}, u32[]{:S(2)}, u32[]{:S(2)}) async-start(bf16[16,4,32,128]{3,2,1,0:T(8,128)(2,1)} %bitcast.2), calls=%async_computation.1 | async-start | bytes 1048576 | tf_op jit(solution)/shard_map/all_to_all | solution.py:72
  27.1 16.6 %copy-start.1 = (bf16[8,8,4,4]{1,3,2,0:T(4,128)(2,1)S(1)}, bf16[8,8,4,4]{1,3,2,0:T(4,128)(2,1)}, u32[]{:S(2)}) copy-start(bf16[8,8,4,4]{1,3,2,0:T(4,128)(2,1)} %param.9) | copy-start | bytes 6148
  40.0 29.1 %all-to-all-start = ((bf16[4,384,512]{2,1,0:T(8,128)(2,1)}), bf16[4,384,512]{2,1,0:T(8,128)(2,1)S(1)}, u32[]{:S(2)}, u32[]{:S(2)}) async-start(bf16[4,384,512]{2,1,0:T(8,128)(2,1)} %broadcast_in_dim.4), calls=%async_computation | async-start | bytes 3145728 | tf_op jit(solution)/shard_map/all_to_all | solution.py:67
  103.7 33.3 %copy-start.3 = (bf16[32,8,4,128]{3,1,2,0:T(8,128)(2,1)}, bf16[32,8,4,128]{3,1,2,0:T(8,128)(2,1)S(1)}, u32[]{:S(2)}) copy-start(bf16[32,8,4,128]{3,1,2,0:T(8,128)(2,1)S(1)} %copy.32) | copy-start | bytes 786436
  103.7 4.4 %collective-permute-start = (bf16[256,512]{1,0:T(8,128)(2,1)S(1)}, bf16[256,512]{1,0:T(8,128)(2,1)S(1)}, u32[]{:S(2)}, u32[]{:S(2)}) collective-permute-start(bf16[256,512]{1,0:T(8,128)(2,1)S(1)} %bitcast.24), channel_id=1, source_target_pairs={{496,0},{0,16},{16,32},{32,48},{48,64},{64,80},{80,96},{96,112},{1... | collective-permute-start | bytes 786440 | tf_op jit(solution)/shard_map/ppermute | solution.py:16
  108.2 16.2 %copy-start.4 = (bf16[256,512]{1,0:T(8,128)(2,1)}, bf16[256,512]{1,0:T(8,128)(2,1)S(1)}, u32[]{:S(2)}) copy-start(bf16[256,512]{1,0:T(8,128)(2,1)S(1)} %collective-permute-done.left) | copy-start | bytes 786436
Sparse Core Ops, SparseCore 0:
  18.4 105.8 all-gather.1

commit v3 on v2

v3 whole, which is shorter than its diff:
```python
import jax
import jax.numpy as jnp
from jax import lax
from jax.experimental import pallas as pl
from jax.experimental.pallas import tpu as pltpu
from jax.sharding import PartitionSpec as P

BF = jnp.bfloat16
F32 = jnp.float32
VM = pl.BlockSpec(memory_space=pltpu.VMEM)


LINE = 4


def line_route(distance):
    return [(i, i - i % LINE + (i + distance) % LINE) for i in range(LINE * LINE)]


def front(own, near, back_, far, cols, local, out, first, second):
    ket = jnp.concatenate([cols[:, s].reshape(512, 128) for s in range(4)], axis=1)
    blocks = (own, near, back_, far)
    for g, block in enumerate(blocks):
        f = jnp.dot(block[:256, :], ket, preferred_element_type=F32)
        for h in range(2):
            part = [f[:, 128 * s : 128 * s + 128].reshape(32, 8, 128) for s in (2 * h, 2 * h + 1)]
            first[32 * g : 32 * g + 32, 16 * h : 16 * h + 16, :] = jnp.concatenate(part, axis=1).astype(BF)
    row = lax.broadcasted_iota(jnp.int32, (256, 32), 0)
    col = lax.broadcasted_iota(jnp.int32, (256, 32), 1)
    spread = ((row >> 5) * 4 + (row & 3) == col).astype(BF)
    row = lax.broadcasted_iota(jnp.int32, (32, 256), 0)
    col = lax.broadcasted_iota(jnp.int32, (32, 256), 1)
    copies = (row == (col & 31)).astype(BF)
    kron = jnp.dot(spread, local[...], preferred_element_type=F32).astype(BF)
    kron = jnp.dot(kron, copies, preferred_element_type=F32)
    row = lax.broadcasted_iota(jnp.int32, (256, 256), 0)
    col = lax.broadcasted_iota(jnp.int32, (256, 256), 1)
    kron = jnp.where(((row >> 2) & 7) == (col >> 5), kron, 0.0).astype(BF)
    for blk in range(0, 16, 2):
        f = [first[8 * i : 8 * i + 8].reshape(256, 128) for i in (blk, blk + 1)]
        o = jnp.dot(kron, jnp.concatenate(f, axis=1), preferred_element_type=F32).astype(BF)
        for i in range(2):
            second[:, 32 * (blk + i) : 32 * (blk + i) + 32, :] = o[:, 128 * i : 128 * i + 128].reshape(8, 32, 128)
    site = jnp.concatenate([block[256:, :] for block in blocks], axis=0)
    for n in range(0, 8, 2):
        f = jnp.concatenate([second[n], second[n + 1]], axis=1)
        o = lax.dot_general(site, f, (((0,), (0,)), ((), ())), preferred_element_type=F32).astype(BF)
        for i in range(2):
            out[:, n + i] = o[:, 128 * i : 128 * i + 128].reshape(16, 32, 128)


def back(left, pair, mix, right, out, mixed, proj, env, sem):
    j = pl.program_id(0)
    fetch = pltpu.make_async_copy(right, env, sem)

    @pl.when(j == 0)
    def _():
        fetch.start()

    m = jnp.dot(left[...], pair[...], preferred_element_type=F32)
    for h in range(2):
        part = [m[:, 256 * i : 256 * i + 256].reshape(32, 8, 256) for i in (2 * h, 2 * h + 1)]
        at = pl.ds(pl.multiple_of(32 * j + 16 * h, 16), 16)
        mixed[:, at, :] = jnp.concatenate(part, axis=1).astype(BF)

    @pl.when(j == 3)
    def _():
        for p in range(32):
            o = jnp.dot(mix[...], mixed[p], preferred_element_type=F32).astype(BF)
            for k in range(8):
                proj[16 * p : 16 * p + 16, 256 * k : 256 * k + 256] = o[16 * k : 16 * k + 16, :]
        fetch.wait()
        out[...] = jnp.dot(proj[...], env[...], preferred_element_type=F32).astype(BF)


def applied(left, pair, mix, right):
    return pl.pallas_call(
        back,
        grid=(4,),
        out_shape=jax.ShapeDtypeStruct((512, 512), BF),
        in_specs=[
            pl.BlockSpec((256, 512), lambda j: (0, 0)),
            pl.BlockSpec((512, 1024), lambda j: (0, j)),
            pl.BlockSpec((128, 128), lambda j: (0, 0)),
            pl.BlockSpec(memory_space=pl.ANY),
        ],
        out_specs=pl.BlockSpec((512, 512), lambda j: (0, 0)),
        scratch_shapes=[
            pltpu.VMEM((32, 128, 256), BF),
            pltpu.VMEM((512, 2048), BF),
            pltpu.VMEM((2048, 512), BF),
            pltpu.SemaphoreType.DMA,
        ],
        compiler_params=pltpu.CompilerParams(vmem_limit_bytes=32 << 20),
        cost_estimate=pl.CostEstimate(flops=2_500_000_000, bytes_accessed=8_000_000, transcendentals=0),
        name="back",
    )(left, pair, mix, right)


def shards(left_env, site, psi, right_env, mpo):
    chi = site.shape[-1]
    lines = [[LINE * y + x for x in range(LINE)] for y in range(LINE)]
    columns = [[LINE * y + x for y in range(LINE)] for x in range(LINE)]
    halves = psi[0].reshape(32, 16, 2, 256).transpose(2, 0, 1, 3).reshape(2, 32, 4096)
    send = jnp.broadcast_to(halves[None], (2, 2, 32, 4096)).reshape(4, 32, 4096)
    pair = lax.all_to_all(send, "bond", 0, 0, axis_index_groups=lines, tiled=True)
    pair = lax.all_gather(pair.reshape(128, 4096), "bond", axis=0, axis_index_groups=columns, tiled=True)
    own = jnp.concatenate([left_env[0].reshape(256, chi), site[0].reshape(128, chi)], axis=0)
    blocks = [own] + [lax.ppermute(own, "bond", line_route(d)) for d in (1, -1, 2)]
    quarters = site[0].reshape(32, 4, 4, 128).transpose(2, 1, 0, 3)
    send = jnp.broadcast_to(quarters[None], (4, 4, 4, 32, 128)).reshape(16, 4, 32, 128)
    cols = lax.all_to_all(send, "bond", 0, 0, tiled=True)
    local = mpo.transpose(1, 3, 2, 0).reshape(32, 32)
    fresh = pl.pallas_call(
        front,
        out_shape=jax.ShapeDtypeStruct((16, 8, 32, 128), BF),
        in_specs=[VM] * 6,
        out_specs=VM,
        scratch_shapes=[pltpu.VMEM((128, 32, 128), BF), pltpu.VMEM((8, 512, 128), BF)],
        compiler_params=pltpu.CompilerParams(vmem_limit_bytes=32 << 20),
        cost_estimate=pl.CostEstimate(flops=2_000_000_000, bytes_accessed=4_000_000, transcendentals=0),
        name="front",
    )(*blocks, cols, local)
    fresh = lax.all_to_all(fresh, "bond", 0, 0, tiled=True).reshape(4, 4, 8, 32, 128).astype(F32)
    fresh = ((fresh[0] + fresh[1]) + (fresh[2] + fresh[3])).astype(BF)
    new_left = fresh.transpose(2, 1, 0, 3).reshape(32, 8, chi)
    source = new_left.reshape(256, chi)
    other = lax.ppermute(source, "bond", [(i, i ^ 1) for i in range(16)])
    two_site = jnp.einsum("mnsu,nkvw->kuwsvm", mpo, mpo, preferred_element_type=F32)
    two_site = two_site.astype(BF).reshape(128, 128)
    sections = lax.axis_size("sec")
    start = lax.axis_index("bond") % 2 * 256
    right = lax.dynamic_slice_in_dim(right_env[0], start, 256, 1).reshape(2048, chi)
    right = lax.ppermute(right, "sec", [((i + 1) % sections, i) for i in range(sections)])
    total = 0.0
    for flip, left in ((0, source), (1, other)):
        part = applied(left, pair, two_site, right)
        route = [(16 * s + b, (s + 1) % sections * 16 + (b ^ flip)) for s in range(sections) for b in range(16)]
        total = total + lax.ppermute(part, ("sec", "bond"), route).astype(F32)
    return (new_left[None], total.astype(BF).reshape(1, 32, 4, 4, chi))


def solution(mesh):
    in_specs = (
        P("sec", "bond", None, None),
        P("sec", "bond", None, None),
        P("sec", "bond", None, None, None),
        P("sec", None, None, None),
        P(),
    )
    out_specs = (P("sec", "bond", None, None), P("sec", "bond", None, None, None))
    return jax.shard_map(shards, mesh=mesh, in_specs=in_specs, out_specs=out_specs, check_vma=False)
```

time: 146 us -> 137 us (0.938)
  the two profiles are of different devices: /device:TPU:97 before, /device:TPU:6 now
where the time goes in v3:
time: 137 us
  blocking collectives  37.9 us (28%)
  starting transfers between devices  32.1 us (23%)
  waiting for transfers between devices  29.9 us (22%)
  between operations  14.2 us (10%)
  Pallas kernels  11.4 us (8%)
  local copies, waits for them, and re-layouts  10.2 us (7%)
    all_to_all x1, blocking collectives, shards(): lax.all_to_all(fresh, 'bond', 0, 0, tiled=True).reshape(4, 4, 8, 32, 128)  20.1 us
    all_to_all x1, blocking collectives, shards(): lax.all_to_all(send, 'bond', 0, 0, axis_index_groups=lines, tiled=True)  17.8 us
    ppermute x2, waiting for transfers between devices, shards(): total = total + lax.ppermute(part, ('sec', 'bond'), route).astype(F32)  13.9 us
    ppermute x3, waiting for transfers between devices, shards(): lax.ppermute(own, 'bond', line_route(d))  10.2 us
    ppermute x3, starting transfers between devices, shards(): lax.ppermute(own, 'bond', line_route(d))  9.21 us
    pallas_call x2, Pallas kernels, applied(): pl.pallas_call(back, grid=(4,), out_shape=jax.ShapeDtypeStruct((512, 512)...  8.4 us
    ppermute x1, starting transfers between devices, shards(): lax.ppermute(right, 'sec', [((i + 1) % sections, i) for i in range(sectio...  7.63 us
    all_to_all x1, starting transfers between devices, shards(): cols = lax.all_to_all(send, 'bond', 0, 0, tiled=True)  7.16 us
  transfers between devices with their start and end apart: 9, of which 6 were waited for; matrix products, arithmetic and copies ran while one was open for 5% of the time, Pallas kernels for 5%

profile of v3, /device:TPU:6, one launch (start us, length us, event | category | flops | bytes accessed | tf_op | source)
XLA Modules:
  0.0 136.8 jit_solution(13672665124756170105)
XLA Ops:
  7.2 1.2 reshape_squeeze.15
  8.5 0.2 broadcast_in_dim.14
  8.9 17.8 %all_to_all.15 = bf16[4,32,4096]{2,1,0:T(8,128)(2,1)} all-to-all(bf16[4,32,4096]{2,1,0:T(8,128)(2,1)S(1)} %bitcast.30), channel_id=1, replica_groups={{0,1,2,3},{4,5,6,7},{8,9,10,11},{12,13,14,15},{16,17,18,19},{20,21,22,2..., dimensions={0} | all-to-all | bytes 2097152 | tf_op jit(solution)/shard_map/all_to_all | solution.py:106
  26.8 3.1 %constant_dynamic-slice_fusion = bf16[1,8,256,512]{3,2,1,0:T(8,128)(2,1)} fusion(bf16[1,8,512,512]{3,2,1,0:T(8,128)(2,1)} %param.8, s32[]{:T(128)S(6)} %select_n.11), kind=kLoop, calls=%fused_computation.14 | loop fusion | bytes 4194308 | tf_op jit(solution)/shard_map/dynamic_slice | solution.py:133
  29.9 7.6 %collective-permute-start.3 = (bf16[2048,512]{1,0:T(8,128)(2,1)}, bf16[2048,512]{1,0:T(8,128)(2,1)S(1)}, u32[]{:S(2)}, u32[]{:S(2)}) collective-permute-start(bf16[2048,512]{1,0:T(8,128)(2,1)} %bitcast.13), channel_id=1, source_target_pairs={{16,0},{32,16},{48,32},{64,48},{80,64},{96,80},{112,96},{128,112},... | collective-permute-start | bytes 6291464 | tf_op jit(solution)/shard_map/ppermute | solution.py:134
  37.6 0.9 broadcast_in_dim.6
  38.5 7.2 %all-to-all-start = ((bf16[16,4,32,128]{3,2,1,0:T(8,128)(2,1)}), bf16[16,4,32,128]{3,2,1,0:T(8,128)(2,1)S(1)}, u32[]{:S(2)}, u32[]{:S(2)}) async-start(bf16[16,4,32,128]{3,2,1,0:T(8,128)(2,1)} %bitcast.2), calls=%async_computation | async-start | bytes 1048576 | tf_op jit(solution)/shard_map/all_to_all | solution.py:112
  45.8 2.0 %collective-permute-start = (bf16[384,512]{1,0:T(8,128)(2,1)S(1)}, bf16[384,512]{1,0:T(8,128)(2,1)S(1)}, u32[]{:S(2)}, u32[]{:S(2)}) collective-permute-start(bf16[384,512]{1,0:T(8,128)(2,1)S(1)} %pad_maximum_fusion.own), channel_id=1, source_target_pairs={{0,1},{1,2},{2,3},{3,0},{4,5},{5,6},{6,7},{7,4},{8,9},{9,10},{10,1... | collective-permute-start | bytes 1179656 | tf_op jit(solution)/shard_map/ppermute | solution.py:109
  47.8 3.8 %collective-permute-start.1 = (bf16[384,512]{1,0:T(8,128)(2,1)S(1)}, bf16[384,512]{1,0:T(8,128)(2,1)}, u32[]{:S(2)}, u32[]{:S(2)}) collective-permute-start(bf16[384,512]{1,0:T(8,128)(2,1)S(1)} %pad_maximum_fusion.own), channel_id=1, source_target_pairs={{0,3},{1,0},{2,1},{3,2},{4,7},{5,4},{6,5},{7,6},{8,11},{9,8},{10,9... | collective-permute-start | bytes 1179656 | tf_op jit(solution)/shard_map/ppermute | solution.py:109
  51.6 3.4 %collective-permute-start.2 = (bf16[384,512]{1,0:T(8,128)(2,1)S(1)}, bf16[384,512]{1,0:T(8,128)(2,1)}, u32[]{:S(2)}, u32[]{:S(2)}) collective-permute-start(bf16[384,512]{1,0:T(8,128)(2,1)S(1)} %pad_maximum_fusion.own), channel_id=1, source_target_pairs={{0,2},{1,3},{2,0},{3,1},{4,6},{5,7},{6,4},{7,5},{8,10},{9,11},{10,... | collective-permute-start | bytes 1179656 | tf_op jit(solution)/shard_map/ppermute | solution.py:109
  55.0 0.1 copy.14
  55.2 4.2 %collective-permute-done.near = bf16[384,512]{1,0:T(8,128)(2,1)S(1)} collective-permute-done((bf16[384,512]{1,0:T(8,128)(2,1)S(1)}, bf16[384,512]{1,0:T(8,128)(2,1)S(1)}, u32[]{:S(2)}, u32[]{:S(2)}) %collective-permute-start) | collective-permute-done | bytes 393248 | tf_op jit(solution)/shard_map/ppermute | solution.py:109
  59.5 6.0 %collective-permute-done.1.back_ = bf16[384,512]{1,0:T(8,128)(2,1)} collective-permute-done((bf16[384,512]{1,0:T(8,128)(2,1)S(1)}, bf16[384,512]{1,0:T(8,128)(2,1)}, u32[]{:S(2)}, u32[]{:S(2)}) %collective-permute-start.1) | collective-permute-done | bytes 393248 | tf_op jit(solution)/shard_map/ppermute | solution.py:109
  65.5 3.0 %front.1 = bf16[16,8,32,128]{3,2,1,0:T(8,128)(2,1)S(1)} custom-call(bf16[384,512]{1,0:T(8,128)(2,1)S(1)} %pad_maximum_fusion.own, bf16[384,512]{1,0:T(8,128)(2,1)S(1)} %collective-permute-done.near, bf16[384,512]{1,0:T(8,128)(2,1)} %collective-permute-done.1.back_, bf16[384,512]{1,0:T(8,128)(2,1)} %collective-permute-done.2.far, ...), custom_call_target="tpu_custom_call" | custom-call | flops 2000000000 | bytes 4000000 | tf_op jit(solution)/shard_map/front/pallas_call | solution.py:114
  68.4 20.1 %all_to_all.16 = bf16[16,8,32,128]{3,2,1,0:T(8,128)(2,1)S(1)} all-to-all(bf16[16,8,32,128]{3,2,1,0:T(8,128)(2,1)S(1)} %front.1), channel_id=1, replica_groups=mesh['sec'=32,'bond'=16] {'bond'}, dimensions={0} | all-to-all | bytes 2097152 | tf_op jit(solution)/shard_map/all_to_all | solution.py:124
  88.5 0.3 convert_element_type.24
  88.8 0.2 fusion.3
  89.2 2.8 %collective-permute-start.5 = (bf16[256,512]{1,0:T(8,128)(2,1)S(1)}, bf16[256,512]{1,0:T(8,128)(2,1)S(1)}, u32[]{:S(2)}, u32[]{:S(2)}) collective-permute-start(bf16[256,512]{1,0:T(8,128)(2,1)S(1)} %bitcast.26), channel_id=1, source_target_pairs={{0,1},{1,0},{2,3},{3,2},{4,5},{5,4},{6,7},{7,6},{8,9},{9,8},{10,11... | collective-permute-start | bytes 786440 | tf_op jit(solution)/shard_map/ppermute | solution.py:128
  92.0 0.3 fusion
  92.3 0.4 copy.20
  92.7 0.5 reshape.48.mix
  93.2 4.2 %collective-permute-done.5.left = bf16[256,512]{1,0:T(8,128)(2,1)S(1)} collective-permute-done((bf16[256,512]{1,0:T(8,128)(2,1)S(1)}, bf16[256,512]{1,0:T(8,128)(2,1)S(1)}, u32[]{:S(2)}, u32[]{:S(2)}) %collective-permute-start.5) | collective-permute-done | bytes 262176 | tf_op jit(solution)/shard_map/ppermute | solution.py:128
  97.5 1.6 %all-gather.2.cloned.1.call-done.pair = bf16[512,4096]{1,0:T(8,128)(2,1)} async-done(((bf16[128,4096]{1,0:T(8,128)(2,1)}), bf16[512,4096]{1,0:T(8,128)(2,1)}) %all-gather.2.cloned.1.call-update) | async-done | bytes 4194320 | tf_op jit(solution)/shard_map/all_gather | solution.py:107
  99.0 2.2 %copy-done.1 = bf16[512,4096]{1,0:T(8,128)(2,1)S(1)} copy-done((bf16[512,4096]{1,0:T(8,128)(2,1)S(1)}, bf16[512,4096]{1,0:T(8,128)(2,1)}, u32[]{:S(2)}) %copy-start.1) | copy-done | bytes 4194328
  101.2 4.2 %back.3 = bf16[512,512]{1,0:T(8,128)(2,1)S(1)} custom-call(bf16[256,512]{1,0:T(8,128)(2,1)S(1)} %collective-permute-done.5.left, bf16[512,4096]{1,0:T(8,128)(2,1)S(1)} %copy-done.1, bf16[128,128]{1,0:T(8,128)(2,1)S(1)} %reshape.48.mix, bf16[2048,512]{1,0:T(8,128)(2,1)S(1)} %collective-permute-done.3.right), custom_call_target="tpu_custom_call" | custom-call | flops 2500000000 | bytes 8000000 | tf_op jit(solution)/shard_map/back/pallas_call | solution.py:77
  105.4 2.4 %collective-permute-start.6 = (bf16[512,512]{1,0:T(8,128)(2,1)S(1)}, bf16[512,512]{1,0:T(8,128)(2,1)S(1)}, u32[]{:S(2)}, u32[]{:S(2)}) collective-permute-start(bf16[512,512]{1,0:T(8,128)(2,1)S(1)} %back.3), channel_id=1, source_target_pairs={{0,17},{1,16},{2,19},{3,18},{4,21},{5,20},{6,23},{7,22},{8,25},{9,... | collective-permute-start | bytes 1572872 | tf_op jit(solution)/shard_map/ppermute | solution.py:139
  107.9 4.2 %back.2 = bf16[512,512]{1,0:T(8,128)(2,1)S(1)} custom-call(bf16[256,512]{1,0:T(8,128)(2,1)S(1)} %bitcast.27, bf16[512,4096]{1,0:T(8,128)(2,1)S(1)} %copy-done.2, bf16[128,128]{1,0:T(8,128)(2,1)S(1)} %reshape.48.mix, bf16[2048,512]{1,0:T(8,128)(2,1)S(1)} %collective-permute-done.3.right), custom_call_target="tpu_custom_call" | custom-call | flops 2500000000 | bytes 8000000 | tf_op jit(solution)/shard_map/back/pallas_call | solution.py:77
  112.1 2.9 %collective-permute-start.4 = (bf16[512,512]{1,0:T(8,128)(2,1)S(1)}, bf16[512,512]{1,0:T(8,128)(2,1)S(1)}, u32[]{:S(2)}, u32[]{:S(2)}) collective-permute-start(bf16[512,512]{1,0:T(8,128)(2,1)S(1)} %back.2), channel_id=1, source_target_pairs={{0,16},{1,17},{2,18},{3,19},{4,20},{5,21},{6,22},{7,23},{8,24},{9,... | collective-permute-start | bytes 1572872 | tf_op jit(solution)/shard_map/ppermute | solution.py:139
  115.0 8.1 %collective-permute-done.6 = bf16[512,512]{1,0:T(8,128)(2,1)S(1)} collective-permute-done((bf16[512,512]{1,0:T(8,128)(2,1)S(1)}, bf16[512,512]{1,0:T(8,128)(2,1)S(1)}, u32[]{:S(2)}, u32[]{:S(2)}) %collective-permute-start.6) | collective-permute-done | bytes 524320 | tf_op jit(solution)/shard_map/ppermute | solution.py:139
  123.0 5.8 %collective-permute-done.4 = bf16[512,512]{1,0:T(8,128)(2,1)S(1)} collective-permute-done((bf16[512,512]{1,0:T(8,128)(2,1)S(1)}, bf16[512,512]{1,0:T(8,128)(2,1)S(1)}, u32[]{:S(2)}, u32[]{:S(2)}) %collective-permute-start.4) | collective-permute-done | bytes 524320 | tf_op jit(solution)/shard_map/ppermute | solution.py:139
  128.9 0.1 add_convert_fusion
  129.0 0.9 reshape.50
  (24 shorter events, 0.6 us)
Async XLA Ops:
  7.2 91.9 %all-gather.2.cloned.1.call-start = ((), (), s32[]{:S(2)}) async-start(), calls=%async_computation.3 | async-start | bytes 5242880 | tf_op jit(solution)/shard_map/all_gather | solution.py:107
  26.7 10.8 %copy-start.3 = (bf16[1,32,4,512]{3,2,1,0:T(4,128)(2,1)S(1)}, bf16[1,32,4,512]{3,2,1,0:T(4,128)(2,1)}, u32[]{:S(2)}) copy-start(bf16[1,32,4,512]{3,2,1,0:T(4,128)(2,1)} %param.6) | copy-start | bytes 393220
  29.9 15.8 %copy-start.5 = (bf16[1,32,8,512]{3,2,1,0:T(8,128)(2,1)S(1)}, bf16[1,32,8,512]{3,2,1,0:T(8,128)(2,1)}, u32[]{:S(2)}) copy-start(bf16[1,32,8,512]{3,2,1,0:T(8,128)(2,1)} %param.5) | copy-start | bytes 786436
  29.9 25.1 %copy-start.4 = (bf16[8,8,4,4]{1,3,2,0:T(4,128)(2,1)S(1)}, bf16[8,8,4,4]{1,3,2,0:T(4,128)(2,1)}, u32[]{:S(2)}) copy-start(bf16[8,8,4,4]{1,3,2,0:T(4,128)(2,1)} %param.9) | copy-start | bytes 6148
  29.9 67.6 %collective-permute-start.3 = (bf16[2048,512]{1,0:T(8,128)(2,1)}, bf16[2048,512]{1,0:T(8,128)(2,1)S(1)}, u32[]{:S(2)}, u32[]{:S(2)}) collective-permute-start(bf16[2048,512]{1,0:T(8,128)(2,1)} %bitcast.13), channel_id=1, source_target_pairs={{16,0},{32,16},{48,32},{64,48},{80,64},{96,80},{112,96},{128,112},... | collective-permute-start | bytes 6291464 | tf_op jit(solution)/shard_map/ppermute | solution.py:134
  38.5 26.9 %all-to-all-start = ((bf16[16,4,32,128]{3,2,1,0:T(8,128)(2,1)}), bf16[16,4,32,128]{3,2,1,0:T(8,128)(2,1)S(1)}, u32[]{:S(2)}, u32[]{:S(2)}) async-start(bf16[16,4,32,128]{3,2,1,0:T(8,128)(2,1)} %bitcast.2), calls=%async_computation | async-start | bytes 1048576 | tf_op jit(solution)/shard_map/all_to_all | solution.py:112
  45.8 13.7 %collective-permute-start = (bf16[384,512]{1,0:T(8,128)(2,1)S(1)}, bf16[384,512]{1,0:T(8,128)(2,1)S(1)}, u32[]{:S(2)}, u32[]{:S(2)}) collective-permute-start(bf16[384,512]{1,0:T(8,128)(2,1)S(1)} %pad_maximum_fusion.own), channel_id=1, source_target_pairs={{0,1},{1,2},{2,3},{3,0},{4,5},{5,6},{6,7},{7,4},{8,9},{9,10},{10,1... | collective-permute-start | bytes 1179656 | tf_op jit(solution)/shard_map/ppermute | solution.py:109
  47.8 17.7 %collective-permute-start.1 = (bf16[384,512]{1,0:T(8,128)(2,1)S(1)}, bf16[384,512]{1,0:T(8,128)(2,1)}, u32[]{:S(2)}, u32[]{:S(2)}) collective-permute-start(bf16[384,512]{1,0:T(8,128)(2,1)S(1)} %pad_maximum_fusion.own), channel_id=1, source_target_pairs={{0,3},{1,0},{2,1},{3,2},{4,7},{5,4},{6,5},{7,6},{8,11},{9,8},{10,9... | collective-permute-start | bytes 1179656 | tf_op jit(solution)/shard_map/ppermute | solution.py:109
  51.6 13.8 %collective-permute-start.2 = (bf16[384,512]{1,0:T(8,128)(2,1)S(1)}, bf16[384,512]{1,0:T(8,128)(2,1)}, u32[]{:S(2)}, u32[]{:S(2)}) collective-permute-start(bf16[384,512]{1,0:T(8,128)(2,1)S(1)} %pad_maximum_fusion.own), channel_id=1, source_target_pairs={{0,2},{1,3},{2,0},{3,1},{4,6},{5,7},{6,4},{7,5},{8,10},{9,11},{10,... | collective-permute-start | bytes 1179656 | tf_op jit(solution)/shard_map/ppermute | solution.py:109
  89.2 18.7 %copy-start = (bf16[32,8,4,128]{3,1,2,0:T(8,128)(2,1)}, bf16[32,8,4,128]{3,1,2,0:T(8,128)(2,1)S(1)}, u32[]{:S(2)}) copy-start(bf16[32,8,4,128]{3,1,2,0:T(8,128)(2,1)S(1)} %copy.35) | copy-start | bytes 786436
  89.2 8.3 %collective-permute-start.5 = (bf16[256,512]{1,0:T(8,128)(2,1)S(1)}, bf16[256,512]{1,0:T(8,128)(2,1)S(1)}, u32[]{:S(2)}, u32[]{:S(2)}) collective-permute-start(bf16[256,512]{1,0:T(8,128)(2,1)S(1)} %bitcast.26), channel_id=1, source_target_pairs={{0,1},{1,0},{2,3},{3,2},{4,5},{5,4},{6,7},{7,6},{8,9},{9,8},{10,11... | collective-permute-start | bytes 786440 | tf_op jit(solution)/shard_map/ppermute | solution.py:128
  99.0 2.2 %copy-start.1 = (bf16[512,4096]{1,0:T(8,128)(2,1)S(1)}, bf16[512,4096]{1,0:T(8,128)(2,1)}, u32[]{:S(2)}) copy-start(bf16[512,4096]{1,0:T(8,128)(2,1)} %all-gather.2.cloned.1.call-done.pair) | copy-start | bytes 12582916
  101.2 6.6 %copy-start.2 = (bf16[512,4096]{1,0:T(8,128)(2,1)S(1)}, bf16[512,4096]{1,0:T(8,128)(2,1)}, u32[]{:S(2)}) copy-start(bf16[512,4096]{1,0:T(8,128)(2,1)} %all-gather.2.cloned.1.call-done.pair) | copy-start | bytes 12582916
  105.4 17.6 %collective-permute-start.6 = (bf16[512,512]{1,0:T(8,128)(2,1)S(1)}, bf16[512,512]{1,0:T(8,128)(2,1)S(1)}, u32[]{:S(2)}, u32[]{:S(2)}) collective-permute-start(bf16[512,512]{1,0:T(8,128)(2,1)S(1)} %back.3), channel_id=1, source_target_pairs={{0,17},{1,16},{2,19},{3,18},{4,21},{5,20},{6,23},{7,22},{8,25},{9,... | collective-permute-start | bytes 1572872 | tf_op jit(solution)/shard_map/ppermute | solution.py:139
  112.1 16.8 %collective-permute-start.4 = (bf16[512,512]{1,0:T(8,128)(2,1)S(1)}, bf16[512,512]{1,0:T(8,128)(2,1)S(1)}, u32[]{:S(2)}, u32[]{:S(2)}) collective-permute-start(bf16[512,512]{1,0:T(8,128)(2,1)S(1)} %back.2), channel_id=1, source_target_pairs={{0,16},{1,17},{2,18},{3,19},{4,20},{5,21},{6,22},{7,23},{8,24},{9,... | collective-permute-start | bytes 1572872 | tf_op jit(solution)/shard_map/ppermute | solution.py:139
Sparse Core Ops, SparseCore 0:
  26.9 72.1 all-gather.1

commit v4 on v3

--- a/solution.py
+++ b/solution.py
@@ -15,6 +15,11 @@
 
 def line_route(distance):
     return [(i, i - i % LINE + (i + distance) % LINE) for i in range(LINE * LINE)]
+
+
+def column_route(distance):
+    size = LINE * LINE
+    return [(i, (i + LINE * distance) % size) for i in range(size)]
 
 
 def front(own, near, back_, far, cols, local, out, first, second):
@@ -49,15 +54,18 @@
             out[:, n + i] = o[:, 128 * i : 128 * i + 128].reshape(16, 32, 128)
 
 
-def back(left, pair, mix, right, out, mixed, proj, env, sem):
+def back(offsets, left, own, up, down, far_a, far_b, mix, right, out, ket, mixed, proj, env, sem):
     j = pl.program_id(0)
     fetch = pltpu.make_async_copy(right, env, sem)
 
     @pl.when(j == 0)
     def _():
         fetch.start()
+        for i in range(4):
+            ket[:, 128 * i : 128 * i + 128] = left[:, pl.ds(pl.multiple_of(offsets[i], 128), 128)]
 
-    m = jnp.dot(left[...], pair[...], preferred_element_type=F32)
+    pair = jnp.concatenate([own[...], up[...], down[...], far_a[...], far_b[...]], axis=0)
+    m = jnp.dot(ket[...], pair, preferred_element_type=F32)
     for h in range(2):
         part = [m[:, 256 * i : 256 * i + 256].reshape(32, 8, 256) for i in (2 * h, 2 * h + 1)]
         at = pl.ds(pl.multiple_of(32 * j + 16 * h, 16), 16)
@@ -73,19 +81,21 @@
         out[...] = jnp.dot(proj[...], env[...], preferred_element_type=F32).astype(BF)
 
 
-def applied(left, pair, mix, right):
+def applied(offsets, left, pieces, mix, right):
     return pl.pallas_call(
         back,
         grid=(4,),
         out_shape=jax.ShapeDtypeStruct((512, 512), BF),
         in_specs=[
+            pl.BlockSpec(memory_space=pltpu.SMEM),
             pl.BlockSpec((256, 512), lambda j: (0, 0)),
-            pl.BlockSpec((512, 1024), lambda j: (0, j)),
+            *[pl.BlockSpec((p.shape[0], 1024), lambda j: (0, j)) for p in pieces],
             pl.BlockSpec((128, 128), lambda j: (0, 0)),
             pl.BlockSpec(memory_space=pl.ANY),
         ],
         out_specs=pl.BlockSpec((512, 512), lambda j: (0, 0)),
         scratch_shapes=[
+            pltpu.VMEM((256, 512), BF),
             pltpu.VMEM((32, 128, 256), BF),
             pltpu.VMEM((512, 2048), BF),
             pltpu.VMEM((2048, 512), BF),
@@ -94,17 +104,22 @@
         compiler_params=pltpu.CompilerParams(vmem_limit_bytes=32 << 20),
         cost_estimate=pl.CostEstimate(flops=2_500_000_000, bytes_accessed=8_000_000, transcendentals=0),
         name="back",
-    )(left, pair, mix, right)
+    )(offsets, left, *pieces, mix, right)
 
 
 def shards(left_env, site, psi, right_env, mpo):
     chi = site.shape[-1]
     lines = [[LINE * y + x for x in range(LINE)] for y in range(LINE)]
-    columns = [[LINE * y + x for y in range(LINE)] for x in range(LINE)]
     halves = psi[0].reshape(32, 16, 2, 256).transpose(2, 0, 1, 3).reshape(2, 32, 4096)
     send = jnp.broadcast_to(halves[None], (2, 2, 32, 4096)).reshape(4, 32, 4096)
     pair = lax.all_to_all(send, "bond", 0, 0, axis_index_groups=lines, tiled=True)
-    pair = lax.all_gather(pair.reshape(128, 4096), "bond", axis=0, axis_index_groups=columns, tiled=True)
+    pair = pair.reshape(128, 4096)
+    up = lax.ppermute(pair, "bond", column_route(1))
+    down = lax.ppermute(pair, "bond", column_route(-1))
+    far_a = lax.ppermute(up[:64], "bond", column_route(1))
+    far_b = lax.ppermute(down[64:], "bond", column_route(-1))
+    pieces = (pair, up, down, far_a, far_b)
+    offsets = (lax.axis_index("bond") // LINE + jnp.array([0, 3, 1, 2], jnp.int32)) % LINE * 128
     own = jnp.concatenate([left_env[0].reshape(256, chi), site[0].reshape(128, chi)], axis=0)
     blocks = [own] + [lax.ppermute(own, "bond", line_route(d)) for d in (1, -1, 2)]
     quarters = site[0].reshape(32, 4, 4, 128).transpose(2, 1, 0, 3)
@@ -134,7 +149,7 @@
     right = lax.ppermute(right, "sec", [((i + 1) % sections, i) for i in range(sections)])
     total = 0.0
     for flip, left in ((0, source), (1, other)):
-        part = applied(left, pair, two_site, right)
+        part = applied(offsets, left, pieces, two_site, right)
         route = [(16 * s + b, (s + 1) % sections * 16 + (b ^ flip)) for s in range(sections) for b in range(16)]
         total = total + lax.ppermute(part, ("sec", "bond"), route).astype(F32)
     return (new_left[None], total.astype(BF).reshape(1, 32, 4, 4, chi))

time: 137 us -> 132 us (0.964)
  the two profiles are of different devices: /device:TPU:6 before, /device:TPU:1 now
where the time goes in v4:
time: 132 us; the launch traced here: 131 us
  starting transfers between devices  69.1 us (52%)
  waiting for transfers between devices  29 us (22%)
  Pallas kernels  15.2 us (12%)
  local copies, waits for them, and re-layouts  13.4 us (10%)
  other arithmetic  1.89 us (1%)
    ppermute x2, waiting for transfers between devices, shards(): total = total + lax.ppermute(part, ('sec', 'bond'), route).astype(F32)  16 us
    ppermute x2, starting transfers between devices, shards(): total = total + lax.ppermute(part, ('sec', 'bond'), route).astype(F32)  12.5 us
    pallas_call x2, Pallas kernels, applied(): pl.pallas_call(back, grid=(4,), out_shape=jax.ShapeDtypeStruct((512, 512)...  11.3 us
    ppermute x3, starting transfers between devices, shards(): lax.ppermute(own, 'bond', line_route(d))  10.5 us
    all_to_all x1, starting transfers between devices, shards(): cols = lax.all_to_all(send, 'bond', 0, 0, tiled=True)  9.23 us
    all_to_all x1, starting transfers between devices, shards(): lax.all_to_all(fresh, 'bond', 0, 0, tiled=True).reshape(4, 4, 8, 32, 128)  8.06 us
    all_to_all x1, waiting for transfers between devices, shards(): lax.all_to_all(send, 'bond', 0, 0, axis_index_groups=lines, tiled=True)  6.25 us
    ppermute x1, starting transfers between devices, shards(): other = lax.ppermute(source, 'bond', [(i, i ^ 1) for i in range(16)])  6.19 us
  transfers between devices with their start and end apart: 14, of which 6 were waited for; matrix products, arithmetic and copies ran while one was open for 10% of the time, Pallas kernels for 12%

profile of v4, /device:TPU:1, one launch (start us, length us, event | category | flops | bytes accessed | tf_op | source)
XLA Modules:
  0.0 130.9 jit_solution(17154231154451121262)
XLA Ops:
  0.6 1.2 reshape_squeeze.15
  2.2 1.1 broadcast_in_dim.15
  3.3 4.8 %all-to-all-start.2 = ((bf16[4,32,4096]{2,1,0:T(8,128)(2,1)}), bf16[4,32,4096]{2,1,0:T(8,128)(2,1)S(1)}, u32[]{:S(2)}, u32[]{:S(2)}) async-start(bf16[4,32,4096]{2,1,0:T(8,128)(2,1)} %bitcast.8), calls=%async_computation.2 | async-start | bytes 2097152 | tf_op jit(solution)/shard_map/all_to_all | solution.py:115
  8.3 3.4 %collective-permute-start = (bf16[384,512]{1,0:T(8,128)(2,1)S(1)}, bf16[384,512]{1,0:T(8,128)(2,1)S(1)}, u32[]{:S(2)}, u32[]{:S(2)}) collective-permute-start(bf16[384,512]{1,0:T(8,128)(2,1)S(1)} %pad_maximum_fusion.own), channel_id=1, source_target_pairs={{0,1},{1,2},{2,3},{3,0},{4,5},{5,6},{6,7},{7,4},{8,9},{9,10},{10,1... | collective-permute-start | bytes 1179656 | tf_op jit(solution)/shard_map/ppermute | solution.py:124
  11.8 6.2 %all-to-all-done.2 = bf16[4,32,4096]{2,1,0:T(8,128)(2,1)S(1)} async-done(((bf16[4,32,4096]{2,1,0:T(8,128)(2,1)}), bf16[4,32,4096]{2,1,0:T(8,128)(2,1)S(1)}, u32[]{:S(2)}, u32[]{:S(2)}) %all-to-all-start.2) | async-done | bytes 1048608 | tf_op jit(solution)/shard_map/all_to_all | solution.py:115
  18.0 0.9 broadcast_in_dim.6
  18.9 9.2 %all-to-all-start = ((bf16[16,4,32,128]{3,2,1,0:T(8,128)(2,1)}), bf16[16,4,32,128]{3,2,1,0:T(8,128)(2,1)S(1)}, u32[]{:S(2)}, u32[]{:S(2)}) async-start(bf16[16,4,32,128]{3,2,1,0:T(8,128)(2,1)} %bitcast.2), calls=%async_computation | async-start | bytes 1048576 | tf_op jit(solution)/shard_map/all_to_all | solution.py:127
  28.2 3.0 %constant_dynamic-slice_fusion = bf16[1,8,256,512]{3,2,1,0:T(8,128)(2,1)} fusion(bf16[1,8,512,512]{3,2,1,0:T(8,128)(2,1)} %param.9, s32[]{:T(128)S(6)} %select_n.23), kind=kLoop, calls=%fused_computation.19 | loop fusion | bytes 4194308 | tf_op jit(solution)/shard_map/dynamic_slice | solution.py:148
  31.2 4.9 %collective-permute-start.7 = (bf16[2048,512]{1,0:T(8,128)(2,1)}, bf16[2048,512]{1,0:T(8,128)(2,1)}, u32[]{:S(2)}, u32[]{:S(2)}) collective-permute-start(bf16[2048,512]{1,0:T(8,128)(2,1)} %bitcast.13), channel_id=1, source_target_pairs={{16,0},{32,16},{48,32},{64,48},{80,64},{96,80},{112,96},{128,112},... | collective-permute-start | bytes 6291464 | tf_op jit(solution)/shard_map/ppermute | solution.py:149
  36.1 4.6 %collective-permute-start.1 = (bf16[384,512]{1,0:T(8,128)(2,1)S(1)}, bf16[384,512]{1,0:T(8,128)(2,1)}, u32[]{:S(2)}, u32[]{:S(2)}) collective-permute-start(bf16[384,512]{1,0:T(8,128)(2,1)S(1)} %pad_maximum_fusion.own), channel_id=1, source_target_pairs={{0,3},{1,0},{2,1},{3,2},{4,7},{5,4},{6,5},{7,6},{8,11},{9,8},{10,9... | collective-permute-start | bytes 1179656 | tf_op jit(solution)/shard_map/ppermute | solution.py:124
  40.8 2.5 %collective-permute-start.2 = (bf16[384,512]{1,0:T(8,128)(2,1)S(1)}, bf16[384,512]{1,0:T(8,128)(2,1)}, u32[]{:S(2)}, u32[]{:S(2)}) collective-permute-start(bf16[384,512]{1,0:T(8,128)(2,1)S(1)} %pad_maximum_fusion.own), channel_id=1, source_target_pairs={{0,2},{1,3},{2,0},{3,1},{4,6},{5,7},{6,4},{7,5},{8,10},{9,11},{10,... | collective-permute-start | bytes 1179656 | tf_op jit(solution)/shard_map/ppermute | solution.py:124
  43.3 3.1 %collective-permute-start.3 = (bf16[128,4096]{1,0:T(8,128)(2,1)S(1)}, bf16[128,4096]{1,0:T(8,128)(2,1)S(1)}, u32[]{:S(2)}, u32[]{:S(2)}) collective-permute-start(bf16[128,4096]{1,0:T(8,128)(2,1)S(1)} %bitcast.26), channel_id=1, source_target_pairs={{0,4},{1,5},{2,6},{3,7},{4,8},{5,9},{6,10},{7,11},{8,12},{9,13},{1... | collective-permute-start | bytes 3145736 | tf_op jit(solution)/shard_map/ppermute | solution.py:117
  46.4 3.4 %collective-permute-start.4 = (bf16[128,4096]{1,0:T(8,128)(2,1)S(1)}, bf16[128,4096]{1,0:T(8,128)(2,1)}, u32[]{:S(2)}, u32[]{:S(2)}) collective-permute-start(bf16[128,4096]{1,0:T(8,128)(2,1)S(1)} %bitcast.27), channel_id=1, source_target_pairs={{0,12},{1,13},{2,14},{3,15},{4,0},{5,1},{6,2},{7,3},{8,4},{9,5},{1... | collective-permute-start | bytes 3145736 | tf_op jit(solution)/shard_map/ppermute | solution.py:118
  50.0 0.9 collective-permute-done.2.far
  50.9 3.9 %front.1 = bf16[16,8,32,128]{3,2,1,0:T(8,128)(2,1)} custom-call(bf16[384,512]{1,0:T(8,128)(2,1)S(1)} %pad_maximum_fusion.own, bf16[384,512]{1,0:T(8,128)(2,1)S(1)} %collective-permute-done.near, bf16[384,512]{1,0:T(8,128)(2,1)} %collective-permute-done.1.back_, bf16[384,512]{1,0:T(8,128)(2,1)} %collective-permute-done.2.far, ...), custom_call_target="tpu_custom_call" | custom-call | flops 2000000000 | bytes 4000000 | tf_op jit(solution)/shard_map/front/pallas_call | solution.py:129
  54.9 8.1 %all-to-all-start.1 = ((bf16[16,8,32,128]{3,2,1,0:T(8,128)(2,1)}), bf16[16,8,32,128]{3,2,1,0:T(8,128)(2,1)}, u32[]{:S(2)}, u32[]{:S(2)}) async-start(bf16[16,8,32,128]{3,2,1,0:T(8,128)(2,1)} %front.1), calls=%async_computation.1 | async-start | bytes 2097152 | tf_op jit(solution)/shard_map/all_to_all | solution.py:139
  62.9 3.0 %collective-permute-done.3.up = bf16[128,4096]{1,0:T(8,128)(2,1)S(1)} collective-permute-done((bf16[128,4096]{1,0:T(8,128)(2,1)S(1)}, bf16[128,4096]{1,0:T(8,128)(2,1)S(1)}, u32[]{:S(2)}, u32[]{:S(2)}) %collective-permute-start.3) | collective-permute-done | bytes 1048608 | tf_op jit(solution)/shard_map/ppermute | solution.py:117
  66.7 2.0 %collective-permute-start.5 = (bf16[64,4096]{1,0:T(8,128)(2,1)}, bf16[64,4096]{1,0:T(8,128)(2,1)S(1)}, u32[]{:S(2)}, u32[]{:S(2)}) collective-permute-start(bf16[64,4096]{1,0:T(8,128)(2,1)} %slice.32), channel_id=1, source_target_pairs={{0,4},{1,5},{2,6},{3,7},{4,8},{5,9},{6,10},{7,11},{8,12},{9,13},{1... | collective-permute-start | bytes 1572872 | tf_op jit(solution)/shard_map/ppermute | solution.py:119
  68.8 1.9 %slice.33 = bf16[64,4096]{1,0:T(8,128)(2,1)} slice(bf16[128,4096]{1,0:T(8,128)(2,1)} %collective-permute-done.4.down), slice={[64:128], [0:4096]} | slice | bytes 1048576 | tf_op jit(solution)/shard_map/slice | solution.py:120
  70.6 4.4 %collective-permute-start.6 = (bf16[64,4096]{1,0:T(8,128)(2,1)}, bf16[64,4096]{1,0:T(8,128)(2,1)S(1)}, u32[]{:S(2)}, u32[]{:S(2)}) collective-permute-start(bf16[64,4096]{1,0:T(8,128)(2,1)} %slice.33), channel_id=1, source_target_pairs={{0,12},{1,13},{2,14},{3,15},{4,0},{5,1},{6,2},{7,3},{8,4},{9,5},{1... | collective-permute-start | bytes 1572872 | tf_op jit(solution)/shard_map/ppermute | solution.py:120
  75.1 1.2 fusion
  76.3 1.5 %convert_element_type.24 = f32[16,8,32,128]{3,2,1,0:T(8,128)S(1)} convert(bf16[16,8,32,128]{3,2,1,0:T(8,128)(2,1)} %all-to-all-done.1) | non-fusion elementwise | flops 524288 | bytes 3145728 | tf_op jit(solution)/shard_map/convert_element_type | solution.py:139
  78.2 6.2 %collective-permute-start.9 = (bf16[256,512]{1,0:T(8,128)(2,1)S(1)}, bf16[256,512]{1,0:T(8,128)(2,1)}, u32[]{:S(2)}, u32[]{:S(2)}) collective-permute-start(bf16[256,512]{1,0:T(8,128)(2,1)S(1)} %bitcast.30), channel_id=1, source_target_pairs={{0,1},{1,0},{2,3},{3,2},{4,5},{5,4},{6,7},{7,6},{8,9},{9,8},{10,11... | collective-permute-start | bytes 786440 | tf_op jit(solution)/shard_map/ppermute | solution.py:143
  84.4 1.2 copy.21
  85.6 1.5 %reshape.48.mix = bf16[128,128]{1,0:T(8,128)(2,1)S(1)} reshape(bf16[8,4,4,4,4,8]{5,4,3,2,1,0:T(4,128)(2,1)} %copy.21) | data formatting | bytes 65536 | tf_op jit(solution)/shard_map/reshape | solution.py:145
  87.9 2.2 %collective-permute-done.6.far_b = bf16[64,4096]{1,0:T(8,128)(2,1)S(1)} collective-permute-done((bf16[64,4096]{1,0:T(8,128)(2,1)}, bf16[64,4096]{1,0:T(8,128)(2,1)S(1)}, u32[]{:S(2)}, u32[]{:S(2)}) %collective-permute-start.6) | collective-permute-done | bytes 524320 | tf_op jit(solution)/shard_map/ppermute | solution.py:120
  90.0 5.6 %back.2 = bf16[512,512]{1,0:T(8,128)(2,1)S(1)} custom-call(s32[4]{0:T(128)S(1)} %fusion.7.offsets, bf16[256,512]{1,0:T(8,128)(2,1)S(1)} %bitcast.31, bf16[128,4096]{1,0:T(8,128)(2,1)S(1)} %bitcast.28, bf16[128,4096]{1,0:T(8,128)(2,1)S(1)} %collective-permute-done.3.up, bf16[128,4096]{1,0:T(8,128)(2,1)} %collective-permute-done.4.down, ...), custom_call_target="tpu_custom_call" | custom-call | flops 2500000000 | bytes 8000000 | tf_op jit(solution)/shard_map/back/pallas_call | solution.py:85
  95.6 10.0 %collective-permute-start.8 = (bf16[512,512]{1,0:T(8,128)(2,1)S(1)}, bf16[512,512]{1,0:T(8,128)(2,1)S(1)}, u32[]{:S(2)}, u32[]{:S(2)}) collective-permute-start(bf16[512,512]{1,0:T(8,128)(2,1)S(1)} %back.2), channel_id=1, source_target_pairs={{0,16},{1,17},{2,18},{3,19},{4,20},{5,21},{6,22},{7,23},{8,24},{9,... | collective-permute-start | bytes 1572872 | tf_op jit(solution)/shard_map/ppermute | solution.py:154
  105.7 5.7 %back.3 = bf16[512,512]{1,0:T(8,128)(2,1)S(1)} custom-call(s32[4]{0:T(128)S(1)} %fusion.7.offsets, bf16[256,512]{1,0:T(8,128)(2,1)} %collective-permute-done.9.left, bf16[128,4096]{1,0:T(8,128)(2,1)S(1)} %bitcast.29, bf16[128,4096]{1,0:T(8,128)(2,1)S(1)} %collective-permute-done.3.up, bf16[128,4096]{1,0:T(8,128)(2,1)} %collective-permute-done.4.down, ...), custom_call_target="tpu_custom_call" | custom-call | flops 2500000000 | bytes 8000000 | tf_op jit(solution)/shard_map/back/pallas_call | solution.py:85
  111.4 2.4 %collective-permute-start.10 = (bf16[512,512]{1,0:T(8,128)(2,1)S(1)}, bf16[512,512]{1,0:T(8,128)(2,1)S(1)}, u32[]{:S(2)}, u32[]{:S(2)}) collective-permute-start(bf16[512,512]{1,0:T(8,128)(2,1)S(1)} %back.3), channel_id=1, source_target_pairs={{0,17},{1,16},{2,19},{3,18},{4,21},{5,20},{6,23},{7,22},{8,25},{9,... | collective-permute-start | bytes 1572872 | tf_op jit(solution)/shard_map/ppermute | solution.py:154
  113.8 16.0 %collective-permute-done.10 = bf16[512,512]{1,0:T(8,128)(2,1)S(1)} collective-permute-done((bf16[512,512]{1,0:T(8,128)(2,1)S(1)}, bf16[512,512]{1,0:T(8,128)(2,1)S(1)}, u32[]{:S(2)}, u32[]{:S(2)}) %collective-permute-start.10) | collective-permute-done | bytes 524320 | tf_op jit(solution)/shard_map/ppermute | solution.py:154
  129.9 0.9 reshape.50
  (34 shorter events, 2.8 us)
Async XLA Ops:
  2.2 6.0 %copy-start.2 = (bf16[1,32,4,512]{3,2,1,0:T(4,128)(2,1)S(1)}, bf16[1,32,4,512]{3,2,1,0:T(4,128)(2,1)}, u32[]{:S(2)}) copy-start(bf16[1,32,4,512]{3,2,1,0:T(4,128)(2,1)} %param.7) | copy-start | bytes 393220
  2.2 6.0 %copy-start.4 = (bf16[1,32,8,512]{3,2,1,0:T(8,128)(2,1)S(1)}, bf16[1,32,8,512]{3,2,1,0:T(8,128)(2,1)}, u32[]{:S(2)}) copy-start(bf16[1,32,8,512]{3,2,1,0:T(8,128)(2,1)} %param.6) | copy-start | bytes 786436
  3.3 14.7 %all-to-all-start.2 = ((bf16[4,32,4096]{2,1,0:T(8,128)(2,1)}), bf16[4,32,4096]{2,1,0:T(8,128)(2,1)S(1)}, u32[]{:S(2)}, u32[]{:S(2)}) async-start(bf16[4,32,4096]{2,1,0:T(8,128)(2,1)} %bitcast.8), calls=%async_computation.2 | async-start | bytes 2097152 | tf_op jit(solution)/shard_map/all_to_all | solution.py:115
  8.3 38.1 %collective-permute-start = (bf16[384,512]{1,0:T(8,128)(2,1)S(1)}, bf16[384,512]{1,0:T(8,128)(2,1)S(1)}, u32[]{:S(2)}, u32[]{:S(2)}) collective-permute-start(bf16[384,512]{1,0:T(8,128)(2,1)S(1)} %pad_maximum_fusion.own), channel_id=1, source_target_pairs={{0,1},{1,2},{2,3},{3,0},{4,5},{5,6},{6,7},{7,4},{8,9},{9,10},{10,1... | collective-permute-start | bytes 1179656 | tf_op jit(solution)/shard_map/ppermute | solution.py:124
  18.9 32.0 %all-to-all-start = ((bf16[16,4,32,128]{3,2,1,0:T(8,128)(2,1)}), bf16[16,4,32,128]{3,2,1,0:T(8,128)(2,1)S(1)}, u32[]{:S(2)}, u32[]{:S(2)}) async-start(bf16[16,4,32,128]{3,2,1,0:T(8,128)(2,1)} %bitcast.2), calls=%async_computation | async-start | bytes 1048576 | tf_op jit(solution)/shard_map/all_to_all | solution.py:127
  28.2 21.6 %copy-start.3 = (bf16[8,8,4,4]{1,3,2,0:T(4,128)(2,1)S(1)}, bf16[8,8,4,4]{1,3,2,0:T(4,128)(2,1)}, u32[]{:S(2)}) copy-start(bf16[8,8,4,4]{1,3,2,0:T(4,128)(2,1)} %param.10) | copy-start | bytes 6148
  31.2 55.9 %collective-permute-start.7 = (bf16[2048,512]{1,0:T(8,128)(2,1)}, bf16[2048,512]{1,0:T(8,128)(2,1)}, u32[]{:S(2)}, u32[]{:S(2)}) collective-permute-start(bf16[2048,512]{1,0:T(8,128)(2,1)} %bitcast.13), channel_id=1, source_target_pairs={{16,0},{32,16},{48,32},{64,48},{80,64},{96,80},{112,96},{128,112},... | collective-permute-start | bytes 6291464 | tf_op jit(solution)/shard_map/ppermute | solution.py:149
  36.1 13.9 %collective-permute-start.1 = (bf16[384,512]{1,0:T(8,128)(2,1)S(1)}, bf16[384,512]{1,0:T(8,128)(2,1)}, u32[]{:S(2)}, u32[]{:S(2)}) collective-permute-start(bf16[384,512]{1,0:T(8,128)(2,1)S(1)} %pad_maximum_fusion.own), channel_id=1, source_target_pairs={{0,3},{1,0},{2,1},{3,2},{4,7},{5,4},{6,5},{7,6},{8,11},{9,8},{10,9... | collective-permute-start | bytes 1179656 | tf_op jit(solution)/shard_map/ppermute | solution.py:124
  40.8 10.1 %collective-permute-start.2 = (bf16[384,512]{1,0:T(8,128)(2,1)S(1)}, bf16[384,512]{1,0:T(8,128)(2,1)}, u32[]{:S(2)}, u32[]{:S(2)}) collective-permute-start(bf16[384,512]{1,0:T(8,128)(2,1)S(1)} %pad_maximum_fusion.own), channel_id=1, source_target_pairs={{0,2},{1,3},{2,0},{3,1},{4,6},{5,7},{6,4},{7,5},{8,10},{9,11},{10,... | collective-permute-start | bytes 1179656 | tf_op jit(solution)/shard_map/ppermute | solution.py:124
  43.3 22.6 %collective-permute-start.3 = (bf16[128,4096]{1,0:T(8,128)(2,1)S(1)}, bf16[128,4096]{1,0:T(8,128)(2,1)S(1)}, u32[]{:S(2)}, u32[]{:S(2)}) collective-permute-start(bf16[128,4096]{1,0:T(8,128)(2,1)S(1)} %bitcast.26), channel_id=1, source_target_pairs={{0,4},{1,5},{2,6},{3,7},{4,8},{5,9},{6,10},{7,11},{8,12},{9,13},{1... | collective-permute-start | bytes 3145736 | tf_op jit(solution)/shard_map/ppermute | solution.py:117
  46.4 22.4 %collective-permute-start.4 = (bf16[128,4096]{1,0:T(8,128)(2,1)S(1)}, bf16[128,4096]{1,0:T(8,128)(2,1)}, u32[]{:S(2)}, u32[]{:S(2)}) collective-permute-start(bf16[128,4096]{1,0:T(8,128)(2,1)S(1)} %bitcast.27), channel_id=1, source_target_pairs={{0,12},{1,13},{2,14},{3,15},{4,0},{5,1},{6,2},{7,3},{8,4},{9,5},{1... | collective-permute-start | bytes 3145736 | tf_op jit(solution)/shard_map/ppermute | solution.py:118
  54.9 21.4 %all-to-all-start.1 = ((bf16[16,8,32,128]{3,2,1,0:T(8,128)(2,1)}), bf16[16,8,32,128]{3,2,1,0:T(8,128)(2,1)}, u32[]{:S(2)}, u32[]{:S(2)}) async-start(bf16[16,8,32,128]{3,2,1,0:T(8,128)(2,1)} %front.1), calls=%async_computation.1 | async-start | bytes 2097152 | tf_op jit(solution)/shard_map/all_to_all | solution.py:139
  66.7 21.1 %collective-permute-start.5 = (bf16[64,4096]{1,0:T(8,128)(2,1)}, bf16[64,4096]{1,0:T(8,128)(2,1)S(1)}, u32[]{:S(2)}, u32[]{:S(2)}) collective-permute-start(bf16[64,4096]{1,0:T(8,128)(2,1)} %slice.32), channel_id=1, source_target_pairs={{0,4},{1,5},{2,6},{3,7},{4,8},{5,9},{6,10},{7,11},{8,12},{9,13},{1... | collective-permute-start | bytes 1572872 | tf_op jit(solution)/shard_map/ppermute | solution.py:119
  70.6 19.4 %collective-permute-start.6 = (bf16[64,4096]{1,0:T(8,128)(2,1)}, bf16[64,4096]{1,0:T(8,128)(2,1)S(1)}, u32[]{:S(2)}, u32[]{:S(2)}) collective-permute-start(bf16[64,4096]{1,0:T(8,128)(2,1)} %slice.33), channel_id=1, source_target_pairs={{0,12},{1,13},{2,14},{3,15},{4,0},{5,1},{6,2},{7,3},{8,4},{9,5},{1... | collective-permute-start | bytes 1572872 | tf_op jit(solution)/shard_map/ppermute | solution.py:120
  77.8 6.6 %copy-start.5 = (s32[4]{0:T(128)S(1)}, s32[4]{0:T(128)}, u32[]{:S(2)}) copy-start(s32[4]{0:T(128)} %constant.52.clone) | copy-start | bytes 52
  77.8 6.6 %copy-start.1 = (bf16[8,4,4,4,4,8]{5,0,1,3,2,4:T(8,128)(2,1)S(1)}, bf16[8,4,4,4,4,8]{5,0,1,3,2,4:T(8,128)(2,1)}, u32[]{:S(2)}) copy-start(bf16[8,4,4,4,4,8]{5,0,1,3,2,4:T(8,128)(2,1)} %fusion) | copy-start | bytes 98308
  78.2 17.5 %copy-start = (bf16[32,8,4,128]{3,1,2,0:T(8,128)(2,1)}, bf16[32,8,4,128]{3,1,2,0:T(8,128)(2,1)S(1)}, u32[]{:S(2)}) copy-start(bf16[32,8,4,128]{3,1,2,0:T(8,128)(2,1)S(1)} %copy.36) | copy-start | bytes 786436
  78.2 27.5 %collective-permute-start.9 = (bf16[256,512]{1,0:T(8,128)(2,1)S(1)}, bf16[256,512]{1,0:T(8,128)(2,1)}, u32[]{:S(2)}, u32[]{:S(2)}) collective-permute-start(bf16[256,512]{1,0:T(8,128)(2,1)S(1)} %bitcast.30), channel_id=1, source_target_pairs={{0,1},{1,0},{2,3},{3,2},{4,5},{5,4},{6,7},{7,6},{8,9},{9,8},{10,11... | collective-permute-start | bytes 786440 | tf_op jit(solution)/shard_map/ppermute | solution.py:143
  95.6 18.2 %collective-permute-start.8 = (bf16[512,512]{1,0:T(8,128)(2,1)S(1)}, bf16[512,512]{1,0:T(8,128)(2,1)S(1)}, u32[]{:S(2)}, u32[]{:S(2)}) collective-permute-start(bf16[512,512]{1,0:T(8,128)(2,1)S(1)} %back.2), channel_id=1, source_target_pairs={{0,16},{1,17},{2,18},{3,19},{4,20},{5,21},{6,22},{7,23},{8,24},{9,... | collective-permute-start | bytes 1572872 | tf_op jit(solution)/shard_map/ppermute | solution.py:154
  111.4 18.4 %collective-permute-start.10 = (bf16[512,512]{1,0:T(8,128)(2,1)S(1)}, bf16[512,512]{1,0:T(8,128)(2,1)S(1)}, u32[]{:S(2)}, u32[]{:S(2)}) collective-permute-start(bf16[512,512]{1,0:T(8,128)(2,1)S(1)} %back.3), channel_id=1, source_target_pairs={{0,17},{1,16},{2,19},{3,18},{4,21},{5,20},{6,23},{7,22},{8,25},{9,... | collective-permute-start | bytes 1572872 | tf_op jit(solution)/shard_map/ppermute | solution.py:154

commit v5 on v4

v5 whole, which is shorter than its diff:
```python
import jax
import jax.numpy as jnp
from jax import lax
from jax.experimental import pallas as pl
from jax.experimental.pallas import tpu as pltpu
from jax.sharding import PartitionSpec as P

BF = jnp.bfloat16
F32 = jnp.float32
VM = pl.BlockSpec(memory_space=pltpu.VMEM)


LINE = 4


def line_route(distance):
    return [(i, i - i % LINE + (i + distance) % LINE) for i in range(LINE * LINE)]


def column_route(distance):
    size = LINE * LINE
    return [(i, (i + LINE * distance) % size) for i in range(size)]


def spread_out(local):
    row = lax.broadcasted_iota(jnp.int32, (256, 32), 0)
    col = lax.broadcasted_iota(jnp.int32, (256, 32), 1)
    spread = ((row >> 5) * 4 + (row & 3) == col).astype(BF)
    row = lax.broadcasted_iota(jnp.int32, (32, 256), 0)
    col = lax.broadcasted_iota(jnp.int32, (32, 256), 1)
    copies = (row == (col & 31)).astype(BF)
    kron = jnp.dot(spread, local[...], preferred_element_type=F32).astype(BF)
    kron = jnp.dot(kron, copies, preferred_element_type=F32)
    row = lax.broadcasted_iota(jnp.int32, (256, 256), 0)
    col = lax.broadcasted_iota(jnp.int32, (256, 256), 1)
    kron = jnp.where(((row >> 2) & 7) == (col >> 5), kron, 0.0).astype(BF)
    return kron


def front(own, near, back_, far, cols, local, out, first, second, held, heldc, sems):
    fetches = [pltpu.make_async_copy(ref, held.at[i], sems.at[i]) for i, ref in enumerate((own, near, back_, far))]
    fetches = [pltpu.make_async_copy(cols, heldc, sems.at[4])] + fetches
    for fetch in fetches:
        fetch.start()
    kron = spread_out(local)
    fetches[0].wait()
    cols = heldc
    ket = jnp.concatenate([cols[:, s].reshape(512, 128) for s in range(4)], axis=1)
    for g in range(4):
        fetches[1 + g].wait()
        block = held[g]
        f = jnp.dot(block[:256, :], ket, preferred_element_type=F32)
        for h in range(2):
            part = [f[:, 128 * s : 128 * s + 128].reshape(32, 8, 128) for s in (2 * h, 2 * h + 1)]
            first[32 * g : 32 * g + 32, 16 * h : 16 * h + 16, :] = jnp.concatenate(part, axis=1).astype(BF)
    for blk in range(0, 16, 2):
        f = [first[8 * i : 8 * i + 8].reshape(256, 128) for i in (blk, blk + 1)]
        o = jnp.dot(kron, jnp.concatenate(f, axis=1), preferred_element_type=F32).astype(BF)
        for i in range(2):
            second[:, 32 * (blk + i) : 32 * (blk + i) + 32, :] = o[:, 128 * i : 128 * i + 128].reshape(8, 32, 128)
    site = held[:, 256:, :].reshape(512, 512)
    for n in range(0, 8, 2):
        f = jnp.concatenate([second[n], second[n + 1]], axis=1)
        o = lax.dot_general(site, f, (((0,), (0,)), ((), ())), preferred_element_type=F32).astype(BF)
        for i in range(2):
            out[:, n + i] = o[:, 128 * i : 128 * i + 128].reshape(16, 32, 128)


def back(offsets, left, own, up, down, far_a, far_b, mix, right, out, mixed, proj):
    ket = [left[:, pl.ds(pl.multiple_of(offsets[i], 128), 128)] for i in range(4)]
    ket = jnp.concatenate(ket, axis=1)
    for h in range(8):
        at = slice(512 * h, 512 * h + 512)
        pair = jnp.concatenate([ref[:, at] for ref in (own, up, down, far_a, far_b)], axis=0)
        m = jnp.dot(ket, pair, preferred_element_type=F32)
        part = [m[:, 256 * i : 256 * i + 256].reshape(32, 8, 256) for i in range(2)]
        mixed[:, 16 * h : 16 * h + 16, :] = jnp.concatenate(part, axis=1).astype(BF)
    for p in range(32):
        o = jnp.dot(mix[...], mixed[p], preferred_element_type=F32).astype(BF)
        for k in range(8):
            proj[16 * p : 16 * p + 16, 256 * k : 256 * k + 256] = o[16 * k : 16 * k + 16, :]
    out[...] = jnp.dot(proj[...], right[...], preferred_element_type=F32).astype(BF)


def applied(offsets, left, pieces, mix, right):
    return pl.pallas_call(
        back,
        out_shape=jax.ShapeDtypeStruct((512, 512), BF),
        in_specs=[pl.BlockSpec(memory_space=pltpu.SMEM)] + [VM] * 8,
        out_specs=VM,
        scratch_shapes=[pltpu.VMEM((32, 128, 256), BF), pltpu.VMEM((512, 2048), BF)],
        compiler_params=pltpu.CompilerParams(vmem_limit_bytes=24 << 20),
        cost_estimate=pl.CostEstimate(flops=2_500_000_000, bytes_accessed=8_000_000, transcendentals=0),
        name="back",
    )(offsets, left, *pieces, mix, right)


def shards(left_env, site, psi, right_env, mpo):
    chi = site.shape[-1]
    sections = lax.axis_size("sec")
    here = lax.axis_index("bond")
    lines = [[LINE * y + x for x in range(LINE)] for y in range(LINE)]

    def next_section(block, flip):
        route = [(16 * s + b, (s + 1) % sections * 16 + (b ^ flip)) for s in range(sections) for b in range(16)]
        return lax.ppermute(block, ("sec", "bond"), route)

    own = jnp.concatenate([left_env[0].reshape(256, chi), site[0].reshape(128, chi)], axis=0)
    blocks = [own] + [lax.ppermute(own, "bond", line_route(d)) for d in (1, -1, 2)]
    pair = next_section(psi[0], 0)
    halves = pair.reshape(32, 16, 2, 256).transpose(2, 0, 1, 3).reshape(2, 32, 4096)
    send = jnp.broadcast_to(halves[None], (2, 2, 32, 4096)).reshape(4, 32, 4096)
    pair = lax.all_to_all(send, "bond", 0, 0, axis_index_groups=lines, tiled=True).reshape(128, 4096)
    local = mpo.transpose(1, 3, 2, 0).reshape(32, 32)
    two_site = jnp.einsum("mnsu,nkvw->kuwsvm", mpo, mpo, preferred_element_type=F32)
    two_site = two_site.astype(BF).reshape(128, 128)
    quarters = site[0].reshape(32, 4, 4, 128).transpose(2, 1, 0, 3)
    cols = jnp.broadcast_to(quarters[None], (4, 4, 4, 32, 128)).reshape(16, 4, 32, 128)
    offsets = (here // LINE + jnp.array([0, 3, 1, 2], jnp.int32)) % LINE * 128
    right = lax.dynamic_slice_in_dim(right_env[0], here % 2 * 256, 256, 1).reshape(2048, chi)
    pair, local, two_site, cols, offsets, right = lax.optimization_barrier(
        (pair, local, two_site, cols, offsets, right)
    )
    up = lax.ppermute(pair, "bond", column_route(1))
    down = lax.ppermute(pair, "bond", column_route(-1))
    far_a = lax.ppermute(up[:64], "bond", column_route(1))
    far_b = lax.ppermute(down[64:], "bond", column_route(-1))
    pieces = (pair, up, down, far_a, far_b)
    cols = lax.all_to_all(cols, "bond", 0, 0, tiled=True)
    fresh = pl.pallas_call(
        front,
        out_shape=jax.ShapeDtypeStruct((16, 8, 32, 128), BF),
        in_specs=[pl.BlockSpec(memory_space=pl.ANY)] * 5 + [VM],
        out_specs=VM,
        scratch_shapes=[
            pltpu.VMEM((128, 32, 128), BF),
            pltpu.VMEM((8, 512, 128), BF),
            pltpu.VMEM((4, 384, 512), BF),
            pltpu.VMEM((16, 4, 32, 128), BF),
            pltpu.SemaphoreType.DMA((5,)),
        ],
        compiler_params=pltpu.CompilerParams(vmem_limit_bytes=56 << 20),
        cost_estimate=pl.CostEstimate(flops=2_000_000_000, bytes_accessed=4_000_000, transcendentals=0),
        name="front",
    )(*blocks, cols, local)
    fresh = lax.all_to_all(fresh, "bond", 0, 0, tiled=True).reshape(4, 4, 8, 32, 128)
    fresh = [fresh[i].astype(F32) for i in range(4)]
    fresh = ((fresh[0] + fresh[1]) + (fresh[2] + fresh[3])).astype(BF)
    new_left = fresh.transpose(2, 1, 0, 3).reshape(32, 8, chi)
    source = new_left.reshape(256, chi)
    other = next_section(source, 1)
    source = next_section(source, 0)
    give = applied(offsets, other, pieces, two_site, right)
    source, give = lax.optimization_barrier((source, give))
    take = lax.ppermute(give, "bond", [(i, i ^ 1) for i in range(16)])
    keep = applied(offsets, source, pieces, two_site, right)
    total = (keep.astype(F32) + take.astype(F32)).astype(BF)
    return (new_left[None], total.reshape(1, 32, 4, 4, chi))


def solution(mesh):
    in_specs = (
        P("sec", "bond", None, None),
        P("sec", "bond", None, None),
        P("sec", "bond", None, None, None),
        P("sec", None, None, None),
        P(),
    )
    out_specs = (P("sec", "bond", None, None), P("sec", "bond", None, None, None))
    return jax.shard_map(shards, mesh=mesh, in_specs=in_specs, out_specs=out_specs, check_vma=False)
```

time: 132 us -> 128 us (0.970)
  the two profiles are of different devices: /device:TPU:1 before, /device:TPU:121 now
where the time goes in v5:
time: 128 us; the launch traced here: 127 us
  starting transfers between devices  54.9 us (43%)
  waiting for transfers between devices  42.3 us (33%)
  Pallas kernels  14.6 us (11%)
  local copies, waits for them, and re-layouts  11.7 us (9%)
  other arithmetic  2.45 us (2%)
    all_to_all x1, waiting for transfers between devices, shards(): lax.all_to_all(send, 'bond', 0, 0, axis_index_groups=lines, tiled=True)  11.2 us
    ppermute x3, starting transfers between devices, next_section(): return lax.ppermute(block, ('sec', 'bond'), route)  11 us
    ppermute x3, waiting for transfers between devices, next_section(): return lax.ppermute(block, ('sec', 'bond'), route)  10.3 us
    ppermute x3, starting transfers between devices, shards(): lax.ppermute(own, 'bond', line_route(d))  9.88 us
    pallas_call x2, Pallas kernels, applied(): pl.pallas_call(back, out_shape=jax.ShapeDtypeStruct((512, 512), BF), in_s...  9.63 us
    ppermute x3, waiting for transfers between devices, shards(): lax.ppermute(own, 'bond', line_route(d))  8.48 us
    ppermute x1, waiting for transfers between devices, shards(): take = lax.ppermute(give, 'bond', [(i, i ^ 1) for i in range(16)])  7.4 us
    ppermute x1, starting transfers between devices, shards(): take = lax.ppermute(give, 'bond', [(i, i ^ 1) for i in range(16)])  6.76 us
  transfers between devices with their start and end apart: 14, of which 8 were waited for; matrix products, arithmetic and copies ran while one was open for 8% of the time, Pallas kernels for 11%

profile of v5, /device:TPU:121, one launch (start us, length us, event | category | flops | bytes accessed | tf_op | source)
XLA Modules:
  0.0 127.3 jit_solution(7293396727884044717)
XLA Ops:
  0.7 3.4 %collective-permute-start.3 = (bf16[32,4,4,512]{3,2,1,0:T(4,128)(2,1)}, bf16[32,4,4,512]{3,2,1,0:T(4,128)(2,1)S(1)}, u32[]{:S(2)}, u32[]{:S(2)}) collective-permute-start(bf16[32,4,4,512]{3,2,1,0:T(4,128)(2,1)} %bitcast.42), channel_id=1, source_target_pairs={{0,16},{1,17},{2,18},{3,19},{4,20},{5,21},{6,22},{7,23},{8,24},{9,... | collective-permute-start | bytes 1572872 | tf_op jit(solution)/shard_map/ppermute | solution.py:106
  4.1 6.4 %collective-permute-done.3 = bf16[32,4,4,512]{3,2,1,0:T(4,128)(2,1)S(1)} collective-permute-done((bf16[32,4,4,512]{3,2,1,0:T(4,128)(2,1)}, bf16[32,4,4,512]{3,2,1,0:T(4,128)(2,1)S(1)}, u32[]{:S(2)}, u32[]{:S(2)}) %collective-permute-start.3) | collective-permute-done | bytes 524320 | tf_op jit(solution)/shard_map/ppermute | solution.py:106
  11.0 1.1 broadcast_in_dim.14
  12.2 4.0 %all-to-all-start = ((bf16[4,32,4096]{2,1,0:T(8,128)(2,1)}), bf16[4,32,4096]{2,1,0:T(8,128)(2,1)S(1)}, u32[]{:S(2)}, u32[]{:S(2)}) async-start(bf16[4,32,4096]{2,1,0:T(8,128)(2,1)} %bitcast.3), calls=%async_computation | async-start | bytes 2097152 | tf_op jit(solution)/shard_map/all_to_all | solution.py:113
  18.4 1.8 %constant_dynamic-slice_fusion = bf16[1,8,256,512]{3,2,1,0:T(8,128)(2,1)S(1)} fusion(bf16[1,8,512,512]{3,2,1,0:T(8,128)(2,1)} %param.9, s32[]{:T(128)S(6)} %select_n.23), kind=kLoop, calls=%fused_computation.16 | loop fusion | bytes 4194308 | tf_op jit(solution)/shard_map/dynamic_slice | solution.py:120
  20.3 11.2 %all-to-all-done = bf16[4,32,4096]{2,1,0:T(8,128)(2,1)S(1)} async-done(((bf16[4,32,4096]{2,1,0:T(8,128)(2,1)}), bf16[4,32,4096]{2,1,0:T(8,128)(2,1)S(1)}, u32[]{:S(2)}, u32[]{:S(2)}) %all-to-all-start) | async-done | bytes 1048608 | tf_op jit(solution)/shard_map/all_to_all | solution.py:113
  31.5 0.9 broadcast_in_dim.15
  32.4 4.8 %all-to-all-start.1 = ((bf16[16,4,32,128]{3,2,1,0:T(8,128)(2,1)}), bf16[16,4,32,128]{3,2,1,0:T(8,128)(2,1)}, u32[]{:S(2)}, u32[]{:S(2)}) async-start(bf16[16,4,32,128]{3,2,1,0:T(8,128)(2,1)} %bitcast.33), calls=%async_computation.1 | async-start | bytes 1048576 | tf_op jit(solution)/shard_map/all_to_all | solution.py:129
  37.2 1.0 pad_maximum_fusion.own
  38.2 4.6 %collective-permute-start.2 = (bf16[384,512]{1,0:T(8,128)(2,1)S(1)}, bf16[384,512]{1,0:T(8,128)(2,1)S(1)}, u32[]{:S(2)}, u32[]{:S(2)}) collective-permute-start(bf16[384,512]{1,0:T(8,128)(2,1)S(1)} %pad_maximum_fusion.own), channel_id=1, source_target_pairs={{0,2},{1,3},{2,0},{3,1},{4,6},{5,7},{6,4},{7,5},{8,10},{9,11},{10,... | collective-permute-start | bytes 1179656 | tf_op jit(solution)/shard_map/ppermute | solution.py:109
  42.8 2.8 %collective-permute-start.1 = (bf16[384,512]{1,0:T(8,128)(2,1)S(1)}, bf16[384,512]{1,0:T(8,128)(2,1)S(1)}, u32[]{:S(2)}, u32[]{:S(2)}) collective-permute-start(bf16[384,512]{1,0:T(8,128)(2,1)S(1)} %pad_maximum_fusion.own), channel_id=1, source_target_pairs={{0,3},{1,0},{2,1},{3,2},{4,7},{5,4},{6,5},{7,6},{8,11},{9,8},{10,9... | collective-permute-start | bytes 1179656 | tf_op jit(solution)/shard_map/ppermute | solution.py:109
  45.6 2.5 %collective-permute-start = (bf16[384,512]{1,0:T(8,128)(2,1)S(1)}, bf16[384,512]{1,0:T(8,128)(2,1)}, u32[]{:S(2)}, u32[]{:S(2)}) collective-permute-start(bf16[384,512]{1,0:T(8,128)(2,1)S(1)} %pad_maximum_fusion.own), channel_id=1, source_target_pairs={{0,1},{1,2},{2,3},{3,0},{4,5},{5,6},{6,7},{7,4},{8,9},{9,10},{10,1... | collective-permute-start | bytes 1179656 | tf_op jit(solution)/shard_map/ppermute | solution.py:109
  48.1 2.5 %collective-permute-start.7 = (bf16[128,4096]{1,0:T(8,128)(2,1)S(1)}, bf16[128,4096]{1,0:T(8,128)(2,1)}, u32[]{:S(2)}, u32[]{:S(2)}) collective-permute-start(bf16[128,4096]{1,0:T(8,128)(2,1)S(1)} %bitcast.29), channel_id=1, source_target_pairs={{0,12},{1,13},{2,14},{3,15},{4,0},{5,1},{6,2},{7,3},{8,4},{9,5},{1... | collective-permute-start | bytes 3145736 | tf_op jit(solution)/shard_map/ppermute | solution.py:125
  50.6 4.0 %collective-permute-start.6 = (bf16[128,4096]{1,0:T(8,128)(2,1)S(1)}, bf16[128,4096]{1,0:T(8,128)(2,1)}, u32[]{:S(2)}, u32[]{:S(2)}) collective-permute-start(bf16[128,4096]{1,0:T(8,128)(2,1)S(1)} %bitcast.30), channel_id=1, source_target_pairs={{0,4},{1,5},{2,6},{3,7},{4,8},{5,9},{6,10},{7,11},{8,12},{9,13},{1... | collective-permute-start | bytes 3145736 | tf_op jit(solution)/shard_map/ppermute | solution.py:124
  54.6 6.7 %collective-permute-done.1.back_ = bf16[384,512]{1,0:T(8,128)(2,1)S(1)} collective-permute-done((bf16[384,512]{1,0:T(8,128)(2,1)S(1)}, bf16[384,512]{1,0:T(8,128)(2,1)S(1)}, u32[]{:S(2)}, u32[]{:S(2)}) %collective-permute-start.1) | collective-permute-done | bytes 393248 | tf_op jit(solution)/shard_map/ppermute | solution.py:109
  62.1 1.8 %collective-permute-done.near = bf16[384,512]{1,0:T(8,128)(2,1)} collective-permute-done((bf16[384,512]{1,0:T(8,128)(2,1)S(1)}, bf16[384,512]{1,0:T(8,128)(2,1)}, u32[]{:S(2)}, u32[]{:S(2)}) %collective-permute-start) | collective-permute-done | bytes 393248 | tf_op jit(solution)/shard_map/ppermute | solution.py:109
  63.9 4.9 %front.1 = bf16[16,8,32,128]{3,2,1,0:T(8,128)(2,1)} custom-call(bf16[384,512]{1,0:T(8,128)(2,1)} %copy-done.1, bf16[384,512]{1,0:T(8,128)(2,1)} %collective-permute-done.near, bf16[384,512]{1,0:T(8,128)(2,1)} %copy-done.5, bf16[384,512]{1,0:T(8,128)(2,1)} %copy-done.4, bf16[16,4,32,128]{3,2,1,0:T(8,128)(2,1)} %all-to-all-done.1.cols, ...), custom_call_target="tpu_custom_call" | custom-call | flops 2000000000 | bytes 4000000 | tf_op jit(solution)/shard_map/front/pallas_call | solution.py:130
  68.8 5.6 %all-to-all-start.2 = ((bf16[16,8,32,128]{3,2,1,0:T(8,128)(2,1)}), bf16[16,8,32,128]{3,2,1,0:T(8,128)(2,1)}, u32[]{:S(2)}, u32[]{:S(2)}) async-start(bf16[16,8,32,128]{3,2,1,0:T(8,128)(2,1)} %front.1), calls=%async_computation.2 | async-start | bytes 2097152 | tf_op jit(solution)/shard_map/all_to_all | solution.py:146
  74.4 1.9 %slice.33 = bf16[64,4096]{1,0:T(8,128)(2,1)} slice(bf16[128,4096]{1,0:T(8,128)(2,1)} %collective-permute-done.7.down), slice={[64:128], [0:4096]} | slice | bytes 1048576 | tf_op jit(solution)/shard_map/slice | solution.py:127
  76.3 2.5 %collective-permute-start.9 = (bf16[64,4096]{1,0:T(8,128)(2,1)}, bf16[64,4096]{1,0:T(8,128)(2,1)}, u32[]{:S(2)}, u32[]{:S(2)}) collective-permute-start(bf16[64,4096]{1,0:T(8,128)(2,1)} %slice.33), channel_id=1, source_target_pairs={{0,12},{1,13},{2,14},{3,15},{4,0},{5,1},{6,2},{7,3},{8,4},{9,5},{1... | collective-permute-start | bytes 1572872 | tf_op jit(solution)/shard_map/ppermute | solution.py:127
  78.8 1.9 %slice.32 = bf16[64,4096]{1,0:T(8,128)(2,1)} slice(bf16[128,4096]{1,0:T(8,128)(2,1)} %collective-permute-done.6.up), slice={[0:64], [0:4096]} | slice | bytes 1048576 | tf_op jit(solution)/shard_map/slice | solution.py:126
  80.6 4.0 %collective-permute-start.8 = (bf16[64,4096]{1,0:T(8,128)(2,1)}, bf16[64,4096]{1,0:T(8,128)(2,1)}, u32[]{:S(2)}, u32[]{:S(2)}) collective-permute-start(bf16[64,4096]{1,0:T(8,128)(2,1)} %slice.32), channel_id=1, source_target_pairs={{0,4},{1,5},{2,6},{3,7},{4,8},{5,9},{6,10},{7,11},{8,12},{9,13},{1... | collective-permute-start | bytes 1572872 | tf_op jit(solution)/shard_map/ppermute | solution.py:126
  84.6 4.1 %all-to-all-done.2 = bf16[16,8,32,128]{3,2,1,0:T(8,128)(2,1)} async-done(((bf16[16,8,32,128]{3,2,1,0:T(8,128)(2,1)}), bf16[16,8,32,128]{3,2,1,0:T(8,128)(2,1)}, u32[]{:S(2)}, u32[]{:S(2)}) %all-to-all-start.2) | async-done | bytes 1048608 | tf_op jit(solution)/shard_map/all_to_all | solution.py:146
  88.7 1.3 %fusion.1 = bf16[32,8,4,128]{3,0,1,2:T(8,128)(2,1)S(1)} fusion(bf16[16,8,32,128]{3,2,1,0:T(8,128)(2,1)} %all-to-all-done.2), kind=kLoop, calls=%fused_computation.6 | loop fusion | flops 1048576 | bytes 1310720 | tf_op jit(solution)/shard_map/transpose | solution.py:149
  90.2 7.2 %collective-permute-start.5 = (bf16[256,512]{1,0:T(8,128)(2,1)S(1)}, bf16[256,512]{1,0:T(8,128)(2,1)S(1)}, u32[]{:S(2)}, u32[]{:S(2)}) collective-permute-start(bf16[256,512]{1,0:T(8,128)(2,1)S(1)} %bitcast.39), channel_id=1, source_target_pairs={{0,17},{1,16},{2,19},{3,18},{4,21},{5,20},{6,23},{7,22},{8,25},{9,... | collective-permute-start | bytes 786440 | tf_op jit(solution)/shard_map/ppermute | solution.py:106
  97.8 0.8 collective-permute-done.9.far_b
  98.5 3.9 %collective-permute-done.5.left = bf16[256,512]{1,0:T(8,128)(2,1)S(1)} collective-permute-done((bf16[256,512]{1,0:T(8,128)(2,1)S(1)}, bf16[256,512]{1,0:T(8,128)(2,1)S(1)}, u32[]{:S(2)}, u32[]{:S(2)}) %collective-permute-start.5) | collective-permute-done | bytes 262176 | tf_op jit(solution)/shard_map/ppermute | solution.py:106
  102.4 4.8 %back.2 = bf16[512,512]{1,0:T(8,128)(2,1)S(1)} custom-call(s32[4]{0:T(128)S(1)} %fusion.5.offsets, bf16[256,512]{1,0:T(8,128)(2,1)S(1)} %collective-permute-done.5.left, bf16[128,4096]{1,0:T(8,128)(2,1)S(1)} %bitcast.31, bf16[128,4096]{1,0:T(8,128)(2,1)} %collective-permute-done.6.up, bf16[128,4096]{1,0:T(8,128)(2,1)} %collective-permute-done.7.down, ...), custom_call_target="tpu_custom_call" | custom-call | flops 2500000000 | bytes 8000000 | tf_op jit(solution)/shard_map/back/pallas_call | solution.py:86
  107.3 6.8 %collective-permute-start.10 = (bf16[512,512]{1,0:T(8,128)(2,1)S(1)}, bf16[512,512]{1,0:T(8,128)(2,1)S(1)}, u32[]{:S(2)}, u32[]{:S(2)}) collective-permute-start(bf16[512,512]{1,0:T(8,128)(2,1)S(1)} %back.2), channel_id=1, source_target_pairs={{0,1},{1,0},{2,3},{3,2},{4,5},{5,4},{6,7},{7,6},{8,9},{9,8},{10,11... | collective-permute-start | bytes 1572872 | tf_op jit(solution)/shard_map/ppermute | solution.py:155
  114.0 4.8 %back.3 = bf16[512,512]{1,0:T(8,128)(2,1)S(1)} custom-call(s32[4]{0:T(128)S(1)} %fusion.5.offsets, bf16[256,512]{1,0:T(8,128)(2,1)S(1)} %collective-permute-done.4.left, bf16[128,4096]{1,0:T(8,128)(2,1)S(1)} %bitcast.32, bf16[128,4096]{1,0:T(8,128)(2,1)} %collective-permute-done.6.up, bf16[128,4096]{1,0:T(8,128)(2,1)} %collective-permute-done.7.down, ...), custom_call_target="tpu_custom_call" | custom-call | flops 2500000000 | bytes 8000000 | tf_op jit(solution)/shard_map/back/pallas_call | solution.py:86
  118.8 7.4 %collective-permute-done.10 = bf16[512,512]{1,0:T(8,128)(2,1)S(1)} collective-permute-done((bf16[512,512]{1,0:T(8,128)(2,1)S(1)}, bf16[512,512]{1,0:T(8,128)(2,1)S(1)}, u32[]{:S(2)}, u32[]{:S(2)}) %collective-permute-start.10) | collective-permute-done | bytes 524320 | tf_op jit(solution)/shard_map/ppermute | solution.py:155
  126.4 0.9 reshape.48
  (35 shorter events, 4.1 us)
Async XLA Ops:
  0.6 15.5 %copy-start = (bf16[1,32,4,512]{3,2,1,0:T(4,128)(2,1)S(1)}, bf16[1,32,4,512]{3,2,1,0:T(4,128)(2,1)}, u32[]{:S(2)}) copy-start(bf16[1,32,4,512]{3,2,1,0:T(4,128)(2,1)} %param.7) | copy-start | bytes 393220
  0.6 15.7 %copy-start.2 = (bf16[8,8,4,4]{1,3,2,0:T(4,128)(2,1)S(1)}, bf16[8,8,4,4]{1,3,2,0:T(4,128)(2,1)}, u32[]{:S(2)}) copy-start(bf16[8,8,4,4]{1,3,2,0:T(4,128)(2,1)} %param.10) | copy-start | bytes 6148
  0.7 9.9 %collective-permute-start.3 = (bf16[32,4,4,512]{3,2,1,0:T(4,128)(2,1)}, bf16[32,4,4,512]{3,2,1,0:T(4,128)(2,1)S(1)}, u32[]{:S(2)}, u32[]{:S(2)}) collective-permute-start(bf16[32,4,4,512]{3,2,1,0:T(4,128)(2,1)} %bitcast.42), channel_id=1, source_target_pairs={{0,16},{1,17},{2,18},{3,19},{4,20},{5,21},{6,22},{7,23},{8,24},{9,... | collective-permute-start | bytes 1572872 | tf_op jit(solution)/shard_map/ppermute | solution.py:106
  12.2 19.4 %all-to-all-start = ((bf16[4,32,4096]{2,1,0:T(8,128)(2,1)}), bf16[4,32,4096]{2,1,0:T(8,128)(2,1)S(1)}, u32[]{:S(2)}, u32[]{:S(2)}) async-start(bf16[4,32,4096]{2,1,0:T(8,128)(2,1)} %bitcast.3), calls=%async_computation | async-start | bytes 2097152 | tf_op jit(solution)/shard_map/all_to_all | solution.py:113
  16.2 4.1 %copy-start.6 = (s32[4]{0:T(128)S(1)}, s32[4]{0:T(128)}, u32[]{:S(2)}) copy-start(s32[4]{0:T(128)} %constant.52.clone) | copy-start | bytes 52
  32.4 31.5 %all-to-all-start.1 = ((bf16[16,4,32,128]{3,2,1,0:T(8,128)(2,1)}), bf16[16,4,32,128]{3,2,1,0:T(8,128)(2,1)}, u32[]{:S(2)}, u32[]{:S(2)}) async-start(bf16[16,4,32,128]{3,2,1,0:T(8,128)(2,1)} %bitcast.33), calls=%async_computation.1 | async-start | bytes 1048576 | tf_op jit(solution)/shard_map/all_to_all | solution.py:129
  38.2 9.9 %copy-start.1 = (bf16[384,512]{1,0:T(8,128)(2,1)}, bf16[384,512]{1,0:T(8,128)(2,1)S(1)}, u32[]{:S(2)}) copy-start(bf16[384,512]{1,0:T(8,128)(2,1)S(1)} %pad_maximum_fusion.own) | copy-start | bytes 1179652
  38.2 16.4 %collective-permute-start.2 = (bf16[384,512]{1,0:T(8,128)(2,1)S(1)}, bf16[384,512]{1,0:T(8,128)(2,1)S(1)}, u32[]{:S(2)}, u32[]{:S(2)}) collective-permute-start(bf16[384,512]{1,0:T(8,128)(2,1)S(1)} %pad_maximum_fusion.own), channel_id=1, source_target_pairs={{0,2},{1,3},{2,0},{3,1},{4,6},{5,7},{6,4},{7,5},{8,10},{9,11},{10,... | collective-permute-start | bytes 1179656 | tf_op jit(solution)/shard_map/ppermute | solution.py:109
  42.8 18.5 %collective-permute-start.1 = (bf16[384,512]{1,0:T(8,128)(2,1)S(1)}, bf16[384,512]{1,0:T(8,128)(2,1)S(1)}, u32[]{:S(2)}, u32[]{:S(2)}) collective-permute-start(bf16[384,512]{1,0:T(8,128)(2,1)S(1)} %pad_maximum_fusion.own), channel_id=1, source_target_pairs={{0,3},{1,0},{2,1},{3,2},{4,7},{5,4},{6,5},{7,6},{8,11},{9,8},{10,9... | collective-permute-start | bytes 1179656 | tf_op jit(solution)/shard_map/ppermute | solution.py:109
  45.6 18.3 %collective-permute-start = (bf16[384,512]{1,0:T(8,128)(2,1)S(1)}, bf16[384,512]{1,0:T(8,128)(2,1)}, u32[]{:S(2)}, u32[]{:S(2)}) collective-permute-start(bf16[384,512]{1,0:T(8,128)(2,1)S(1)} %pad_maximum_fusion.own), channel_id=1, source_target_pairs={{0,1},{1,2},{2,3},{3,0},{4,5},{5,6},{6,7},{7,4},{8,9},{9,10},{10,1... | collective-permute-start | bytes 1179656 | tf_op jit(solution)/shard_map/ppermute | solution.py:109
  48.1 26.3 %collective-permute-start.7 = (bf16[128,4096]{1,0:T(8,128)(2,1)S(1)}, bf16[128,4096]{1,0:T(8,128)(2,1)}, u32[]{:S(2)}, u32[]{:S(2)}) collective-permute-start(bf16[128,4096]{1,0:T(8,128)(2,1)S(1)} %bitcast.29), channel_id=1, source_target_pairs={{0,12},{1,13},{2,14},{3,15},{4,0},{5,1},{6,2},{7,3},{8,4},{9,5},{1... | collective-permute-start | bytes 3145736 | tf_op jit(solution)/shard_map/ppermute | solution.py:125
  50.6 28.2 %collective-permute-start.6 = (bf16[128,4096]{1,0:T(8,128)(2,1)S(1)}, bf16[128,4096]{1,0:T(8,128)(2,1)}, u32[]{:S(2)}, u32[]{:S(2)}) collective-permute-start(bf16[128,4096]{1,0:T(8,128)(2,1)S(1)} %bitcast.30), channel_id=1, source_target_pairs={{0,4},{1,5},{2,6},{3,7},{4,8},{5,9},{6,10},{7,11},{8,12},{9,13},{1... | collective-permute-start | bytes 3145736 | tf_op jit(solution)/shard_map/ppermute | solution.py:124
  54.6 6.7 %copy-start.4 = (bf16[384,512]{1,0:T(8,128)(2,1)}, bf16[384,512]{1,0:T(8,128)(2,1)S(1)}, u32[]{:S(2)}) copy-start(bf16[384,512]{1,0:T(8,128)(2,1)S(1)} %collective-permute-done.2.far) | copy-start | bytes 1179652
  61.3 0.8 copy-start.5
  68.8 19.9 %all-to-all-start.2 = ((bf16[16,8,32,128]{3,2,1,0:T(8,128)(2,1)}), bf16[16,8,32,128]{3,2,1,0:T(8,128)(2,1)}, u32[]{:S(2)}, u32[]{:S(2)}) async-start(bf16[16,8,32,128]{3,2,1,0:T(8,128)(2,1)} %front.1), calls=%async_computation.2 | async-start | bytes 2097152 | tf_op jit(solution)/shard_map/all_to_all | solution.py:146
  76.3 22.3 %collective-permute-start.9 = (bf16[64,4096]{1,0:T(8,128)(2,1)}, bf16[64,4096]{1,0:T(8,128)(2,1)}, u32[]{:S(2)}, u32[]{:S(2)}) collective-permute-start(bf16[64,4096]{1,0:T(8,128)(2,1)} %slice.33), channel_id=1, source_target_pairs={{0,12},{1,13},{2,14},{3,15},{4,0},{5,1},{6,2},{7,3},{8,4},{9,5},{1... | collective-permute-start | bytes 1572872 | tf_op jit(solution)/shard_map/ppermute | solution.py:127
  80.6 17.9 %collective-permute-start.8 = (bf16[64,4096]{1,0:T(8,128)(2,1)}, bf16[64,4096]{1,0:T(8,128)(2,1)}, u32[]{:S(2)}, u32[]{:S(2)}) collective-permute-start(bf16[64,4096]{1,0:T(8,128)(2,1)} %slice.32), channel_id=1, source_target_pairs={{0,4},{1,5},{2,6},{3,7},{4,8},{5,9},{6,10},{7,11},{8,12},{9,13},{1... | collective-permute-start | bytes 1572872 | tf_op jit(solution)/shard_map/ppermute | solution.py:126
  90.2 17.1 %copy-start.3 = (bf16[32,8,4,128]{3,1,2,0:T(8,128)(2,1)}, bf16[32,8,4,128]{3,1,2,0:T(8,128)(2,1)S(1)}, u32[]{:S(2)}) copy-start(bf16[32,8,4,128]{3,1,2,0:T(8,128)(2,1)S(1)} %copy.36) | copy-start | bytes 786436
  90.2 12.2 %collective-permute-start.5 = (bf16[256,512]{1,0:T(8,128)(2,1)S(1)}, bf16[256,512]{1,0:T(8,128)(2,1)S(1)}, u32[]{:S(2)}, u32[]{:S(2)}) collective-permute-start(bf16[256,512]{1,0:T(8,128)(2,1)S(1)} %bitcast.39), channel_id=1, source_target_pairs={{0,17},{1,16},{2,19},{3,18},{4,21},{5,20},{6,23},{7,22},{8,25},{9,... | collective-permute-start | bytes 786440 | tf_op jit(solution)/shard_map/ppermute | solution.py:106
  97.4 9.8 %collective-permute-start.4 = (bf16[256,512]{1,0:T(8,128)(2,1)S(1)}, bf16[256,512]{1,0:T(8,128)(2,1)S(1)}, u32[]{:S(2)}, u32[]{:S(2)}) collective-permute-start(bf16[256,512]{1,0:T(8,128)(2,1)S(1)} %bitcast.40), channel_id=1, source_target_pairs={{0,16},{1,17},{2,18},{3,19},{4,20},{5,21},{6,22},{7,23},{8,24},{9,... | collective-permute-start | bytes 786440 | tf_op jit(solution)/shard_map/ppermute | solution.py:106
  107.3 19.0 %collective-permute-start.10 = (bf16[512,512]{1,0:T(8,128)(2,1)S(1)}, bf16[512,512]{1,0:T(8,128)(2,1)S(1)}, u32[]{:S(2)}, u32[]{:S(2)}) collective-permute-start(bf16[512,512]{1,0:T(8,128)(2,1)S(1)} %back.2), channel_id=1, source_target_pairs={{0,1},{1,0},{2,3},{3,2},{4,5},{5,4},{6,7},{7,6},{8,9},{9,8},{10,11... | collective-permute-start | bytes 1572872 | tf_op jit(solution)/shard_map/ppermute | solution.py:155

commit v6 on v5

--- a/solution.py
+++ b/solution.py
@@ -11,15 +11,28 @@
 
 
 LINE = 4
+SIZE = LINE * LINE
 
 
-def line_route(distance):
-    return [(i, i - i % LINE + (i + distance) % LINE) for i in range(LINE * LINE)]
+def turned(b):
+    return b % LINE * LINE + b // LINE
 
 
-def column_route(distance):
-    size = LINE * LINE
-    return [(i, (i + LINE * distance) % size) for i in range(size)]
+def routed(sections, step, ahead=0):
+    pairs = []
+    for s in range(sections):
+        t = (s + ahead) % sections
+        for b in range(SIZE):
+            pairs.append((SIZE * s + b, SIZE * t + (turned(step(turned(b))) if t % 2 else step(b))))
+    return pairs
+
+
+def along_line(distance):
+    return lambda b: b - b % LINE + (b + distance) % LINE
+
+
+def along_column(distance):
+    return lambda b: (b + LINE * distance) % SIZE
 
 
 def spread_out(local):
@@ -99,32 +112,40 @@
     chi = site.shape[-1]
     sections = lax.axis_size("sec")
     here = lax.axis_index("bond")
-    lines = [[LINE * y + x for x in range(LINE)] for y in range(LINE)]
+    odd = lax.axis_index("sec") % 2 == 1
+    row = jnp.where(odd, here % LINE, here // LINE)
+    column = jnp.where(odd, here // LINE, here % LINE)
 
-    def next_section(block, flip):
-        route = [(16 * s + b, (s + 1) % sections * 16 + (b ^ flip)) for s in range(sections) for b in range(16)]
-        return lax.ppermute(block, ("sec", "bond"), route)
+    def moved(block, step, ahead=0):
+        return lax.ppermute(block, ("sec", "bond"), routed(sections, step, ahead))
 
+    lines = []
+    for s in range(sections):
+        for y in range(LINE):
+            line = [LINE * y + x for x in range(LINE)]
+            lines.append([SIZE * s + (turned(b) if s % 2 else b) for b in line])
     own = jnp.concatenate([left_env[0].reshape(256, chi), site[0].reshape(128, chi)], axis=0)
-    blocks = [own] + [lax.ppermute(own, "bond", line_route(d)) for d in (1, -1, 2)]
-    pair = next_section(psi[0], 0)
+    blocks = [own] + [moved(own, along_line(d)) for d in (1, -1, 2)]
+    pair = moved(psi[0], lambda b: b, 1)
     halves = pair.reshape(32, 16, 2, 256).transpose(2, 0, 1, 3).reshape(2, 32, 4096)
     send = jnp.broadcast_to(halves[None], (2, 2, 32, 4096)).reshape(4, 32, 4096)
-    pair = lax.all_to_all(send, "bond", 0, 0, axis_index_groups=lines, tiled=True).reshape(128, 4096)
+    pair = lax.all_to_all(send, ("sec", "bond"), 0, 0, axis_index_groups=lines, tiled=True).reshape(128, 4096)
     local = mpo.transpose(1, 3, 2, 0).reshape(32, 32)
     two_site = jnp.einsum("mnsu,nkvw->kuwsvm", mpo, mpo, preferred_element_type=F32)
     two_site = two_site.astype(BF).reshape(128, 128)
-    quarters = site[0].reshape(32, 4, 4, 128).transpose(2, 1, 0, 3)
-    cols = jnp.broadcast_to(quarters[None], (4, 4, 4, 32, 128)).reshape(16, 4, 32, 128)
-    offsets = (here // LINE + jnp.array([0, 3, 1, 2], jnp.int32)) % LINE * 128
-    right = lax.dynamic_slice_in_dim(right_env[0], here % 2 * 256, 256, 1).reshape(2048, chi)
+    turn = site[0].reshape(32, 4, 4, 4, 32).transpose(0, 1, 3, 2, 4).reshape(32, 4, chi)
+    tensor = jnp.where(odd, site[0], turn)
+    quarters = tensor.reshape(32, 4, 4, 128).transpose(2, 1, 0, 3)
+    cols = jnp.where(odd, quarters[:, None], quarters[None]).reshape(16, 4, 32, 128)
+    offsets = (row + jnp.array([0, 3, 1, 2], jnp.int32)) % LINE * 128
+    right = lax.dynamic_slice_in_dim(right_env[0], column % 2 * 256, 256, 1).reshape(2048, chi)
     pair, local, two_site, cols, offsets, right = lax.optimization_barrier(
         (pair, local, two_site, cols, offsets, right)
     )
-    up = lax.ppermute(pair, "bond", column_route(1))
-    down = lax.ppermute(pair, "bond", column_route(-1))
-    far_a = lax.ppermute(up[:64], "bond", column_route(1))
-    far_b = lax.ppermute(down[64:], "bond", column_route(-1))
+    up = moved(pair, along_column(1))
+    down = moved(pair, along_column(-1))
+    far_a = moved(up[:64], along_column(1))
+    far_b = moved(down[64:], along_column(-1))
     pieces = (pair, up, down, far_a, far_b)
     cols = lax.all_to_all(cols, "bond", 0, 0, tiled=True)
     fresh = pl.pallas_call(
@@ -144,15 +165,18 @@
         name="front",
     )(*blocks, cols, local)
     fresh = lax.all_to_all(fresh, "bond", 0, 0, tiled=True).reshape(4, 4, 8, 32, 128)
+    fresh = jnp.where(odd, fresh.transpose(1, 0, 2, 3, 4), fresh)
     fresh = [fresh[i].astype(F32) for i in range(4)]
     fresh = ((fresh[0] + fresh[1]) + (fresh[2] + fresh[3])).astype(BF)
-    new_left = fresh.transpose(2, 1, 0, 3).reshape(32, 8, chi)
-    source = new_left.reshape(256, chi)
-    other = next_section(source, 1)
-    source = next_section(source, 0)
+    source = fresh.transpose(2, 1, 0, 3).reshape(256, chi)
+    new_left = source.reshape(32, 8, chi)
+    turn = new_left.reshape(32, 8, 4, 4, 32).transpose(0, 1, 3, 2, 4).reshape(32, 8, chi)
+    new_left = jnp.where(odd, new_left, turn)
+    other = moved(source, lambda b: b ^ 1, 1)
+    source = moved(source, lambda b: b, 1)
     give = applied(offsets, other, pieces, two_site, right)
     source, give = lax.optimization_barrier((source, give))
-    take = lax.ppermute(give, "bond", [(i, i ^ 1) for i in range(16)])
+    take = moved(give, lambda b: b ^ 1)
     keep = applied(offsets, source, pieces, two_site, right)
     total = (keep.astype(F32) + take.astype(F32)).astype(BF)
     return (new_left[None], total.reshape(1, 32, 4, 4, chi))

time: 128 us -> 135 us (1.055)
  the two profiles are of different devices: /device:TPU:121 before, /device:TPU:2 now
where the time goes in v6:
time: 135 us; the launch traced here: 133 us
  starting transfers between devices  50.8 us (38%)
  waiting for transfers between devices  32.4 us (24%)
  local copies, waits for them, and re-layouts  24.3 us (18%)
  Pallas kernels  15.4 us (11%)
  other arithmetic  8.34 us (6%)
    ppermute x11, starting transfers between devices, moved(): return lax.ppermute(block, ('sec', 'bond'), routed(sections, step, ahead))  31.1 us
    ppermute x11, waiting for transfers between devices, moved(): return lax.ppermute(block, ('sec', 'bond'), routed(sections, step, ahead))  22.5 us
    pallas_call x2, Pallas kernels, applied(): pl.pallas_call(back, out_shape=jax.ShapeDtypeStruct((512, 512), BF), in_s...  10.4 us
    all_to_all x1, starting transfers between devices, shards(): lax.all_to_all(fresh, 'bond', 0, 0, tiled=True).reshape(4, 4, 8, 32, 128)  8.3 us
    all_to_all x1, waiting for transfers between devices, shards(): lax.all_to_all(send, ('sec', 'bond'), 0, 0, axis_index_groups=lines, tile...  6.62 us
    all_to_all x1, starting transfers between devices, shards(): cols = lax.all_to_all(cols, 'bond', 0, 0, tiled=True)  6.55 us
    another operation x2, local copies, waits for them, and re-layouts, shards(): new_left.reshape(32, 8, 4, 4, 32).transpose(0, 1, 3, 2, 4)  5.82 us
    pallas_call x1, Pallas kernels, shards(): pl.pallas_call(front, out_shape=jax.ShapeDtypeStruct((16, 8, 32, 128), BF...  4.94 us
  transfers between devices with their start and end apart: 14, of which 7 were waited for; matrix products, arithmetic and copies ran while one was open for 22% of the time, Pallas kernels for 12%

profile of v6, /device:TPU:2, one launch (start us, length us, event | category | flops | bytes accessed | tf_op | source)
XLA Modules:
  0.0 133.4 jit_solution(13704092319880907996)
XLA Ops:
  2.6 1.2 reshape_squeeze.11
  5.4 1.2 fusion
  8.0 8.6 %collective-permute-done.3 = bf16[32,4,4,512]{3,2,1,0:T(4,128)(2,1)S(1)} collective-permute-done((bf16[32,4,4,512]{3,2,1,0:T(4,128)(2,1)}, bf16[32,4,4,512]{3,2,1,0:T(4,128)(2,1)S(1)}, u32[]{:S(2)}, u32[]{:S(2)}) %collective-permute-start.3) | collective-permute-done | bytes 524320 | tf_op jit(solution)/shard_map/ppermute | solution.py:120
  18.3 4.8 %all-to-all-start = ((bf16[4,32,4096]{2,1,0:T(8,128)(2,1)}), bf16[4,32,4096]{2,1,0:T(8,128)(2,1)S(1)}, u32[]{:S(2)}, u32[]{:S(2)}) async-start(bf16[4,32,4096]{2,1,0:T(8,128)(2,1)} %bitcast.3), calls=%async_computation | async-start | bytes 2097152 | tf_op jit(solution)/shard_map/all_to_all | solution.py:132
  23.2 1.8 %constant_dynamic-slice_fusion = bf16[1,8,256,512]{3,2,1,0:T(8,128)(2,1)S(1)} fusion(bf16[1,8,512,512]{3,2,1,0:T(8,128)(2,1)} %param.9, s32[]{:T(128)S(6)} %select_n.95), kind=kLoop, calls=%fused_computation.20 | loop fusion | bytes 4194308 | tf_op jit(solution)/shard_map/dynamic_slice | solution.py:141
  25.9 6.6 %all-to-all-done = bf16[4,32,4096]{2,1,0:T(8,128)(2,1)S(1)} async-done(((bf16[4,32,4096]{2,1,0:T(8,128)(2,1)}), bf16[4,32,4096]{2,1,0:T(8,128)(2,1)S(1)}, u32[]{:S(2)}, u32[]{:S(2)}) %all-to-all-start) | async-done | bytes 1048608 | tf_op jit(solution)/shard_map/all_to_all | solution.py:132
  32.6 6.6 %all-to-all-start.1 = ((bf16[16,4,32,128]{3,2,1,0:T(8,128)(2,1)}), bf16[16,4,32,128]{3,2,1,0:T(8,128)(2,1)}, u32[]{:S(2)}, u32[]{:S(2)}) async-start(bf16[16,4,32,128]{3,2,1,0:T(8,128)(2,1)} %bitcast.54), calls=%async_computation.1 | async-start | bytes 1048576 | tf_op jit(solution)/shard_map/all_to_all | solution.py:150
  40.1 4.0 %collective-permute-start.2 = (bf16[384,512]{1,0:T(8,128)(2,1)S(1)}, bf16[384,512]{1,0:T(8,128)(2,1)S(1)}, u32[]{:S(2)}, u32[]{:S(2)}) collective-permute-start(bf16[384,512]{1,0:T(8,128)(2,1)S(1)} %pad_maximum_fusion.own), channel_id=1, source_target_pairs={{0,2},{1,3},{2,0},{3,1},{4,6},{5,7},{6,4},{7,5},{8,10},{9,11},{10,... | collective-permute-start | bytes 1179656 | tf_op jit(solution)/shard_map/ppermute | solution.py:120
  44.1 3.4 %collective-permute-start.1 = (bf16[384,512]{1,0:T(8,128)(2,1)S(1)}, bf16[384,512]{1,0:T(8,128)(2,1)S(1)}, u32[]{:S(2)}, u32[]{:S(2)}) collective-permute-start(bf16[384,512]{1,0:T(8,128)(2,1)S(1)} %pad_maximum_fusion.own), channel_id=1, source_target_pairs={{0,3},{1,0},{2,1},{3,2},{4,7},{5,4},{6,5},{7,6},{8,11},{9,8},{10,9... | collective-permute-start | bytes 1179656 | tf_op jit(solution)/shard_map/ppermute | solution.py:120
  47.5 2.5 %collective-permute-start = (bf16[384,512]{1,0:T(8,128)(2,1)S(1)}, bf16[384,512]{1,0:T(8,128)(2,1)}, u32[]{:S(2)}, u32[]{:S(2)}) collective-permute-start(bf16[384,512]{1,0:T(8,128)(2,1)S(1)} %pad_maximum_fusion.own), channel_id=1, source_target_pairs={{0,1},{1,2},{2,3},{3,0},{4,5},{5,6},{6,7},{7,4},{8,9},{9,10},{10,1... | collective-permute-start | bytes 1179656 | tf_op jit(solution)/shard_map/ppermute | solution.py:120
  50.0 4.6 %collective-permute-start.7 = (bf16[128,4096]{1,0:T(8,128)(2,1)S(1)}, bf16[128,4096]{1,0:T(8,128)(2,1)}, u32[]{:S(2)}, u32[]{:S(2)}) collective-permute-start(bf16[128,4096]{1,0:T(8,128)(2,1)S(1)} %bitcast.48), channel_id=1, source_target_pairs={{0,12},{1,13},{2,14},{3,15},{4,0},{5,1},{6,2},{7,3},{8,4},{9,5},{1... | collective-permute-start | bytes 3145736 | tf_op jit(solution)/shard_map/ppermute | solution.py:120
  54.5 1.9 %collective-permute-start.6 = (bf16[128,4096]{1,0:T(8,128)(2,1)S(1)}, bf16[128,4096]{1,0:T(8,128)(2,1)}, u32[]{:S(2)}, u32[]{:S(2)}) collective-permute-start(bf16[128,4096]{1,0:T(8,128)(2,1)S(1)} %bitcast.49), channel_id=1, source_target_pairs={{0,4},{1,5},{2,6},{3,7},{4,8},{5,9},{6,10},{7,11},{8,12},{9,13},{1... | collective-permute-start | bytes 3145736 | tf_op jit(solution)/shard_map/ppermute | solution.py:120
  56.5 5.5 %collective-permute-done.1.back_ = bf16[384,512]{1,0:T(8,128)(2,1)S(1)} collective-permute-done((bf16[384,512]{1,0:T(8,128)(2,1)S(1)}, bf16[384,512]{1,0:T(8,128)(2,1)S(1)}, u32[]{:S(2)}, u32[]{:S(2)}) %collective-permute-start.1) | collective-permute-done | bytes 393248 | tf_op jit(solution)/shard_map/ppermute | solution.py:120
  62.8 4.9 %front.1 = bf16[16,8,32,128]{3,2,1,0:T(8,128)(2,1)} custom-call(bf16[384,512]{1,0:T(8,128)(2,1)} %copy-done.1, bf16[384,512]{1,0:T(8,128)(2,1)} %collective-permute-done.near, bf16[384,512]{1,0:T(8,128)(2,1)} %copy-done.3, bf16[384,512]{1,0:T(8,128)(2,1)} %copy-done.2, bf16[16,4,32,128]{3,2,1,0:T(8,128)(2,1)} %all-to-all-done.1.cols, ...), custom_call_target="tpu_custom_call" | custom-call | flops 2000000000 | bytes 4000000 | tf_op jit(solution)/shard_map/front/pallas_call | solution.py:151
  67.7 8.3 %all-to-all-start.2 = ((bf16[16,8,32,128]{3,2,1,0:T(8,128)(2,1)}), bf16[16,8,32,128]{3,2,1,0:T(8,128)(2,1)}, u32[]{:S(2)}, u32[]{:S(2)}) async-start(bf16[16,8,32,128]{3,2,1,0:T(8,128)(2,1)} %front.1), calls=%async_computation.2 | async-start | bytes 2097152 | tf_op jit(solution)/shard_map/all_to_all | solution.py:167
  76.0 1.9 %slice.29 = bf16[64,4096]{1,0:T(8,128)(2,1)} slice(bf16[128,4096]{1,0:T(8,128)(2,1)} %collective-permute-done.7.down), slice={[64:128], [0:4096]} | slice | bytes 1048576 | tf_op jit(solution)/shard_map/slice | solution.py:148
  77.9 4.6 %collective-permute-start.9 = (bf16[64,4096]{1,0:T(8,128)(2,1)}, bf16[64,4096]{1,0:T(8,128)(2,1)}, u32[]{:S(2)}, u32[]{:S(2)}) collective-permute-start(bf16[64,4096]{1,0:T(8,128)(2,1)} %slice.29), channel_id=1, source_target_pairs={{0,12},{1,13},{2,14},{3,15},{4,0},{5,1},{6,2},{7,3},{8,4},{9,5},{1... | collective-permute-start | bytes 1572872 | tf_op jit(solution)/shard_map/ppermute | solution.py:120
  82.5 1.9 %slice.28 = bf16[64,4096]{1,0:T(8,128)(2,1)} slice(bf16[128,4096]{1,0:T(8,128)(2,1)} %collective-permute-done.6.up), slice={[0:64], [0:4096]} | slice | bytes 1048576 | tf_op jit(solution)/shard_map/slice | solution.py:147
  84.4 1.9 %collective-permute-start.8 = (bf16[64,4096]{1,0:T(8,128)(2,1)}, bf16[64,4096]{1,0:T(8,128)(2,1)}, u32[]{:S(2)}, u32[]{:S(2)}) collective-permute-start(bf16[64,4096]{1,0:T(8,128)(2,1)} %slice.28), channel_id=1, source_target_pairs={{0,4},{1,5},{2,6},{3,7},{4,8},{5,9},{6,10},{7,11},{8,12},{9,13},{1... | collective-permute-start | bytes 1572872 | tf_op jit(solution)/shard_map/ppermute | solution.py:120
  86.3 3.3 %all-to-all-done.2 = bf16[16,8,32,128]{3,2,1,0:T(8,128)(2,1)} async-done(((bf16[16,8,32,128]{3,2,1,0:T(8,128)(2,1)}), bf16[16,8,32,128]{3,2,1,0:T(8,128)(2,1)}, u32[]{:S(2)}, u32[]{:S(2)}) %all-to-all-start.2) | async-done | bytes 1048608 | tf_op jit(solution)/shard_map/all_to_all | solution.py:167
  89.6 2.1 %bitcast_select_fusion = bf16[4,4,8,32,128]{4,2,1,3,0:T(8,128)(2,1)S(1)} fusion(bf16[4,4,8,32,128]{4,3,2,1,0:T(8,128)(2,1)} %bitcast.13, pred[]{:T(512)S(6)} %eq.10), kind=kLoop, calls=%fused_computation.2 | loop fusion | flops 524288 | bytes 2097153 | tf_op jit(solution)/shard_map/jit(_where)/select_n | solution.py:168
  91.8 1.9 %collective-permute-start.5 = (bf16[256,512]{1,0:T(8,128)(2,1)S(1)}, bf16[256,512]{1,0:T(8,128)(2,1)S(1)}, u32[]{:S(2)}, u32[]{:S(2)}) collective-permute-start(bf16[256,512]{1,0:T(8,128)(2,1)S(1)} %fusion.6), channel_id=1, source_target_pairs={{0,20},{1,21},{2,22},{3,23},{4,16},{5,17},{6,18},{7,19},{8,28},{9,... | collective-permute-start | bytes 786440 | tf_op jit(solution)/shard_map/ppermute | solution.py:120
  93.8 3.2 %collective-permute-done.8.far_a = bf16[64,4096]{1,0:T(8,128)(2,1)} collective-permute-done((bf16[64,4096]{1,0:T(8,128)(2,1)}, bf16[64,4096]{1,0:T(8,128)(2,1)}, u32[]{:S(2)}, u32[]{:S(2)}) %collective-permute-start.8) | collective-permute-done | bytes 524320 | tf_op jit(solution)/shard_map/ppermute | solution.py:120
  97.0 4.7 %collective-permute-done.5.left = bf16[256,512]{1,0:T(8,128)(2,1)S(1)} collective-permute-done((bf16[256,512]{1,0:T(8,128)(2,1)S(1)}, bf16[256,512]{1,0:T(8,128)(2,1)S(1)}, u32[]{:S(2)}, u32[]{:S(2)}) %collective-permute-start.5) | collective-permute-done | bytes 262176 | tf_op jit(solution)/shard_map/ppermute | solution.py:120
  101.7 5.6 %back.2 = bf16[512,512]{1,0:T(8,128)(2,1)} custom-call(s32[4]{0:T(128)S(1)} %fusion.5.offsets, bf16[256,512]{1,0:T(8,128)(2,1)S(1)} %collective-permute-done.5.left, bf16[128,4096]{1,0:T(8,128)(2,1)S(1)} %bitcast.50, bf16[128,4096]{1,0:T(8,128)(2,1)} %collective-permute-done.6.up, bf16[128,4096]{1,0:T(8,128)(2,1)} %collective-permute-done.7.down, ...), custom_call_target="tpu_custom_call" | custom-call | flops 2500000000 | bytes 8000000 | tf_op jit(solution)/shard_map/back/pallas_call | solution.py:99
  107.8 6.4 %collective-permute-start.10 = (bf16[512,512]{1,0:T(8,128)(2,1)}, bf16[512,512]{1,0:T(8,128)(2,1)}, u32[]{:S(2)}, u32[]{:S(2)}) collective-permute-start(bf16[512,512]{1,0:T(8,128)(2,1)} %back.2), channel_id=1, source_target_pairs={{0,1},{1,0},{2,3},{3,2},{4,5},{5,4},{6,7},{7,6},{8,9},{9,8},{10,11... | collective-permute-start | bytes 1572872 | tf_op jit(solution)/shard_map/ppermute | solution.py:120
  115.0 2.8 %reshape_reshape_reshape.3 = bf16[32,8,4,4,32]{4,3,1,2,0:T(4,128)(2,1)} reshape(bf16[32,8,4,128]{3,1,2,0:T(8,128)(2,1)} %fusion.7) | data formatting | bytes 524288 | tf_op jit(solution)/shard_map/reshape;reshape;reshape | solution.py:173
  117.7 3.1 %copy.61 = bf16[32,8,4,4,32]{4,2,3,1,0:T(4,128)(2,1)} copy(bf16[32,8,4,4,32]{4,3,1,2,0:T(4,128)(2,1)} %reshape_reshape_reshape.3) | data formatting | bytes 524288 | tf_op jit(solution)/shard_map/reshape;reshape;reshape | solution.py:173
  120.8 3.5 %reshape.83 = bf16[1,32,8,512]{3,2,1,0:T(8,128)(2,1)} reshape(bf16[32,8,4,4,32]{4,3,2,1,0:T(4,128)(2,1)} %bitcast.52) | data formatting | bytes 524288 | tf_op jit(solution)/shard_map/reshape | solution.py:173
  124.3 2.1 %bitcast_select_fusion.1 = bf16[1,32,8,512]{3,2,1,0:T(8,128)(2,1)} fusion(bf16[1,32,8,512]{3,2,1,0:T(8,128)(2,1)} %reshape.83, pred[]{:T(512)S(6)} %eq.10, bf16[4,4,8,32,128]{4,2,1,3,0:T(8,128)(2,1)} %copy-done), kind=kLoop, calls=%fused_computation.10 | loop fusion | flops 1179648 | bytes 1572865 | tf_op jit(solution)/shard_map/jit(_where)/select_n | solution.py:174
  126.5 4.8 %back.3 = bf16[512,512]{1,0:T(8,128)(2,1)S(1)} custom-call(s32[4]{0:T(128)S(1)} %fusion.5.offsets, bf16[256,512]{1,0:T(8,128)(2,1)S(1)} %collective-permute-done.4.left, bf16[128,4096]{1,0:T(8,128)(2,1)S(1)} %bitcast.51, bf16[128,4096]{1,0:T(8,128)(2,1)} %collective-permute-done.6.up, bf16[128,4096]{1,0:T(8,128)(2,1)} %collective-permute-done.7.down, ...), custom_call_target="tpu_custom_call" | custom-call | flops 2500000000 | bytes 8000000 | tf_op jit(solution)/shard_map/back/pallas_call | solution.py:99
  131.3 1.2 add_convert_fusion
  (40 shorter events, 11.7 us)
Async XLA Ops:
  0.6 16.0 %collective-permute-start.3 = (bf16[32,4,4,512]{3,2,1,0:T(4,128)(2,1)}, bf16[32,4,4,512]{3,2,1,0:T(4,128)(2,1)S(1)}, u32[]{:S(2)}, u32[]{:S(2)}) collective-permute-start(bf16[32,4,4,512]{3,2,1,0:T(4,128)(2,1)} %bitcast.59), channel_id=1, source_target_pairs={{0,16},{1,17},{2,18},{3,19},{4,20},{5,21},{6,22},{7,23},{8,24},{9,... | collective-permute-start | bytes 1572872 | tf_op jit(solution)/shard_map/ppermute | solution.py:120
  17.2 7.9 %copy-start.4 = (s32[4]{0:T(128)S(1)}, s32[4]{0:T(128)}, u32[]{:S(2)}) copy-start(s32[4]{0:T(128)} %constant.70.clone) | copy-start | bytes 52
  18.3 14.3 %all-to-all-start = ((bf16[4,32,4096]{2,1,0:T(8,128)(2,1)}), bf16[4,32,4096]{2,1,0:T(8,128)(2,1)S(1)}, u32[]{:S(2)}, u32[]{:S(2)}) async-start(bf16[4,32,4096]{2,1,0:T(8,128)(2,1)} %bitcast.3), calls=%async_computation | async-start | bytes 2097152 | tf_op jit(solution)/shard_map/all_to_all | solution.py:132
  32.6 30.2 %all-to-all-start.1 = ((bf16[16,4,32,128]{3,2,1,0:T(8,128)(2,1)}), bf16[16,4,32,128]{3,2,1,0:T(8,128)(2,1)}, u32[]{:S(2)}, u32[]{:S(2)}) async-start(bf16[16,4,32,128]{3,2,1,0:T(8,128)(2,1)} %bitcast.54), calls=%async_computation.1 | async-start | bytes 1048576 | tf_op jit(solution)/shard_map/all_to_all | solution.py:150
  40.1 9.9 %copy-start.1 = (bf16[384,512]{1,0:T(8,128)(2,1)}, bf16[384,512]{1,0:T(8,128)(2,1)S(1)}, u32[]{:S(2)}) copy-start(bf16[384,512]{1,0:T(8,128)(2,1)S(1)} %pad_maximum_fusion.own) | copy-start | bytes 1179652
  40.1 16.4 %collective-permute-start.2 = (bf16[384,512]{1,0:T(8,128)(2,1)S(1)}, bf16[384,512]{1,0:T(8,128)(2,1)S(1)}, u32[]{:S(2)}, u32[]{:S(2)}) collective-permute-start(bf16[384,512]{1,0:T(8,128)(2,1)S(1)} %pad_maximum_fusion.own), channel_id=1, source_target_pairs={{0,2},{1,3},{2,0},{3,1},{4,6},{5,7},{6,4},{7,5},{8,10},{9,11},{10,... | collective-permute-start | bytes 1179656 | tf_op jit(solution)/shard_map/ppermute | solution.py:120
  44.1 17.9 %collective-permute-start.1 = (bf16[384,512]{1,0:T(8,128)(2,1)S(1)}, bf16[384,512]{1,0:T(8,128)(2,1)S(1)}, u32[]{:S(2)}, u32[]{:S(2)}) collective-permute-start(bf16[384,512]{1,0:T(8,128)(2,1)S(1)} %pad_maximum_fusion.own), channel_id=1, source_target_pairs={{0,3},{1,0},{2,1},{3,2},{4,7},{5,4},{6,5},{7,6},{8,11},{9,8},{10,9... | collective-permute-start | bytes 1179656 | tf_op jit(solution)/shard_map/ppermute | solution.py:120
  47.5 15.3 %collective-permute-start = (bf16[384,512]{1,0:T(8,128)(2,1)S(1)}, bf16[384,512]{1,0:T(8,128)(2,1)}, u32[]{:S(2)}, u32[]{:S(2)}) collective-permute-start(bf16[384,512]{1,0:T(8,128)(2,1)S(1)} %pad_maximum_fusion.own), channel_id=1, source_target_pairs={{0,1},{1,2},{2,3},{3,0},{4,5},{5,6},{6,7},{7,4},{8,9},{9,10},{10,1... | collective-permute-start | bytes 1179656 | tf_op jit(solution)/shard_map/ppermute | solution.py:120
  50.0 26.1 %collective-permute-start.7 = (bf16[128,4096]{1,0:T(8,128)(2,1)S(1)}, bf16[128,4096]{1,0:T(8,128)(2,1)}, u32[]{:S(2)}, u32[]{:S(2)}) collective-permute-start(bf16[128,4096]{1,0:T(8,128)(2,1)S(1)} %bitcast.48), channel_id=1, source_target_pairs={{0,12},{1,13},{2,14},{3,15},{4,0},{5,1},{6,2},{7,3},{8,4},{9,5},{1... | collective-permute-start | bytes 3145736 | tf_op jit(solution)/shard_map/ppermute | solution.py:120
  54.5 28.0 %collective-permute-start.6 = (bf16[128,4096]{1,0:T(8,128)(2,1)S(1)}, bf16[128,4096]{1,0:T(8,128)(2,1)}, u32[]{:S(2)}, u32[]{:S(2)}) collective-permute-start(bf16[128,4096]{1,0:T(8,128)(2,1)S(1)} %bitcast.49), channel_id=1, source_target_pairs={{0,4},{1,5},{2,6},{3,7},{4,8},{5,9},{6,10},{7,11},{8,12},{9,13},{1... | collective-permute-start | bytes 3145736 | tf_op jit(solution)/shard_map/ppermute | solution.py:120
  56.5 5.5 %copy-start.2 = (bf16[384,512]{1,0:T(8,128)(2,1)}, bf16[384,512]{1,0:T(8,128)(2,1)S(1)}, u32[]{:S(2)}) copy-start(bf16[384,512]{1,0:T(8,128)(2,1)S(1)} %collective-permute-done.2.far) | copy-start | bytes 1179652
  62.0 0.8 copy-start.3
  67.7 21.8 %all-to-all-start.2 = ((bf16[16,8,32,128]{3,2,1,0:T(8,128)(2,1)}), bf16[16,8,32,128]{3,2,1,0:T(8,128)(2,1)}, u32[]{:S(2)}, u32[]{:S(2)}) async-start(bf16[16,8,32,128]{3,2,1,0:T(8,128)(2,1)} %front.1), calls=%async_computation.2 | async-start | bytes 2097152 | tf_op jit(solution)/shard_map/all_to_all | solution.py:167
  77.9 15.9 %collective-permute-start.9 = (bf16[64,4096]{1,0:T(8,128)(2,1)}, bf16[64,4096]{1,0:T(8,128)(2,1)}, u32[]{:S(2)}, u32[]{:S(2)}) collective-permute-start(bf16[64,4096]{1,0:T(8,128)(2,1)} %slice.29), channel_id=1, source_target_pairs={{0,12},{1,13},{2,14},{3,15},{4,0},{5,1},{6,2},{7,3},{8,4},{9,5},{1... | collective-permute-start | bytes 1572872 | tf_op jit(solution)/shard_map/ppermute | solution.py:120
  84.4 12.6 %collective-permute-start.8 = (bf16[64,4096]{1,0:T(8,128)(2,1)}, bf16[64,4096]{1,0:T(8,128)(2,1)}, u32[]{:S(2)}, u32[]{:S(2)}) collective-permute-start(bf16[64,4096]{1,0:T(8,128)(2,1)} %slice.28), channel_id=1, source_target_pairs={{0,4},{1,5},{2,6},{3,7},{4,8},{5,9},{6,10},{7,11},{8,12},{9,13},{1... | collective-permute-start | bytes 1572872 | tf_op jit(solution)/shard_map/ppermute | solution.py:120
  91.7 22.4 %copy-start = (bf16[4,4,8,32,128]{4,2,1,3,0:T(8,128)(2,1)}, bf16[4,4,8,32,128]{4,2,1,3,0:T(8,128)(2,1)S(1)}, u32[]{:S(2)}) copy-start(bf16[4,4,8,32,128]{4,2,1,3,0:T(8,128)(2,1)S(1)} %bitcast_select_fusion) | copy-start | bytes 3145732
  91.8 9.8 %collective-permute-start.5 = (bf16[256,512]{1,0:T(8,128)(2,1)S(1)}, bf16[256,512]{1,0:T(8,128)(2,1)S(1)}, u32[]{:S(2)}, u32[]{:S(2)}) collective-permute-start(bf16[256,512]{1,0:T(8,128)(2,1)S(1)} %fusion.6), channel_id=1, source_target_pairs={{0,20},{1,21},{2,22},{3,23},{4,16},{5,17},{6,18},{7,19},{8,28},{9,... | collective-permute-start | bytes 786440 | tf_op jit(solution)/shard_map/ppermute | solution.py:120
  93.8 14.0 %collective-permute-start.4 = (bf16[256,512]{1,0:T(8,128)(2,1)S(1)}, bf16[256,512]{1,0:T(8,128)(2,1)S(1)}, u32[]{:S(2)}, u32[]{:S(2)}) collective-permute-start(bf16[256,512]{1,0:T(8,128)(2,1)S(1)} %fusion.6), channel_id=1, source_target_pairs={{0,16},{1,17},{2,18},{3,19},{4,20},{5,21},{6,22},{7,23},{8,24},{9,... | collective-permute-start | bytes 786440 | tf_op jit(solution)/shard_map/ppermute | solution.py:120
  107.8 23.5 %collective-permute-start.10 = (bf16[512,512]{1,0:T(8,128)(2,1)}, bf16[512,512]{1,0:T(8,128)(2,1)}, u32[]{:S(2)}, u32[]{:S(2)}) collective-permute-start(bf16[512,512]{1,0:T(8,128)(2,1)} %back.2), channel_id=1, source_target_pairs={{0,1},{1,0},{2,3},{3,2},{4,5},{5,4},{6,7},{7,6},{8,9},{9,8},{10,11... | collective-permute-start | bytes 1572872 | tf_op jit(solution)/shard_map/ppermute | solution.py:120

commit v7 on v6

--- a/solution.py
+++ b/solution.py
@@ -169,9 +169,12 @@
     fresh = [fresh[i].astype(F32) for i in range(4)]
     fresh = ((fresh[0] + fresh[1]) + (fresh[2] + fresh[3])).astype(BF)
     source = fresh.transpose(2, 1, 0, 3).reshape(256, chi)
-    new_left = source.reshape(32, 8, chi)
-    turn = new_left.reshape(32, 8, 4, 4, 32).transpose(0, 1, 3, 2, 4).reshape(32, 8, chi)
-    new_left = jnp.where(odd, new_left, turn)
+    i = lax.broadcasted_iota(jnp.int32, (chi, chi), 0)
+    j = lax.broadcasted_iota(jnp.int32, (chi, chi), 1)
+    place = jnp.where(odd, i, i // 32 % 4 * 128 + i // 128 * 32 + i % 32)
+    place = (place == j).astype(BF)
+    source, place = lax.optimization_barrier((source, place))
+    new_left = jnp.dot(source, place, preferred_element_type=F32).astype(BF).reshape(32, 8, chi)
     other = moved(source, lambda b: b ^ 1, 1)
     source = moved(source, lambda b: b, 1)
     give = applied(offsets, other, pieces, two_site, right)

time: 135 us -> 123 us (0.911)
  local copies, waits for them, and re-layouts: 24.3 us -> 15 us
  other arithmetic: 8.34 us -> 6.38 us
    another operation x2 -> x0, local copies, waits for them, and re-layouts: 5.82 us -> none  [shards(): new_left.reshape(32, 8, 4, 4, 32).transpose(0, 1, 3, 2, 4)]
    reshape x1 -> x0, local copies, waits for them, and re-layouts: 3.52 us -> none  [shards(): new_left.reshape(32, 8, 4, 4, 32).transpose(0, 1, 3, 2, 4)]
    select_n x1 -> x0, other arithmetic: 2.14 us -> none  [shards(): new_left = jnp.where(odd, new_left, turn)]
    all_to_all x1, waiting for transfers between devices: 3.26 us -> 1.15 us  [shards(): lax.all_to_all(fresh, 'bond', 0, 0, tiled=True).reshape(4, 4, 8, 32, 128)]
    convert_element_type x0 -> x1, other arithmetic: none -> 2.04 us  [shards(): place = (place == j).astype(BF)]
    ppermute x11, waiting for transfers between devices: 22.5 us -> 24.4 us  [moved(): return lax.ppermute(block, ('sec', 'bond'), routed(sections, step, ahead))]
  transfers between devices with their start and end apart: 14 -> 14, of which waited for: 7 -> 8; matrix products, arithmetic and copies ran while one was open for 22% -> 17% of each run, Pallas kernels for 12% -> 12%
where the time goes in v7:
time: 123 us; the launch traced here: 122 us
  starting transfers between devices  50.2 us (41%)
  waiting for transfers between devices  32.2 us (26%)
  local copies, waits for them, and re-layouts  15 us (12%)
  Pallas kernels  14.6 us (12%)
  other arithmetic  6.38 us (5%)
  matrix products  2.18 us (2%)
    ppermute x11, starting transfers between devices, moved(): return lax.ppermute(block, ('sec', 'bond'), routed(sections, step, ahead))  30.5 us
    ppermute x11, waiting for transfers between devices, moved(): return lax.ppermute(block, ('sec', 'bond'), routed(sections, step, ahead))  24.4 us
    pallas_call x2, Pallas kernels, applied(): pl.pallas_call(back, out_shape=jax.ShapeDtypeStruct((512, 512), BF), in_s...  9.64 us
    all_to_all x1, starting transfers between devices, shards(): lax.all_to_all(fresh, 'bond', 0, 0, tiled=True).reshape(4, 4, 8, 32, 128)  8.3 us
    all_to_all x1, waiting for transfers between devices, shards(): lax.all_to_all(send, ('sec', 'bond'), 0, 0, axis_index_groups=lines, tile...  6.62 us
    all_to_all x1, starting transfers between devices, shards(): cols = lax.all_to_all(cols, 'bond', 0, 0, tiled=True)  6.55 us
    pallas_call x1, Pallas kernels, shards(): pl.pallas_call(front, out_shape=jax.ShapeDtypeStruct((16, 8, 32, 128), BF...  4.95 us
    all_to_all x1, starting transfers between devices, shards(): lax.all_to_all(send, ('sec', 'bond'), 0, 0, axis_index_groups=lines, tile...  4.82 us
  transfers between devices with their start and end apart: 14, of which 8 were waited for; matrix products, arithmetic and copies ran while one was open for 17% of the time, Pallas kernels for 12%

profile of v7, /device:TPU:2, one launch (start us, length us, event | category | flops | bytes accessed | tf_op | source)
XLA Modules:
  0.0 121.5 jit_solution(11822439737537419587)
XLA Ops:
  2.6 1.2 %reshape_squeeze.11 = bf16[32,4,4,4,32]{4,3,2,1,0:T(4,128)(2,1)S(1)} reshape(bf16[1,32,4,512]{3,2,1,0:T(4,128)(2,1)} %param.7) | data formatting | bytes 262144 | tf_op jit(solution)/shard_map/reshape;squeeze | solution.py:136
  5.4 1.2 fusion
  8.0 8.6 %collective-permute-done.3 = bf16[32,4,4,512]{3,2,1,0:T(4,128)(2,1)S(1)} collective-permute-done((bf16[32,4,4,512]{3,2,1,0:T(4,128)(2,1)}, bf16[32,4,4,512]{3,2,1,0:T(4,128)(2,1)S(1)}, u32[]{:S(2)}, u32[]{:S(2)}) %collective-permute-start.3) | collective-permute-done | bytes 524320 | tf_op jit(solution)/shard_map/ppermute | solution.py:120
  17.2 1.1 broadcast_in_dim.26
  18.3 4.8 %all-to-all-start = ((bf16[4,32,4096]{2,1,0:T(8,128)(2,1)}), bf16[4,32,4096]{2,1,0:T(8,128)(2,1)S(1)}, u32[]{:S(2)}, u32[]{:S(2)}) async-start(bf16[4,32,4096]{2,1,0:T(8,128)(2,1)} %bitcast.3), calls=%async_computation | async-start | bytes 2097152 | tf_op jit(solution)/shard_map/all_to_all | solution.py:132
  23.3 1.8 %constant_dynamic-slice_fusion = bf16[1,8,256,512]{3,2,1,0:T(8,128)(2,1)S(1)} fusion(bf16[1,8,512,512]{3,2,1,0:T(8,128)(2,1)} %param.9, s32[]{:T(128)S(6)} %select_n.105), kind=kLoop, calls=%fused_computation.48 | loop fusion | bytes 4194308 | tf_op jit(solution)/shard_map/dynamic_slice | solution.py:141
  25.9 6.6 %all-to-all-done = bf16[4,32,4096]{2,1,0:T(8,128)(2,1)S(1)} async-done(((bf16[4,32,4096]{2,1,0:T(8,128)(2,1)}), bf16[4,32,4096]{2,1,0:T(8,128)(2,1)S(1)}, u32[]{:S(2)}, u32[]{:S(2)}) %all-to-all-start) | async-done | bytes 1048608 | tf_op jit(solution)/shard_map/all_to_all | solution.py:132
  32.6 6.6 %all-to-all-start.1 = ((bf16[16,4,32,128]{3,2,1,0:T(8,128)(2,1)}), bf16[16,4,32,128]{3,2,1,0:T(8,128)(2,1)}, u32[]{:S(2)}, u32[]{:S(2)}) async-start(bf16[16,4,32,128]{3,2,1,0:T(8,128)(2,1)} %bitcast.46), calls=%async_computation.1 | async-start | bytes 1048576 | tf_op jit(solution)/shard_map/all_to_all | solution.py:150
  40.1 4.0 %collective-permute-start.2 = (bf16[384,512]{1,0:T(8,128)(2,1)S(1)}, bf16[384,512]{1,0:T(8,128)(2,1)S(1)}, u32[]{:S(2)}, u32[]{:S(2)}) collective-permute-start(bf16[384,512]{1,0:T(8,128)(2,1)S(1)} %pad_maximum_fusion.own), channel_id=1, source_target_pairs={{0,2},{1,3},{2,0},{3,1},{4,6},{5,7},{6,4},{7,5},{8,10},{9,11},{10,... | collective-permute-start | bytes 1179656 | tf_op jit(solution)/shard_map/ppermute | solution.py:120
  44.1 3.4 %collective-permute-start.1 = (bf16[384,512]{1,0:T(8,128)(2,1)S(1)}, bf16[384,512]{1,0:T(8,128)(2,1)S(1)}, u32[]{:S(2)}, u32[]{:S(2)}) collective-permute-start(bf16[384,512]{1,0:T(8,128)(2,1)S(1)} %pad_maximum_fusion.own), channel_id=1, source_target_pairs={{0,3},{1,0},{2,1},{3,2},{4,7},{5,4},{6,5},{7,6},{8,11},{9,8},{10,9... | collective-permute-start | bytes 1179656 | tf_op jit(solution)/shard_map/ppermute | solution.py:120
  47.5 2.5 %collective-permute-start = (bf16[384,512]{1,0:T(8,128)(2,1)S(1)}, bf16[384,512]{1,0:T(8,128)(2,1)}, u32[]{:S(2)}, u32[]{:S(2)}) collective-permute-start(bf16[384,512]{1,0:T(8,128)(2,1)S(1)} %pad_maximum_fusion.own), channel_id=1, source_target_pairs={{0,1},{1,2},{2,3},{3,0},{4,5},{5,6},{6,7},{7,4},{8,9},{9,10},{10,1... | collective-permute-start | bytes 1179656 | tf_op jit(solution)/shard_map/ppermute | solution.py:120
  50.0 4.6 %collective-permute-start.7 = (bf16[128,4096]{1,0:T(8,128)(2,1)S(1)}, bf16[128,4096]{1,0:T(8,128)(2,1)}, u32[]{:S(2)}, u32[]{:S(2)}) collective-permute-start(bf16[128,4096]{1,0:T(8,128)(2,1)S(1)} %bitcast.41), channel_id=1, source_target_pairs={{0,12},{1,13},{2,14},{3,15},{4,0},{5,1},{6,2},{7,3},{8,4},{9,5},{1... | collective-permute-start | bytes 3145736 | tf_op jit(solution)/shard_map/ppermute | solution.py:120
  54.6 1.9 %collective-permute-start.6 = (bf16[128,4096]{1,0:T(8,128)(2,1)S(1)}, bf16[128,4096]{1,0:T(8,128)(2,1)}, u32[]{:S(2)}, u32[]{:S(2)}) collective-permute-start(bf16[128,4096]{1,0:T(8,128)(2,1)S(1)} %bitcast.42), channel_id=1, source_target_pairs={{0,4},{1,5},{2,6},{3,7},{4,8},{5,9},{6,10},{7,11},{8,12},{9,13},{1... | collective-permute-start | bytes 3145736 | tf_op jit(solution)/shard_map/ppermute | solution.py:120
  56.5 5.5 %collective-permute-done.1.back_ = bf16[384,512]{1,0:T(8,128)(2,1)S(1)} collective-permute-done((bf16[384,512]{1,0:T(8,128)(2,1)S(1)}, bf16[384,512]{1,0:T(8,128)(2,1)S(1)}, u32[]{:S(2)}, u32[]{:S(2)}) %collective-permute-start.1) | collective-permute-done | bytes 393248 | tf_op jit(solution)/shard_map/ppermute | solution.py:120
  62.8 5.0 %front.1 = bf16[16,8,32,128]{3,2,1,0:T(8,128)(2,1)} custom-call(bf16[384,512]{1,0:T(8,128)(2,1)} %copy-done.1, bf16[384,512]{1,0:T(8,128)(2,1)} %collective-permute-done.near, bf16[384,512]{1,0:T(8,128)(2,1)} %copy-done.3, bf16[384,512]{1,0:T(8,128)(2,1)} %copy-done.2, bf16[16,4,32,128]{3,2,1,0:T(8,128)(2,1)} %all-to-all-done.1.cols, ...), custom_call_target="tpu_custom_call" | custom-call | flops 2000000000 | bytes 4000000 | tf_op jit(solution)/shard_map/front/pallas_call | solution.py:151
  67.8 8.3 %all-to-all-start.2 = ((bf16[16,8,32,128]{3,2,1,0:T(8,128)(2,1)}), bf16[16,8,32,128]{3,2,1,0:T(8,128)(2,1)}, u32[]{:S(2)}, u32[]{:S(2)}) async-start(bf16[16,8,32,128]{3,2,1,0:T(8,128)(2,1)} %front.1), calls=%async_computation.2 | async-start | bytes 2097152 | tf_op jit(solution)/shard_map/all_to_all | solution.py:167
  76.1 2.0 %fusion.8 = bf16[512,512]{1,0:T(8,128)(2,1)} fusion(s32[512]{0:T(512)S(1)} %get-tuple-element.24, s32[512]{0:T(512)S(1)} %get-tuple-element.25, s32[512]{0:T(512)S(1)} %get-tuple-element.22, s32[512]{0:T(512)S(1)} %get-tuple-element.28, s32[512]{0:T(512)S(1)} %get-tuple-element.23, s32[512]{0:T(512)S(1)} %get-tuple-element.29, ...), kind=kLoop, calls=%fused_computation.17 | loop fusion | flops 5505024 | bytes 538113 | tf_op jit(solution)/shard_map/convert_element_type | solution.py:175
  78.2 1.9 %slice.29 = bf16[64,4096]{1,0:T(8,128)(2,1)} slice(bf16[128,4096]{1,0:T(8,128)(2,1)} %collective-permute-done.7.down), slice={[64:128], [0:4096]} | slice | bytes 1048576 | tf_op jit(solution)/shard_map/slice | solution.py:148
  80.0 4.6 %collective-permute-start.9 = (bf16[64,4096]{1,0:T(8,128)(2,1)}, bf16[64,4096]{1,0:T(8,128)(2,1)}, u32[]{:S(2)}, u32[]{:S(2)}) collective-permute-start(bf16[64,4096]{1,0:T(8,128)(2,1)} %slice.29), channel_id=1, source_target_pairs={{0,12},{1,13},{2,14},{3,15},{4,0},{5,1},{6,2},{7,3},{8,4},{9,5},{1... | collective-permute-start | bytes 1572872 | tf_op jit(solution)/shard_map/ppermute | solution.py:120
  84.6 1.9 %slice.28 = bf16[64,4096]{1,0:T(8,128)(2,1)} slice(bf16[128,4096]{1,0:T(8,128)(2,1)} %collective-permute-done.6.up), slice={[0:64], [0:4096]} | slice | bytes 1048576 | tf_op jit(solution)/shard_map/slice | solution.py:147
  86.5 1.9 %collective-permute-start.8 = (bf16[64,4096]{1,0:T(8,128)(2,1)}, bf16[64,4096]{1,0:T(8,128)(2,1)}, u32[]{:S(2)}, u32[]{:S(2)}) collective-permute-start(bf16[64,4096]{1,0:T(8,128)(2,1)} %slice.28), channel_id=1, source_target_pairs={{0,4},{1,5},{2,6},{3,7},{4,8},{5,9},{6,10},{7,11},{8,12},{9,13},{1... | collective-permute-start | bytes 1572872 | tf_op jit(solution)/shard_map/ppermute | solution.py:120
  88.4 1.1 all-to-all-done.2
  89.6 2.1 %bitcast_select_fusion = bf16[4,4,8,32,128]{4,2,1,3,0:T(8,128)(2,1)S(1)} fusion(bf16[4,4,8,32,128]{4,3,2,1,0:T(8,128)(2,1)} %bitcast.13, pred[]{:T(512)S(6)} %eq.16), kind=kLoop, calls=%fused_computation.15 | loop fusion | flops 524288 | bytes 2097153 | tf_op jit(solution)/shard_map/jit(_where)/select_n | solution.py:168
  91.9 2.1 %collective-permute-start.5 = (bf16[256,512]{1,0:T(8,128)(2,1)S(1)}, bf16[256,512]{1,0:T(8,128)(2,1)S(1)}, u32[]{:S(2)}, u32[]{:S(2)}) collective-permute-start(bf16[256,512]{1,0:T(8,128)(2,1)S(1)} %fusion.9), channel_id=1, source_target_pairs={{0,20},{1,21},{2,22},{3,23},{4,16},{5,17},{6,18},{7,19},{8,28},{9,... | collective-permute-start | bytes 786440 | tf_op jit(solution)/shard_map/ppermute | solution.py:120
  94.0 5.1 %collective-permute-done.8.far_a = bf16[64,4096]{1,0:T(8,128)(2,1)} collective-permute-done((bf16[64,4096]{1,0:T(8,128)(2,1)}, bf16[64,4096]{1,0:T(8,128)(2,1)}, u32[]{:S(2)}, u32[]{:S(2)}) %collective-permute-start.8) | collective-permute-done | bytes 524320 | tf_op jit(solution)/shard_map/ppermute | solution.py:120
  99.1 2.7 %collective-permute-done.5.left = bf16[256,512]{1,0:T(8,128)(2,1)S(1)} collective-permute-done((bf16[256,512]{1,0:T(8,128)(2,1)S(1)}, bf16[256,512]{1,0:T(8,128)(2,1)S(1)}, u32[]{:S(2)}, u32[]{:S(2)}) %collective-permute-start.5) | collective-permute-done | bytes 262176 | tf_op jit(solution)/shard_map/ppermute | solution.py:120
  101.8 4.8 %back.2 = bf16[512,512]{1,0:T(8,128)(2,1)S(1)} custom-call(s32[4]{0:T(128)S(1)} %fusion.22.offsets, bf16[256,512]{1,0:T(8,128)(2,1)S(1)} %collective-permute-done.5.left, bf16[128,4096]{1,0:T(8,128)(2,1)S(1)} %bitcast.43, bf16[128,4096]{1,0:T(8,128)(2,1)} %collective-permute-done.6.up, bf16[128,4096]{1,0:T(8,128)(2,1)} %collective-permute-done.7.down, ...), custom_call_target="tpu_custom_call" | custom-call | flops 2500000000 | bytes 8000000 | tf_op jit(solution)/shard_map/back/pallas_call | solution.py:99
  106.6 1.3 %collective-permute-done.4.left = bf16[256,512]{1,0:T(8,128)(2,1)S(1)} collective-permute-done((bf16[256,512]{1,0:T(8,128)(2,1)S(1)}, bf16[256,512]{1,0:T(8,128)(2,1)S(1)}, u32[]{:S(2)}, u32[]{:S(2)}) %collective-permute-start.4) | collective-permute-done | bytes 262176 | tf_op jit(solution)/shard_map/ppermute | solution.py:120
  107.9 5.6 %collective-permute-start.10 = (bf16[512,512]{1,0:T(8,128)(2,1)S(1)}, bf16[512,512]{1,0:T(8,128)(2,1)S(1)}, u32[]{:S(2)}, u32[]{:S(2)}) collective-permute-start(bf16[512,512]{1,0:T(8,128)(2,1)S(1)} %back.2), channel_id=1, source_target_pairs={{0,1},{1,0},{2,3},{3,2},{4,5},{5,4},{6,7},{7,6},{8,9},{9,8},{10,11... | collective-permute-start | bytes 1572872 | tf_op jit(solution)/shard_map/ppermute | solution.py:120
  113.5 1.0 fusion.1
  114.5 4.8 %back.3 = bf16[512,512]{1,0:T(8,128)(2,1)S(1)} custom-call(s32[4]{0:T(128)S(1)} %fusion.22.offsets, bf16[256,512]{1,0:T(8,128)(2,1)S(1)} %collective-permute-done.4.left, bf16[128,4096]{1,0:T(8,128)(2,1)S(1)} %bitcast.44, bf16[128,4096]{1,0:T(8,128)(2,1)} %collective-permute-done.6.up, bf16[128,4096]{1,0:T(8,128)(2,1)} %collective-permute-done.7.down, ...), custom_call_target="tpu_custom_call" | custom-call | flops 2500000000 | bytes 8000000 | tf_op jit(solution)/shard_map/back/pallas_call | solution.py:99
  119.4 1.1 collective-permute-done.10
  (42 shorter events, 9.4 us)
Async XLA Ops:
  0.6 16.0 %collective-permute-start.3 = (bf16[32,4,4,512]{3,2,1,0:T(4,128)(2,1)}, bf16[32,4,4,512]{3,2,1,0:T(4,128)(2,1)S(1)}, u32[]{:S(2)}, u32[]{:S(2)}) collective-permute-start(bf16[32,4,4,512]{3,2,1,0:T(4,128)(2,1)} %bitcast.51), channel_id=1, source_target_pairs={{0,16},{1,17},{2,18},{3,19},{4,20},{5,21},{6,22},{7,23},{8,24},{9,... | collective-permute-start | bytes 1572872 | tf_op jit(solution)/shard_map/ppermute | solution.py:120
  17.2 7.9 %copy-start.4 = (s32[4]{0:T(128)S(1)}, s32[4]{0:T(128)}, u32[]{:S(2)}) copy-start(s32[4]{0:T(128)} %constant.118.clone) | copy-start | bytes 52
  18.3 14.3 %all-to-all-start = ((bf16[4,32,4096]{2,1,0:T(8,128)(2,1)}), bf16[4,32,4096]{2,1,0:T(8,128)(2,1)S(1)}, u32[]{:S(2)}, u32[]{:S(2)}) async-start(bf16[4,32,4096]{2,1,0:T(8,128)(2,1)} %bitcast.3), calls=%async_computation | async-start | bytes 2097152 | tf_op jit(solution)/shard_map/all_to_all | solution.py:132
  32.6 30.2 %all-to-all-start.1 = ((bf16[16,4,32,128]{3,2,1,0:T(8,128)(2,1)}), bf16[16,4,32,128]{3,2,1,0:T(8,128)(2,1)}, u32[]{:S(2)}, u32[]{:S(2)}) async-start(bf16[16,4,32,128]{3,2,1,0:T(8,128)(2,1)} %bitcast.46), calls=%async_computation.1 | async-start | bytes 1048576 | tf_op jit(solution)/shard_map/all_to_all | solution.py:150
  40.1 9.9 %copy-start.1 = (bf16[384,512]{1,0:T(8,128)(2,1)}, bf16[384,512]{1,0:T(8,128)(2,1)S(1)}, u32[]{:S(2)}) copy-start(bf16[384,512]{1,0:T(8,128)(2,1)S(1)} %pad_maximum_fusion.own) | copy-start | bytes 1179652
  40.1 16.4 %collective-permute-start.2 = (bf16[384,512]{1,0:T(8,128)(2,1)S(1)}, bf16[384,512]{1,0:T(8,128)(2,1)S(1)}, u32[]{:S(2)}, u32[]{:S(2)}) collective-permute-start(bf16[384,512]{1,0:T(8,128)(2,1)S(1)} %pad_maximum_fusion.own), channel_id=1, source_target_pairs={{0,2},{1,3},{2,0},{3,1},{4,6},{5,7},{6,4},{7,5},{8,10},{9,11},{10,... | collective-permute-start | bytes 1179656 | tf_op jit(solution)/shard_map/ppermute | solution.py:120
  44.1 17.9 %collective-permute-start.1 = (bf16[384,512]{1,0:T(8,128)(2,1)S(1)}, bf16[384,512]{1,0:T(8,128)(2,1)S(1)}, u32[]{:S(2)}, u32[]{:S(2)}) collective-permute-start(bf16[384,512]{1,0:T(8,128)(2,1)S(1)} %pad_maximum_fusion.own), channel_id=1, source_target_pairs={{0,3},{1,0},{2,1},{3,2},{4,7},{5,4},{6,5},{7,6},{8,11},{9,8},{10,9... | collective-permute-start | bytes 1179656 | tf_op jit(solution)/shard_map/ppermute | solution.py:120
  47.5 15.3 %collective-permute-start = (bf16[384,512]{1,0:T(8,128)(2,1)S(1)}, bf16[384,512]{1,0:T(8,128)(2,1)}, u32[]{:S(2)}, u32[]{:S(2)}) collective-permute-start(bf16[384,512]{1,0:T(8,128)(2,1)S(1)} %pad_maximum_fusion.own), channel_id=1, source_target_pairs={{0,1},{1,2},{2,3},{3,0},{4,5},{5,6},{6,7},{7,4},{8,9},{9,10},{10,1... | collective-permute-start | bytes 1179656 | tf_op jit(solution)/shard_map/ppermute | solution.py:120
  50.0 28.2 %collective-permute-start.7 = (bf16[128,4096]{1,0:T(8,128)(2,1)S(1)}, bf16[128,4096]{1,0:T(8,128)(2,1)}, u32[]{:S(2)}, u32[]{:S(2)}) collective-permute-start(bf16[128,4096]{1,0:T(8,128)(2,1)S(1)} %bitcast.41), channel_id=1, source_target_pairs={{0,12},{1,13},{2,14},{3,15},{4,0},{5,1},{6,2},{7,3},{8,4},{9,5},{1... | collective-permute-start | bytes 3145736 | tf_op jit(solution)/shard_map/ppermute | solution.py:120
  54.6 30.1 %collective-permute-start.6 = (bf16[128,4096]{1,0:T(8,128)(2,1)S(1)}, bf16[128,4096]{1,0:T(8,128)(2,1)}, u32[]{:S(2)}, u32[]{:S(2)}) collective-permute-start(bf16[128,4096]{1,0:T(8,128)(2,1)S(1)} %bitcast.42), channel_id=1, source_target_pairs={{0,4},{1,5},{2,6},{3,7},{4,8},{5,9},{6,10},{7,11},{8,12},{9,13},{1... | collective-permute-start | bytes 3145736 | tf_op jit(solution)/shard_map/ppermute | solution.py:120
  56.5 5.5 %copy-start.2 = (bf16[384,512]{1,0:T(8,128)(2,1)}, bf16[384,512]{1,0:T(8,128)(2,1)S(1)}, u32[]{:S(2)}) copy-start(bf16[384,512]{1,0:T(8,128)(2,1)S(1)} %collective-permute-done.2.far) | copy-start | bytes 1179652
  62.0 0.8 copy-start.3
  67.8 21.8 %all-to-all-start.2 = ((bf16[16,8,32,128]{3,2,1,0:T(8,128)(2,1)}), bf16[16,8,32,128]{3,2,1,0:T(8,128)(2,1)}, u32[]{:S(2)}, u32[]{:S(2)}) async-start(bf16[16,8,32,128]{3,2,1,0:T(8,128)(2,1)} %front.1), calls=%async_computation.2 | async-start | bytes 2097152 | tf_op jit(solution)/shard_map/all_to_all | solution.py:167
  80.0 13.9 %collective-permute-start.9 = (bf16[64,4096]{1,0:T(8,128)(2,1)}, bf16[64,4096]{1,0:T(8,128)(2,1)}, u32[]{:S(2)}, u32[]{:S(2)}) collective-permute-start(bf16[64,4096]{1,0:T(8,128)(2,1)} %slice.29), channel_id=1, source_target_pairs={{0,12},{1,13},{2,14},{3,15},{4,0},{5,1},{6,2},{7,3},{8,4},{9,5},{1... | collective-permute-start | bytes 1572872 | tf_op jit(solution)/shard_map/ppermute | solution.py:120
  86.5 12.6 %collective-permute-start.8 = (bf16[64,4096]{1,0:T(8,128)(2,1)}, bf16[64,4096]{1,0:T(8,128)(2,1)}, u32[]{:S(2)}, u32[]{:S(2)}) collective-permute-start(bf16[64,4096]{1,0:T(8,128)(2,1)} %slice.28), channel_id=1, source_target_pairs={{0,4},{1,5},{2,6},{3,7},{4,8},{5,9},{6,10},{7,11},{8,12},{9,13},{1... | collective-permute-start | bytes 1572872 | tf_op jit(solution)/shard_map/ppermute | solution.py:120
  91.9 21.7 %copy-start = (bf16[512,512]{1,0:T(8,128)(2,1)S(1)}, bf16[512,512]{1,0:T(8,128)(2,1)}, u32[]{:S(2)}) copy-start(bf16[512,512]{1,0:T(8,128)(2,1)} %fusion.8) | copy-start | bytes 1572868
  91.9 9.9 %collective-permute-start.5 = (bf16[256,512]{1,0:T(8,128)(2,1)S(1)}, bf16[256,512]{1,0:T(8,128)(2,1)S(1)}, u32[]{:S(2)}, u32[]{:S(2)}) collective-permute-start(bf16[256,512]{1,0:T(8,128)(2,1)S(1)} %fusion.9), channel_id=1, source_target_pairs={{0,20},{1,21},{2,22},{3,23},{4,16},{5,17},{6,18},{7,19},{8,28},{9,... | collective-permute-start | bytes 786440 | tf_op jit(solution)/shard_map/ppermute | solution.py:120
  93.9 14.0 %collective-permute-start.4 = (bf16[256,512]{1,0:T(8,128)(2,1)S(1)}, bf16[256,512]{1,0:T(8,128)(2,1)S(1)}, u32[]{:S(2)}, u32[]{:S(2)}) collective-permute-start(bf16[256,512]{1,0:T(8,128)(2,1)S(1)} %fusion.9), channel_id=1, source_target_pairs={{0,16},{1,17},{2,18},{3,19},{4,20},{5,21},{6,22},{7,23},{8,24},{9,... | collective-permute-start | bytes 786440 | tf_op jit(solution)/shard_map/ppermute | solution.py:120
  107.9 12.6 %collective-permute-start.10 = (bf16[512,512]{1,0:T(8,128)(2,1)S(1)}, bf16[512,512]{1,0:T(8,128)(2,1)S(1)}, u32[]{:S(2)}, u32[]{:S(2)}) collective-permute-start(bf16[512,512]{1,0:T(8,128)(2,1)S(1)} %back.2), channel_id=1, source_target_pairs={{0,1},{1,0},{2,3},{3,2},{4,5},{5,4},{6,7},{7,6},{8,9},{9,8},{10,11... | collective-permute-start | bytes 1572872 | tf_op jit(solution)/shard_map/ppermute | solution.py:120

commit v8 on v7

--- a/solution.py
+++ b/solution.py
@@ -127,6 +127,7 @@
     own = jnp.concatenate([left_env[0].reshape(256, chi), site[0].reshape(128, chi)], axis=0)
     blocks = [own] + [moved(own, along_line(d)) for d in (1, -1, 2)]
     pair = moved(psi[0], lambda b: b, 1)
+    pair, blocks[1], blocks[2] = lax.optimization_barrier((pair, blocks[1], blocks[2]))
     halves = pair.reshape(32, 16, 2, 256).transpose(2, 0, 1, 3).reshape(2, 32, 4096)
     send = jnp.broadcast_to(halves[None], (2, 2, 32, 4096)).reshape(4, 32, 4096)
     pair = lax.all_to_all(send, ("sec", "bond"), 0, 0, axis_index_groups=lines, tiled=True).reshape(128, 4096)

time: 123 us -> 118 us (0.959)
  waiting for transfers between devices: 32.2 us -> 28.6 us
    ppermute x11, waiting for transfers between devices: 24.4 us -> 17 us  [moved(): return lax.ppermute(block, ('sec', 'bond'), routed(sections, step, ahead))]
    all_to_all x1, waiting for transfers between devices: 1.15 us -> 5.01 us  [shards(): lax.all_to_all(fresh, 'bond', 0, 0, tiled=True).reshape(4, 4, 8, 32, 128)]
  transfers between devices with their start and end apart: 14 -> 14, of which waited for: 8 -> 7; matrix products, arithmetic and copies ran while one was open for 17% -> 17% of each run, Pallas kernels for 12% -> 13%
where the time goes in v8:
time: 118 us; the launch traced here: 116 us
  starting transfers between devices  49.3 us (42%)
  waiting for transfers between devices  28.6 us (24%)
  Pallas kernels  14.6 us (12%)
  local copies, waits for them, and re-layouts  14.3 us (12%)
  other arithmetic  6.39 us (5%)
  matrix products  2.18 us (2%)
    ppermute x11, starting transfers between devices, moved(): return lax.ppermute(block, ('sec', 'bond'), routed(sections, step, ahead))  31 us
    ppermute x11, waiting for transfers between devices, moved(): return lax.ppermute(block, ('sec', 'bond'), routed(sections, step, ahead))  17 us
    pallas_call x2, Pallas kernels, applied(): pl.pallas_call(back, out_shape=jax.ShapeDtypeStruct((512, 512), BF), in_s...  9.65 us
    all_to_all x1, starting transfers between devices, shards(): lax.all_to_all(fresh, 'bond', 0, 0, tiled=True).reshape(4, 4, 8, 32, 128)  8.19 us
    all_to_all x1, waiting for transfers between devices, shards(): lax.all_to_all(send, ('sec', 'bond'), 0, 0, axis_index_groups=lines, tile...  6.59 us
    all_to_all x1, starting transfers between devices, shards(): cols = lax.all_to_all(cols, 'bond', 0, 0, tiled=True)  5.42 us
    all_to_all x1, waiting for transfers between devices, shards(): lax.all_to_all(fresh, 'bond', 0, 0, tiled=True).reshape(4, 4, 8, 32, 128)  5.01 us
    pallas_call x1, Pallas kernels, shards(): pl.pallas_call(front, out_shape=jax.ShapeDtypeStruct((16, 8, 32, 128), BF...  4.95 us
  transfers between devices with their start and end apart: 14, of which 7 were waited for; matrix products, arithmetic and copies ran while one was open for 17% of the time, Pallas kernels for 13%

profile of v8, /device:TPU:2, one launch (start us, length us, event | category | flops | bytes accessed | tf_op | source)
XLA Modules:
  0.0 116.4 jit_solution(2154007380758100170)
XLA Ops:
  1.6 1.0 pad_maximum_fusion.own
  2.6 7.8 %collective-permute-start.2 = (bf16[384,512]{1,0:T(8,128)(2,1)S(1)}, bf16[384,512]{1,0:T(8,128)(2,1)S(1)}, u32[]{:S(2)}, u32[]{:S(2)}) collective-permute-start(bf16[384,512]{1,0:T(8,128)(2,1)S(1)} %pad_maximum_fusion.own), channel_id=1, source_target_pairs={{0,3},{1,0},{2,1},{3,2},{4,7},{5,4},{6,5},{7,6},{8,11},{9,8},{10,9... | collective-permute-start | bytes 1179656 | tf_op jit(solution)/shard_map/ppermute | solution.py:120
  10.4 1.9 %collective-permute-start.1 = (bf16[384,512]{1,0:T(8,128)(2,1)S(1)}, bf16[384,512]{1,0:T(8,128)(2,1)S(1)}, u32[]{:S(2)}, u32[]{:S(2)}) collective-permute-start(bf16[384,512]{1,0:T(8,128)(2,1)S(1)} %pad_maximum_fusion.own), channel_id=1, source_target_pairs={{0,1},{1,2},{2,3},{3,0},{4,5},{5,6},{6,7},{7,4},{8,9},{9,10},{10,1... | collective-permute-start | bytes 1179656 | tf_op jit(solution)/shard_map/ppermute | solution.py:120
  13.4 1.2 %reshape_squeeze.11 = bf16[32,4,4,4,32]{4,3,2,1,0:T(4,128)(2,1)S(1)} reshape(bf16[1,32,4,512]{3,2,1,0:T(4,128)(2,1)} %param.7) | data formatting | bytes 262144 | tf_op jit(solution)/shard_map/reshape;squeeze | solution.py:137
  16.2 1.2 %fusion = bf16[8,4,4,4,4,8]{5,0,1,3,2,4:T(8,128)(2,1)S(1)} fusion(bf16[8,8,4,4,1,1]{1,3,2,0,5,4:T(4,128)(2,1)} %bitcast.49), kind=kOutput, calls=%fused_computation.6 | convolution fusion | flops 278528 | bytes 34816 | tf_op jit(solution)/shard_map/mnsu,nkvw->kuwsvm/dot_general | solution.py:135
  18.8 1.3 %collective-permute-done.1.near = bf16[384,512]{1,0:T(8,128)(2,1)S(1)} collective-permute-done((bf16[384,512]{1,0:T(8,128)(2,1)S(1)}, bf16[384,512]{1,0:T(8,128)(2,1)S(1)}, u32[]{:S(2)}, u32[]{:S(2)}) %collective-permute-start.1) | collective-permute-done | bytes 393248 | tf_op jit(solution)/shard_map/ppermute | solution.py:120
  20.6 1.1 broadcast_in_dim.26
  21.8 4.7 %all-to-all-start = ((bf16[4,32,4096]{2,1,0:T(8,128)(2,1)}), bf16[4,32,4096]{2,1,0:T(8,128)(2,1)S(1)}, u32[]{:S(2)}, u32[]{:S(2)}) async-start(bf16[4,32,4096]{2,1,0:T(8,128)(2,1)} %bitcast.3), calls=%async_computation | async-start | bytes 2097152 | tf_op jit(solution)/shard_map/all_to_all | solution.py:133
  26.6 1.8 %constant_dynamic-slice_fusion = bf16[1,8,256,512]{3,2,1,0:T(8,128)(2,1)S(1)} fusion(bf16[1,8,512,512]{3,2,1,0:T(8,128)(2,1)} %param.9, s32[]{:T(128)S(6)} %select_n.105), kind=kLoop, calls=%fused_computation.48 | loop fusion | bytes 4194308 | tf_op jit(solution)/shard_map/dynamic_slice | solution.py:142
  29.3 6.6 %all-to-all-done = bf16[4,32,4096]{2,1,0:T(8,128)(2,1)S(1)} async-done(((bf16[4,32,4096]{2,1,0:T(8,128)(2,1)}), bf16[4,32,4096]{2,1,0:T(8,128)(2,1)S(1)}, u32[]{:S(2)}, u32[]{:S(2)}) %all-to-all-start) | async-done | bytes 1048608 | tf_op jit(solution)/shard_map/all_to_all | solution.py:133
  35.9 5.4 %all-to-all-start.1 = ((bf16[16,4,32,128]{3,2,1,0:T(8,128)(2,1)}), bf16[16,4,32,128]{3,2,1,0:T(8,128)(2,1)}, u32[]{:S(2)}, u32[]{:S(2)}) async-start(bf16[16,4,32,128]{3,2,1,0:T(8,128)(2,1)} %bitcast.46), calls=%async_computation.1 | async-start | bytes 1048576 | tf_op jit(solution)/shard_map/all_to_all | solution.py:151
  41.3 4.0 %collective-permute-start.3 = (bf16[384,512]{1,0:T(8,128)(2,1)}, bf16[384,512]{1,0:T(8,128)(2,1)}, u32[]{:S(2)}, u32[]{:S(2)}) collective-permute-start(bf16[384,512]{1,0:T(8,128)(2,1)} %copy-done.1), channel_id=1, source_target_pairs={{0,2},{1,3},{2,0},{3,1},{4,6},{5,7},{6,4},{7,5},{8,10},{9,11},{10,... | collective-permute-start | bytes 1179656 | tf_op jit(solution)/shard_map/ppermute | solution.py:120
  45.3 4.7 %collective-permute-start.7 = (bf16[128,4096]{1,0:T(8,128)(2,1)S(1)}, bf16[128,4096]{1,0:T(8,128)(2,1)}, u32[]{:S(2)}, u32[]{:S(2)}) collective-permute-start(bf16[128,4096]{1,0:T(8,128)(2,1)S(1)} %bitcast.41), channel_id=1, source_target_pairs={{0,12},{1,13},{2,14},{3,15},{4,0},{5,1},{6,2},{7,3},{8,4},{9,5},{1... | collective-permute-start | bytes 3145736 | tf_op jit(solution)/shard_map/ppermute | solution.py:120
  50.0 1.9 %collective-permute-start.6 = (bf16[128,4096]{1,0:T(8,128)(2,1)S(1)}, bf16[128,4096]{1,0:T(8,128)(2,1)}, u32[]{:S(2)}, u32[]{:S(2)}) collective-permute-start(bf16[128,4096]{1,0:T(8,128)(2,1)S(1)} %bitcast.42), channel_id=1, source_target_pairs={{0,4},{1,5},{2,6},{3,7},{4,8},{5,9},{6,10},{7,11},{8,12},{9,13},{1... | collective-permute-start | bytes 3145736 | tf_op jit(solution)/shard_map/ppermute | solution.py:120
  51.9 4.8 %collective-permute-done.3.far = bf16[384,512]{1,0:T(8,128)(2,1)} collective-permute-done((bf16[384,512]{1,0:T(8,128)(2,1)}, bf16[384,512]{1,0:T(8,128)(2,1)}, u32[]{:S(2)}, u32[]{:S(2)}) %collective-permute-start.3) | collective-permute-done | bytes 393248 | tf_op jit(solution)/shard_map/ppermute | solution.py:120
  56.7 5.0 %front.1 = bf16[16,8,32,128]{3,2,1,0:T(8,128)(2,1)} custom-call(bf16[384,512]{1,0:T(8,128)(2,1)} %copy-done.1, bf16[384,512]{1,0:T(8,128)(2,1)} %copy-done.3, bf16[384,512]{1,0:T(8,128)(2,1)} %copy-done.2, bf16[384,512]{1,0:T(8,128)(2,1)} %collective-permute-done.3.far, bf16[16,4,32,128]{3,2,1,0:T(8,128)(2,1)} %all-to-all-done.1.cols, ...), custom_call_target="tpu_custom_call" | custom-call | flops 2000000000 | bytes 4000000 | tf_op jit(solution)/shard_map/front/pallas_call | solution.py:152
  61.7 8.2 %all-to-all-start.2 = ((bf16[16,8,32,128]{3,2,1,0:T(8,128)(2,1)}), bf16[16,8,32,128]{3,2,1,0:T(8,128)(2,1)}, u32[]{:S(2)}, u32[]{:S(2)}) async-start(bf16[16,8,32,128]{3,2,1,0:T(8,128)(2,1)} %front.1), calls=%async_computation.2 | async-start | bytes 2097152 | tf_op jit(solution)/shard_map/all_to_all | solution.py:168
  69.9 2.0 %fusion.8 = bf16[512,512]{1,0:T(8,128)(2,1)} fusion(s32[512]{0:T(512)S(1)} %get-tuple-element.30, s32[512]{0:T(512)S(1)} %get-tuple-element.31, s32[512]{0:T(512)S(1)} %get-tuple-element.28, s32[512]{0:T(512)S(1)} %get-tuple-element.34, s32[512]{0:T(512)S(1)} %get-tuple-element.29, s32[512]{0:T(512)S(1)} %get-tuple-element.35, ...), kind=kLoop, calls=%fused_computation.17 | loop fusion | flops 5505024 | bytes 538113 | tf_op jit(solution)/shard_map/convert_element_type | solution.py:176
  72.0 1.9 %slice.29 = bf16[64,4096]{1,0:T(8,128)(2,1)} slice(bf16[128,4096]{1,0:T(8,128)(2,1)} %collective-permute-done.7.down), slice={[64:128], [0:4096]} | slice | bytes 1048576 | tf_op jit(solution)/shard_map/slice | solution.py:149
  73.8 4.6 %collective-permute-start.9 = (bf16[64,4096]{1,0:T(8,128)(2,1)}, bf16[64,4096]{1,0:T(8,128)(2,1)}, u32[]{:S(2)}, u32[]{:S(2)}) collective-permute-start(bf16[64,4096]{1,0:T(8,128)(2,1)} %slice.29), channel_id=1, source_target_pairs={{0,12},{1,13},{2,14},{3,15},{4,0},{5,1},{6,2},{7,3},{8,4},{9,5},{1... | collective-permute-start | bytes 1572872 | tf_op jit(solution)/shard_map/ppermute | solution.py:120
  78.4 1.9 %slice.28 = bf16[64,4096]{1,0:T(8,128)(2,1)} slice(bf16[128,4096]{1,0:T(8,128)(2,1)} %collective-permute-done.6.up), slice={[0:64], [0:4096]} | slice | bytes 1048576 | tf_op jit(solution)/shard_map/slice | solution.py:148
  80.3 1.9 %collective-permute-start.8 = (bf16[64,4096]{1,0:T(8,128)(2,1)}, bf16[64,4096]{1,0:T(8,128)(2,1)}, u32[]{:S(2)}, u32[]{:S(2)}) collective-permute-start(bf16[64,4096]{1,0:T(8,128)(2,1)} %slice.28), channel_id=1, source_target_pairs={{0,4},{1,5},{2,6},{3,7},{4,8},{5,9},{6,10},{7,11},{8,12},{9,13},{1... | collective-permute-start | bytes 1572872 | tf_op jit(solution)/shard_map/ppermute | solution.py:120
  82.2 5.0 %all-to-all-done.2 = bf16[16,8,32,128]{3,2,1,0:T(8,128)(2,1)} async-done(((bf16[16,8,32,128]{3,2,1,0:T(8,128)(2,1)}), bf16[16,8,32,128]{3,2,1,0:T(8,128)(2,1)}, u32[]{:S(2)}, u32[]{:S(2)}) %all-to-all-start.2) | async-done | bytes 1048608 | tf_op jit(solution)/shard_map/all_to_all | solution.py:168
  87.2 2.1 %bitcast_select_fusion = bf16[4,4,8,32,128]{4,2,1,3,0:T(8,128)(2,1)S(1)} fusion(bf16[4,4,8,32,128]{4,3,2,1,0:T(8,128)(2,1)} %bitcast.13, pred[]{:T(512)S(6)} %eq.16), kind=kLoop, calls=%fused_computation.15 | loop fusion | flops 524288 | bytes 2097153 | tf_op jit(solution)/shard_map/jit(_where)/select_n | solution.py:169
  89.5 2.1 %collective-permute-start.5 = (bf16[256,512]{1,0:T(8,128)(2,1)S(1)}, bf16[256,512]{1,0:T(8,128)(2,1)S(1)}, u32[]{:S(2)}, u32[]{:S(2)}) collective-permute-start(bf16[256,512]{1,0:T(8,128)(2,1)S(1)} %fusion.9), channel_id=1, source_target_pairs={{0,20},{1,21},{2,22},{3,23},{4,16},{5,17},{6,18},{7,19},{8,28},{9,... | collective-permute-start | bytes 786440 | tf_op jit(solution)/shard_map/ppermute | solution.py:120
  91.6 1.3 %collective-permute-done.8.far_a = bf16[64,4096]{1,0:T(8,128)(2,1)} collective-permute-done((bf16[64,4096]{1,0:T(8,128)(2,1)}, bf16[64,4096]{1,0:T(8,128)(2,1)}, u32[]{:S(2)}, u32[]{:S(2)}) %collective-permute-start.8) | collective-permute-done | bytes 524320 | tf_op jit(solution)/shard_map/ppermute | solution.py:120
  92.9 6.6 %collective-permute-done.5.left = bf16[256,512]{1,0:T(8,128)(2,1)S(1)} collective-permute-done((bf16[256,512]{1,0:T(8,128)(2,1)S(1)}, bf16[256,512]{1,0:T(8,128)(2,1)S(1)}, u32[]{:S(2)}, u32[]{:S(2)}) %collective-permute-start.5) | collective-permute-done | bytes 262176 | tf_op jit(solution)/shard_map/ppermute | solution.py:120
  99.5 4.8 %back.2 = bf16[512,512]{1,0:T(8,128)(2,1)S(1)} custom-call(s32[4]{0:T(128)S(1)} %fusion.22.offsets, bf16[256,512]{1,0:T(8,128)(2,1)S(1)} %collective-permute-done.5.left, bf16[128,4096]{1,0:T(8,128)(2,1)S(1)} %bitcast.43, bf16[128,4096]{1,0:T(8,128)(2,1)} %collective-permute-done.6.up, bf16[128,4096]{1,0:T(8,128)(2,1)} %collective-permute-done.7.down, ...), custom_call_target="tpu_custom_call" | custom-call | flops 2500000000 | bytes 8000000 | tf_op jit(solution)/shard_map/back/pallas_call | solution.py:99
  104.3 2.1 %collective-permute-start.10 = (bf16[512,512]{1,0:T(8,128)(2,1)S(1)}, bf16[512,512]{1,0:T(8,128)(2,1)S(1)}, u32[]{:S(2)}, u32[]{:S(2)}) collective-permute-start(bf16[512,512]{1,0:T(8,128)(2,1)S(1)} %back.2), channel_id=1, source_target_pairs={{0,1},{1,0},{2,3},{3,2},{4,5},{5,4},{6,7},{7,6},{8,9},{9,8},{10,11... | collective-permute-start | bytes 1572872 | tf_op jit(solution)/shard_map/ppermute | solution.py:120
  106.4 1.0 fusion.1
  107.4 4.8 %back.3 = bf16[512,512]{1,0:T(8,128)(2,1)S(1)} custom-call(s32[4]{0:T(128)S(1)} %fusion.22.offsets, bf16[256,512]{1,0:T(8,128)(2,1)S(1)} %collective-permute-done.4.left, bf16[128,4096]{1,0:T(8,128)(2,1)S(1)} %bitcast.44, bf16[128,4096]{1,0:T(8,128)(2,1)} %collective-permute-done.6.up, bf16[128,4096]{1,0:T(8,128)(2,1)} %collective-permute-done.7.down, ...), custom_call_target="tpu_custom_call" | custom-call | flops 2500000000 | bytes 8000000 | tf_op jit(solution)/shard_map/back/pallas_call | solution.py:99
  112.3 3.1 %collective-permute-done.10 = bf16[512,512]{1,0:T(8,128)(2,1)S(1)} collective-permute-done((bf16[512,512]{1,0:T(8,128)(2,1)S(1)}, bf16[512,512]{1,0:T(8,128)(2,1)S(1)}, u32[]{:S(2)}, u32[]{:S(2)}) %collective-permute-start.10) | collective-permute-done | bytes 524320 | tf_op jit(solution)/shard_map/ppermute | solution.py:120
  (42 shorter events, 7.6 us)
Async XLA Ops:
  0.6 19.5 %collective-permute-start = (bf16[32,4,4,512]{3,2,1,0:T(4,128)(2,1)}, bf16[32,4,4,512]{3,2,1,0:T(4,128)(2,1)S(1)}, u32[]{:S(2)}, u32[]{:S(2)}) collective-permute-start(bf16[32,4,4,512]{3,2,1,0:T(4,128)(2,1)} %bitcast.51), channel_id=1, source_target_pairs={{0,16},{1,17},{2,18},{3,19},{4,20},{5,21},{6,22},{7,23},{8,24},{9,... | collective-permute-start | bytes 1572872 | tf_op jit(solution)/shard_map/ppermute | solution.py:120
  2.6 24.0 %copy-start.1 = (bf16[384,512]{1,0:T(8,128)(2,1)}, bf16[384,512]{1,0:T(8,128)(2,1)S(1)}, u32[]{:S(2)}) copy-start(bf16[384,512]{1,0:T(8,128)(2,1)S(1)} %pad_maximum_fusion.own) | copy-start | bytes 1179652
  2.6 16.2 %collective-permute-start.2 = (bf16[384,512]{1,0:T(8,128)(2,1)S(1)}, bf16[384,512]{1,0:T(8,128)(2,1)S(1)}, u32[]{:S(2)}, u32[]{:S(2)}) collective-permute-start(bf16[384,512]{1,0:T(8,128)(2,1)S(1)} %pad_maximum_fusion.own), channel_id=1, source_target_pairs={{0,3},{1,0},{2,1},{3,2},{4,7},{5,4},{6,5},{7,6},{8,11},{9,8},{10,9... | collective-permute-start | bytes 1179656 | tf_op jit(solution)/shard_map/ppermute | solution.py:120
  10.4 9.7 %collective-permute-start.1 = (bf16[384,512]{1,0:T(8,128)(2,1)S(1)}, bf16[384,512]{1,0:T(8,128)(2,1)S(1)}, u32[]{:S(2)}, u32[]{:S(2)}) collective-permute-start(bf16[384,512]{1,0:T(8,128)(2,1)S(1)} %pad_maximum_fusion.own), channel_id=1, source_target_pairs={{0,1},{1,2},{2,3},{3,0},{4,5},{5,6},{6,7},{7,4},{8,9},{9,10},{10,1... | collective-permute-start | bytes 1179656 | tf_op jit(solution)/shard_map/ppermute | solution.py:120
  18.8 7.8 %copy-start.2 = (bf16[384,512]{1,0:T(8,128)(2,1)}, bf16[384,512]{1,0:T(8,128)(2,1)S(1)}, u32[]{:S(2)}) copy-start(bf16[384,512]{1,0:T(8,128)(2,1)S(1)} %collective-permute-done.2.back_) | copy-start | bytes 1179652
  20.1 6.5 %copy-start.3 = (bf16[384,512]{1,0:T(8,128)(2,1)}, bf16[384,512]{1,0:T(8,128)(2,1)S(1)}, u32[]{:S(2)}) copy-start(bf16[384,512]{1,0:T(8,128)(2,1)S(1)} %collective-permute-done.1.near) | copy-start | bytes 1179652
  20.6 7.8 %copy-start.4 = (s32[4]{0:T(128)S(1)}, s32[4]{0:T(128)}, u32[]{:S(2)}) copy-start(s32[4]{0:T(128)} %constant.118.clone) | copy-start | bytes 52
  21.8 14.1 %all-to-all-start = ((bf16[4,32,4096]{2,1,0:T(8,128)(2,1)}), bf16[4,32,4096]{2,1,0:T(8,128)(2,1)S(1)}, u32[]{:S(2)}, u32[]{:S(2)}) async-start(bf16[4,32,4096]{2,1,0:T(8,128)(2,1)} %bitcast.3), calls=%async_computation | async-start | bytes 2097152 | tf_op jit(solution)/shard_map/all_to_all | solution.py:133
  35.9 20.8 %all-to-all-start.1 = ((bf16[16,4,32,128]{3,2,1,0:T(8,128)(2,1)}), bf16[16,4,32,128]{3,2,1,0:T(8,128)(2,1)}, u32[]{:S(2)}, u32[]{:S(2)}) async-start(bf16[16,4,32,128]{3,2,1,0:T(8,128)(2,1)} %bitcast.46), calls=%async_computation.1 | async-start | bytes 1048576 | tf_op jit(solution)/shard_map/all_to_all | solution.py:151
  41.3 15.4 %collective-permute-start.3 = (bf16[384,512]{1,0:T(8,128)(2,1)}, bf16[384,512]{1,0:T(8,128)(2,1)}, u32[]{:S(2)}, u32[]{:S(2)}) collective-permute-start(bf16[384,512]{1,0:T(8,128)(2,1)} %copy-done.1), channel_id=1, source_target_pairs={{0,2},{1,3},{2,0},{3,1},{4,6},{5,7},{6,4},{7,5},{8,10},{9,11},{10,... | collective-permute-start | bytes 1179656 | tf_op jit(solution)/shard_map/ppermute | solution.py:120
  45.3 26.6 %collective-permute-start.7 = (bf16[128,4096]{1,0:T(8,128)(2,1)S(1)}, bf16[128,4096]{1,0:T(8,128)(2,1)}, u32[]{:S(2)}, u32[]{:S(2)}) collective-permute-start(bf16[128,4096]{1,0:T(8,128)(2,1)S(1)} %bitcast.41), channel_id=1, source_target_pairs={{0,12},{1,13},{2,14},{3,15},{4,0},{5,1},{6,2},{7,3},{8,4},{9,5},{1... | collective-permute-start | bytes 3145736 | tf_op jit(solution)/shard_map/ppermute | solution.py:120
  50.0 28.4 %collective-permute-start.6 = (bf16[128,4096]{1,0:T(8,128)(2,1)S(1)}, bf16[128,4096]{1,0:T(8,128)(2,1)}, u32[]{:S(2)}, u32[]{:S(2)}) collective-permute-start(bf16[128,4096]{1,0:T(8,128)(2,1)S(1)} %bitcast.42), channel_id=1, source_target_pairs={{0,4},{1,5},{2,6},{3,7},{4,8},{5,9},{6,10},{7,11},{8,12},{9,13},{1... | collective-permute-start | bytes 3145736 | tf_op jit(solution)/shard_map/ppermute | solution.py:120
  61.7 25.6 %all-to-all-start.2 = ((bf16[16,8,32,128]{3,2,1,0:T(8,128)(2,1)}), bf16[16,8,32,128]{3,2,1,0:T(8,128)(2,1)}, u32[]{:S(2)}, u32[]{:S(2)}) async-start(bf16[16,8,32,128]{3,2,1,0:T(8,128)(2,1)} %front.1), calls=%async_computation.2 | async-start | bytes 2097152 | tf_op jit(solution)/shard_map/all_to_all | solution.py:168
  73.8 17.8 %collective-permute-start.9 = (bf16[64,4096]{1,0:T(8,128)(2,1)}, bf16[64,4096]{1,0:T(8,128)(2,1)}, u32[]{:S(2)}, u32[]{:S(2)}) collective-permute-start(bf16[64,4096]{1,0:T(8,128)(2,1)} %slice.29), channel_id=1, source_target_pairs={{0,12},{1,13},{2,14},{3,15},{4,0},{5,1},{6,2},{7,3},{8,4},{9,5},{1... | collective-permute-start | bytes 1572872 | tf_op jit(solution)/shard_map/ppermute | solution.py:120
  80.3 12.6 %collective-permute-start.8 = (bf16[64,4096]{1,0:T(8,128)(2,1)}, bf16[64,4096]{1,0:T(8,128)(2,1)}, u32[]{:S(2)}, u32[]{:S(2)}) collective-permute-start(bf16[64,4096]{1,0:T(8,128)(2,1)} %slice.28), channel_id=1, source_target_pairs={{0,4},{1,5},{2,6},{3,7},{4,8},{5,9},{6,10},{7,11},{8,12},{9,13},{1... | collective-permute-start | bytes 1572872 | tf_op jit(solution)/shard_map/ppermute | solution.py:120
  89.5 16.9 %copy-start = (bf16[512,512]{1,0:T(8,128)(2,1)S(1)}, bf16[512,512]{1,0:T(8,128)(2,1)}, u32[]{:S(2)}) copy-start(bf16[512,512]{1,0:T(8,128)(2,1)} %fusion.8) | copy-start | bytes 1572868
  89.5 9.9 %collective-permute-start.5 = (bf16[256,512]{1,0:T(8,128)(2,1)S(1)}, bf16[256,512]{1,0:T(8,128)(2,1)S(1)}, u32[]{:S(2)}, u32[]{:S(2)}) collective-permute-start(bf16[256,512]{1,0:T(8,128)(2,1)S(1)} %fusion.9), channel_id=1, source_target_pairs={{0,20},{1,21},{2,22},{3,23},{4,16},{5,17},{6,18},{7,19},{8,28},{9,... | collective-permute-start | bytes 786440 | tf_op jit(solution)/shard_map/ppermute | solution.py:120
  91.6 12.7 %collective-permute-start.4 = (bf16[256,512]{1,0:T(8,128)(2,1)S(1)}, bf16[256,512]{1,0:T(8,128)(2,1)S(1)}, u32[]{:S(2)}, u32[]{:S(2)}) collective-permute-start(bf16[256,512]{1,0:T(8,128)(2,1)S(1)} %fusion.9), channel_id=1, source_target_pairs={{0,16},{1,17},{2,18},{3,19},{4,20},{5,21},{6,22},{7,23},{8,24},{9,... | collective-permute-start | bytes 786440 | tf_op jit(solution)/shard_map/ppermute | solution.py:120
  104.3 11.1 %collective-permute-start.10 = (bf16[512,512]{1,0:T(8,128)(2,1)S(1)}, bf16[512,512]{1,0:T(8,128)(2,1)S(1)}, u32[]{:S(2)}, u32[]{:S(2)}) collective-permute-start(bf16[512,512]{1,0:T(8,128)(2,1)S(1)} %back.2), channel_id=1, source_target_pairs={{0,1},{1,0},{2,3},{3,2},{4,5},{5,4},{6,7},{7,6},{8,9},{9,8},{10,11... | collective-permute-start | bytes 1572872 | tf_op jit(solution)/shard_map/ppermute | solution.py:120

commit v9 on v8

--- a/solution.py
+++ b/solution.py
@@ -140,8 +140,8 @@
     cols = jnp.where(odd, quarters[:, None], quarters[None]).reshape(16, 4, 32, 128)
     offsets = (row + jnp.array([0, 3, 1, 2], jnp.int32)) % LINE * 128
     right = lax.dynamic_slice_in_dim(right_env[0], column % 2 * 256, 256, 1).reshape(2048, chi)
-    pair, local, two_site, cols, offsets, right = lax.optimization_barrier(
-        (pair, local, two_site, cols, offsets, right)
+    pair, blocks[3], local, two_site, cols, offsets, right = lax.optimization_barrier(
+        (pair, blocks[3], local, two_site, cols, offsets, right)
     )
     up = moved(pair, along_column(1))
     down = moved(pair, along_column(-1))

time: 118 us -> 114 us (0.966)
  starting transfers between devices: 49.3 us -> 46 us
    ppermute x11, waiting for transfers between devices: 17 us -> 11 us  [moved(): return lax.ppermute(block, ('sec', 'bond'), routed(sections, step, ahead))]
    all_to_all x1, waiting for transfers between devices: 0.01 us -> 5.18 us  [shards(): cols = lax.all_to_all(cols, 'bond', 0, 0, tiled=True)]
    all_to_all x1, starting transfers between devices: 8.19 us -> 4.77 us  [shards(): lax.all_to_all(fresh, 'bond', 0, 0, tiled=True).reshape(4, 4, 8, 32, 128)]
  transfers between devices with their start and end apart: 14 -> 14, of which waited for: 7 -> 6; matrix products, arithmetic and copies ran while one was open for 17% -> 20% of each run, Pallas kernels for 13% -> 13%
where the time goes in v9:
time: 114 us; the launch traced here: 113 us
  starting transfers between devices  46 us (40%)
  waiting for transfers between devices  27.8 us (24%)
  Pallas kernels  14.6 us (13%)
  local copies, waits for them, and re-layouts  14.2 us (12%)
  other arithmetic  7.13 us (6%)
  matrix products  2.19 us (2%)
    ppermute x11, starting transfers between devices, moved(): return lax.ppermute(block, ('sec', 'bond'), routed(sections, step, ahead))  31 us
    ppermute x11, waiting for transfers between devices, moved(): return lax.ppermute(block, ('sec', 'bond'), routed(sections, step, ahead))  11 us
    pallas_call x2, Pallas kernels, applied(): pl.pallas_call(back, out_shape=jax.ShapeDtypeStruct((512, 512), BF), in_s...  9.66 us
    all_to_all x1, waiting for transfers between devices, shards(): lax.all_to_all(send, ('sec', 'bond'), 0, 0, axis_index_groups=lines, tile...  6.68 us
    all_to_all x1, starting transfers between devices, shards(): cols = lax.all_to_all(cols, 'bond', 0, 0, tiled=True)  5.56 us
    all_to_all x1, waiting for transfers between devices, shards(): cols = lax.all_to_all(cols, 'bond', 0, 0, tiled=True)  5.18 us
    all_to_all x1, waiting for transfers between devices, shards(): lax.all_to_all(fresh, 'bond', 0, 0, tiled=True).reshape(4, 4, 8, 32, 128)  4.96 us
    pallas_call x1, Pallas kernels, shards(): pl.pallas_call(front, out_shape=jax.ShapeDtypeStruct((16, 8, 32, 128), BF...  4.96 us
  transfers between devices with their start and end apart: 14, of which 6 were waited for; matrix products, arithmetic and copies ran while one was open for 20% of the time, Pallas kernels for 13%

profile of v9, /device:TPU:2, one launch (start us, length us, event | category | flops | bytes accessed | tf_op | source)
XLA Modules:
  0.0 113.0 jit_solution(6994590607786365968)
XLA Ops:
  1.6 1.7 %pad_maximum_fusion.own = bf16[384,512]{1,0:T(8,128)(2,1)} fusion(bf16[128,512]{1,0:T(8,128)(2,1)S(1)} %reshape_squeeze.10, bf16[256,512]{1,0:T(8,128)(2,1)} %bitcast.50), kind=kLoop, calls=%fused_computation.22 | loop fusion | flops 786432 | bytes 786432 | tf_op jit(solution)/shard_map/concatenate | solution.py:127
  3.3 7.8 %collective-permute-start.2 = (bf16[384,512]{1,0:T(8,128)(2,1)}, bf16[384,512]{1,0:T(8,128)(2,1)S(1)}, u32[]{:S(2)}, u32[]{:S(2)}) collective-permute-start(bf16[384,512]{1,0:T(8,128)(2,1)} %pad_maximum_fusion.own), channel_id=1, source_target_pairs={{0,3},{1,0},{2,1},{3,2},{4,7},{5,4},{6,5},{7,6},{8,11},{9,8},{10,9... | collective-permute-start | bytes 1179656 | tf_op jit(solution)/shard_map/ppermute | solution.py:120
  11.1 1.9 %collective-permute-start.1 = (bf16[384,512]{1,0:T(8,128)(2,1)}, bf16[384,512]{1,0:T(8,128)(2,1)S(1)}, u32[]{:S(2)}, u32[]{:S(2)}) collective-permute-start(bf16[384,512]{1,0:T(8,128)(2,1)} %pad_maximum_fusion.own), channel_id=1, source_target_pairs={{0,1},{1,2},{2,3},{3,0},{4,5},{5,6},{6,7},{7,4},{8,9},{9,10},{10,1... | collective-permute-start | bytes 1179656 | tf_op jit(solution)/shard_map/ppermute | solution.py:120
  13.1 4.0 %collective-permute-start.3 = (bf16[384,512]{1,0:T(8,128)(2,1)}, bf16[384,512]{1,0:T(8,128)(2,1)}, u32[]{:S(2)}, u32[]{:S(2)}) collective-permute-start(bf16[384,512]{1,0:T(8,128)(2,1)} %pad_maximum_fusion.own), channel_id=1, source_target_pairs={{0,2},{1,3},{2,0},{3,1},{4,6},{5,7},{6,4},{7,5},{8,10},{9,11},{10,... | collective-permute-start | bytes 1179656 | tf_op jit(solution)/shard_map/ppermute | solution.py:120
  17.1 1.0 reshape.67
  18.1 1.2 %reshape_squeeze.11 = bf16[32,4,4,4,32]{4,3,2,1,0:T(4,128)(2,1)S(1)} reshape(bf16[1,32,4,512]{3,2,1,0:T(4,128)(2,1)} %param.7) | data formatting | bytes 262144 | tf_op jit(solution)/shard_map/reshape;squeeze | solution.py:137
  20.9 1.2 %fusion = bf16[8,4,4,4,4,8]{5,0,1,3,2,4:T(8,128)(2,1)S(1)} fusion(bf16[8,8,4,4,1,1]{1,3,2,0,5,4:T(4,128)(2,1)} %bitcast.49), kind=kOutput, calls=%fused_computation.6 | convolution fusion | flops 278528 | bytes 34816 | tf_op jit(solution)/shard_map/mnsu,nkvw->kuwsvm/dot_general | solution.py:135
  24.1 1.1 broadcast_in_dim.26
  25.2 4.7 %all-to-all-start = ((bf16[4,32,4096]{2,1,0:T(8,128)(2,1)}), bf16[4,32,4096]{2,1,0:T(8,128)(2,1)S(1)}, u32[]{:S(2)}, u32[]{:S(2)}) async-start(bf16[4,32,4096]{2,1,0:T(8,128)(2,1)} %bitcast.3), calls=%async_computation | async-start | bytes 2097152 | tf_op jit(solution)/shard_map/all_to_all | solution.py:133
  30.1 1.7 %constant_dynamic-slice_fusion = bf16[1,8,256,512]{3,2,1,0:T(8,128)(2,1)S(1)} fusion(bf16[1,8,512,512]{3,2,1,0:T(8,128)(2,1)} %param.9, s32[]{:T(128)S(6)} %select_n.105), kind=kLoop, calls=%fused_computation.48 | loop fusion | bytes 4194308 | tf_op jit(solution)/shard_map/dynamic_slice | solution.py:142
  32.7 6.7 %all-to-all-done = bf16[4,32,4096]{2,1,0:T(8,128)(2,1)S(1)} async-done(((bf16[4,32,4096]{2,1,0:T(8,128)(2,1)}), bf16[4,32,4096]{2,1,0:T(8,128)(2,1)S(1)}, u32[]{:S(2)}, u32[]{:S(2)}) %all-to-all-start) | async-done | bytes 1048608 | tf_op jit(solution)/shard_map/all_to_all | solution.py:133
  39.4 5.6 %all-to-all-start.1 = ((bf16[16,4,32,128]{3,2,1,0:T(8,128)(2,1)}), bf16[16,4,32,128]{3,2,1,0:T(8,128)(2,1)}, u32[]{:S(2)}, u32[]{:S(2)}) async-start(bf16[16,4,32,128]{3,2,1,0:T(8,128)(2,1)} %bitcast.46), calls=%async_computation.1 | async-start | bytes 1048576 | tf_op jit(solution)/shard_map/all_to_all | solution.py:151
  44.9 4.6 %collective-permute-start.7 = (bf16[128,4096]{1,0:T(8,128)(2,1)S(1)}, bf16[128,4096]{1,0:T(8,128)(2,1)}, u32[]{:S(2)}, u32[]{:S(2)}) collective-permute-start(bf16[128,4096]{1,0:T(8,128)(2,1)S(1)} %bitcast.41), channel_id=1, source_target_pairs={{0,12},{1,13},{2,14},{3,15},{4,0},{5,1},{6,2},{7,3},{8,4},{9,5},{1... | collective-permute-start | bytes 3145736 | tf_op jit(solution)/shard_map/ppermute | solution.py:120
  49.5 1.9 %collective-permute-start.6 = (bf16[128,4096]{1,0:T(8,128)(2,1)S(1)}, bf16[128,4096]{1,0:T(8,128)(2,1)}, u32[]{:S(2)}, u32[]{:S(2)}) collective-permute-start(bf16[128,4096]{1,0:T(8,128)(2,1)S(1)} %bitcast.42), channel_id=1, source_target_pairs={{0,4},{1,5},{2,6},{3,7},{4,8},{5,9},{6,10},{7,11},{8,12},{9,13},{1... | collective-permute-start | bytes 3145736 | tf_op jit(solution)/shard_map/ppermute | solution.py:120
  51.4 5.2 %all-to-all-done.1.cols = bf16[16,4,32,128]{3,2,1,0:T(8,128)(2,1)} async-done(((bf16[16,4,32,128]{3,2,1,0:T(8,128)(2,1)}), bf16[16,4,32,128]{3,2,1,0:T(8,128)(2,1)}, u32[]{:S(2)}, u32[]{:S(2)}) %all-to-all-start.1) | async-done | bytes 524320 | tf_op jit(solution)/shard_map/all_to_all | solution.py:151
  56.6 5.0 %front.1 = bf16[16,8,32,128]{3,2,1,0:T(8,128)(2,1)} custom-call(bf16[384,512]{1,0:T(8,128)(2,1)} %pad_maximum_fusion.own, bf16[384,512]{1,0:T(8,128)(2,1)} %copy-done.2, bf16[384,512]{1,0:T(8,128)(2,1)} %copy-done.1, bf16[384,512]{1,0:T(8,128)(2,1)} %collective-permute-done.3.far, bf16[16,4,32,128]{3,2,1,0:T(8,128)(2,1)} %all-to-all-done.1.cols, ...), custom_call_target="tpu_custom_call" | custom-call | flops 2000000000 | bytes 4000000 | tf_op jit(solution)/shard_map/front/pallas_call | solution.py:152
  61.6 4.8 %all-to-all-start.2 = ((bf16[16,8,32,128]{3,2,1,0:T(8,128)(2,1)}), bf16[16,8,32,128]{3,2,1,0:T(8,128)(2,1)}, u32[]{:S(2)}, u32[]{:S(2)}) async-start(bf16[16,8,32,128]{3,2,1,0:T(8,128)(2,1)} %front.1), calls=%async_computation.2 | async-start | bytes 2097152 | tf_op jit(solution)/shard_map/all_to_all | solution.py:168
  66.4 2.0 %fusion.8 = bf16[512,512]{1,0:T(8,128)(2,1)} fusion(s32[512]{0:T(512)S(1)} %get-tuple-element.32, s32[512]{0:T(512)S(1)} %get-tuple-element.33, s32[512]{0:T(512)S(1)} %get-tuple-element.30, s32[512]{0:T(512)S(1)} %get-tuple-element.36, s32[512]{0:T(512)S(1)} %get-tuple-element.31, s32[512]{0:T(512)S(1)} %get-tuple-element.37, ...), kind=kLoop, calls=%fused_computation.17 | loop fusion | flops 5505024 | bytes 538113 | tf_op jit(solution)/shard_map/convert_element_type | solution.py:176
  68.5 1.9 %slice.29 = bf16[64,4096]{1,0:T(8,128)(2,1)} slice(bf16[128,4096]{1,0:T(8,128)(2,1)} %collective-permute-done.7.down), slice={[64:128], [0:4096]} | slice | bytes 1048576 | tf_op jit(solution)/shard_map/slice | solution.py:149
  70.3 4.7 %collective-permute-start.9 = (bf16[64,4096]{1,0:T(8,128)(2,1)}, bf16[64,4096]{1,0:T(8,128)(2,1)}, u32[]{:S(2)}, u32[]{:S(2)}) collective-permute-start(bf16[64,4096]{1,0:T(8,128)(2,1)} %slice.29), channel_id=1, source_target_pairs={{0,12},{1,13},{2,14},{3,15},{4,0},{5,1},{6,2},{7,3},{8,4},{9,5},{1... | collective-permute-start | bytes 1572872 | tf_op jit(solution)/shard_map/ppermute | solution.py:120
  75.0 1.9 %slice.28 = bf16[64,4096]{1,0:T(8,128)(2,1)} slice(bf16[128,4096]{1,0:T(8,128)(2,1)} %collective-permute-done.6.up), slice={[0:64], [0:4096]} | slice | bytes 1048576 | tf_op jit(solution)/shard_map/slice | solution.py:148
  76.9 1.9 %collective-permute-start.8 = (bf16[64,4096]{1,0:T(8,128)(2,1)}, bf16[64,4096]{1,0:T(8,128)(2,1)}, u32[]{:S(2)}, u32[]{:S(2)}) collective-permute-start(bf16[64,4096]{1,0:T(8,128)(2,1)} %slice.28), channel_id=1, source_target_pairs={{0,4},{1,5},{2,6},{3,7},{4,8},{5,9},{6,10},{7,11},{8,12},{9,13},{1... | collective-permute-start | bytes 1572872 | tf_op jit(solution)/shard_map/ppermute | solution.py:120
  78.8 5.0 %all-to-all-done.2 = bf16[16,8,32,128]{3,2,1,0:T(8,128)(2,1)} async-done(((bf16[16,8,32,128]{3,2,1,0:T(8,128)(2,1)}), bf16[16,8,32,128]{3,2,1,0:T(8,128)(2,1)}, u32[]{:S(2)}, u32[]{:S(2)}) %all-to-all-start.2) | async-done | bytes 1048608 | tf_op jit(solution)/shard_map/all_to_all | solution.py:168
  83.8 2.1 %bitcast_select_fusion = bf16[4,4,8,32,128]{4,2,1,3,0:T(8,128)(2,1)S(1)} fusion(bf16[4,4,8,32,128]{4,3,2,1,0:T(8,128)(2,1)} %bitcast.13, pred[]{:T(512)S(6)} %eq.16), kind=kLoop, calls=%fused_computation.15 | loop fusion | flops 524288 | bytes 2097153 | tf_op jit(solution)/shard_map/jit(_where)/select_n | solution.py:169
  86.1 2.1 %collective-permute-start.5 = (bf16[256,512]{1,0:T(8,128)(2,1)S(1)}, bf16[256,512]{1,0:T(8,128)(2,1)S(1)}, u32[]{:S(2)}, u32[]{:S(2)}) collective-permute-start(bf16[256,512]{1,0:T(8,128)(2,1)S(1)} %fusion.9), channel_id=1, source_target_pairs={{0,20},{1,21},{2,22},{3,23},{4,16},{5,17},{6,18},{7,19},{8,28},{9,... | collective-permute-start | bytes 786440 | tf_op jit(solution)/shard_map/ppermute | solution.py:120
  88.2 1.3 %collective-permute-done.8.far_a = bf16[64,4096]{1,0:T(8,128)(2,1)} collective-permute-done((bf16[64,4096]{1,0:T(8,128)(2,1)}, bf16[64,4096]{1,0:T(8,128)(2,1)}, u32[]{:S(2)}, u32[]{:S(2)}) %collective-permute-start.8) | collective-permute-done | bytes 524320 | tf_op jit(solution)/shard_map/ppermute | solution.py:120
  89.5 6.5 %collective-permute-done.5.left = bf16[256,512]{1,0:T(8,128)(2,1)S(1)} collective-permute-done((bf16[256,512]{1,0:T(8,128)(2,1)S(1)}, bf16[256,512]{1,0:T(8,128)(2,1)S(1)}, u32[]{:S(2)}, u32[]{:S(2)}) %collective-permute-start.5) | collective-permute-done | bytes 262176 | tf_op jit(solution)/shard_map/ppermute | solution.py:120
  96.0 4.8 %back.2 = bf16[512,512]{1,0:T(8,128)(2,1)S(1)} custom-call(s32[4]{0:T(128)S(1)} %fusion.22.offsets, bf16[256,512]{1,0:T(8,128)(2,1)S(1)} %collective-permute-done.5.left, bf16[128,4096]{1,0:T(8,128)(2,1)S(1)} %bitcast.43, bf16[128,4096]{1,0:T(8,128)(2,1)} %collective-permute-done.6.up, bf16[128,4096]{1,0:T(8,128)(2,1)} %collective-permute-done.7.down, ...), custom_call_target="tpu_custom_call" | custom-call | flops 2500000000 | bytes 8000000 | tf_op jit(solution)/shard_map/back/pallas_call | solution.py:99
  100.8 2.1 %collective-permute-start.10 = (bf16[512,512]{1,0:T(8,128)(2,1)S(1)}, bf16[512,512]{1,0:T(8,128)(2,1)S(1)}, u32[]{:S(2)}, u32[]{:S(2)}) collective-permute-start(bf16[512,512]{1,0:T(8,128)(2,1)S(1)} %back.2), channel_id=1, source_target_pairs={{0,1},{1,0},{2,3},{3,2},{4,5},{5,4},{6,7},{7,6},{8,9},{9,8},{10,11... | collective-permute-start | bytes 1572872 | tf_op jit(solution)/shard_map/ppermute | solution.py:120
  103.0 1.0 fusion.1
  104.0 4.8 %back.3 = bf16[512,512]{1,0:T(8,128)(2,1)S(1)} custom-call(s32[4]{0:T(128)S(1)} %fusion.22.offsets, bf16[256,512]{1,0:T(8,128)(2,1)S(1)} %collective-permute-done.4.left, bf16[128,4096]{1,0:T(8,128)(2,1)S(1)} %bitcast.44, bf16[128,4096]{1,0:T(8,128)(2,1)} %collective-permute-done.6.up, bf16[128,4096]{1,0:T(8,128)(2,1)} %collective-permute-done.7.down, ...), custom_call_target="tpu_custom_call" | custom-call | flops 2500000000 | bytes 8000000 | tf_op jit(solution)/shard_map/back/pallas_call | solution.py:99
  108.8 3.1 %collective-permute-done.10 = bf16[512,512]{1,0:T(8,128)(2,1)S(1)} collective-permute-done((bf16[512,512]{1,0:T(8,128)(2,1)S(1)}, bf16[512,512]{1,0:T(8,128)(2,1)S(1)}, u32[]{:S(2)}, u32[]{:S(2)}) %collective-permute-start.10) | collective-permute-done | bytes 524320 | tf_op jit(solution)/shard_map/ppermute | solution.py:120
  (40 shorter events, 6.7 us)
Async XLA Ops:
  0.6 22.9 %collective-permute-start = (bf16[32,4,4,512]{3,2,1,0:T(4,128)(2,1)}, bf16[32,4,4,512]{3,2,1,0:T(4,128)(2,1)S(1)}, u32[]{:S(2)}, u32[]{:S(2)}) collective-permute-start(bf16[32,4,4,512]{3,2,1,0:T(4,128)(2,1)} %bitcast.51), channel_id=1, source_target_pairs={{0,16},{1,17},{2,18},{3,19},{4,20},{5,21},{6,22},{7,23},{8,24},{9,... | collective-permute-start | bytes 1572872 | tf_op jit(solution)/shard_map/ppermute | solution.py:120
  3.3 20.2 %collective-permute-start.2 = (bf16[384,512]{1,0:T(8,128)(2,1)}, bf16[384,512]{1,0:T(8,128)(2,1)S(1)}, u32[]{:S(2)}, u32[]{:S(2)}) collective-permute-start(bf16[384,512]{1,0:T(8,128)(2,1)} %pad_maximum_fusion.own), channel_id=1, source_target_pairs={{0,3},{1,0},{2,1},{3,2},{4,7},{5,4},{6,5},{7,6},{8,11},{9,8},{10,9... | collective-permute-start | bytes 1179656 | tf_op jit(solution)/shard_map/ppermute | solution.py:120
  11.1 12.4 %collective-permute-start.1 = (bf16[384,512]{1,0:T(8,128)(2,1)}, bf16[384,512]{1,0:T(8,128)(2,1)S(1)}, u32[]{:S(2)}, u32[]{:S(2)}) collective-permute-start(bf16[384,512]{1,0:T(8,128)(2,1)} %pad_maximum_fusion.own), channel_id=1, source_target_pairs={{0,1},{1,2},{2,3},{3,0},{4,5},{5,6},{6,7},{7,4},{8,9},{9,10},{10,1... | collective-permute-start | bytes 1179656 | tf_op jit(solution)/shard_map/ppermute | solution.py:120
  13.1 19.6 %collective-permute-start.3 = (bf16[384,512]{1,0:T(8,128)(2,1)}, bf16[384,512]{1,0:T(8,128)(2,1)}, u32[]{:S(2)}, u32[]{:S(2)}) collective-permute-start(bf16[384,512]{1,0:T(8,128)(2,1)} %pad_maximum_fusion.own), channel_id=1, source_target_pairs={{0,2},{1,3},{2,0},{3,1},{4,6},{5,7},{6,4},{7,5},{8,10},{9,11},{10,... | collective-permute-start | bytes 1179656 | tf_op jit(solution)/shard_map/ppermute | solution.py:120
  23.2 6.9 %copy-start.3 = (s32[4]{0:T(128)S(1)}, s32[4]{0:T(128)}, u32[]{:S(2)}) copy-start(s32[4]{0:T(128)} %constant.118.clone) | copy-start | bytes 52
  23.5 6.5 %copy-start.1 = (bf16[384,512]{1,0:T(8,128)(2,1)}, bf16[384,512]{1,0:T(8,128)(2,1)S(1)}, u32[]{:S(2)}) copy-start(bf16[384,512]{1,0:T(8,128)(2,1)S(1)} %collective-permute-done.2.back_) | copy-start | bytes 1179652
  23.5 6.5 %copy-start.2 = (bf16[384,512]{1,0:T(8,128)(2,1)}, bf16[384,512]{1,0:T(8,128)(2,1)S(1)}, u32[]{:S(2)}) copy-start(bf16[384,512]{1,0:T(8,128)(2,1)S(1)} %collective-permute-done.1.near) | copy-start | bytes 1179652
  25.2 14.2 %all-to-all-start = ((bf16[4,32,4096]{2,1,0:T(8,128)(2,1)}), bf16[4,32,4096]{2,1,0:T(8,128)(2,1)S(1)}, u32[]{:S(2)}, u32[]{:S(2)}) async-start(bf16[4,32,4096]{2,1,0:T(8,128)(2,1)} %bitcast.3), calls=%async_computation | async-start | bytes 2097152 | tf_op jit(solution)/shard_map/all_to_all | solution.py:133
  39.4 17.2 %all-to-all-start.1 = ((bf16[16,4,32,128]{3,2,1,0:T(8,128)(2,1)}), bf16[16,4,32,128]{3,2,1,0:T(8,128)(2,1)}, u32[]{:S(2)}, u32[]{:S(2)}) async-start(bf16[16,4,32,128]{3,2,1,0:T(8,128)(2,1)} %bitcast.46), calls=%async_computation.1 | async-start | bytes 1048576 | tf_op jit(solution)/shard_map/all_to_all | solution.py:151
  44.9 23.5 %collective-permute-start.7 = (bf16[128,4096]{1,0:T(8,128)(2,1)S(1)}, bf16[128,4096]{1,0:T(8,128)(2,1)}, u32[]{:S(2)}, u32[]{:S(2)}) collective-permute-start(bf16[128,4096]{1,0:T(8,128)(2,1)S(1)} %bitcast.41), channel_id=1, source_target_pairs={{0,12},{1,13},{2,14},{3,15},{4,0},{5,1},{6,2},{7,3},{8,4},{9,5},{1... | collective-permute-start | bytes 3145736 | tf_op jit(solution)/shard_map/ppermute | solution.py:120
  49.5 25.5 %collective-permute-start.6 = (bf16[128,4096]{1,0:T(8,128)(2,1)S(1)}, bf16[128,4096]{1,0:T(8,128)(2,1)}, u32[]{:S(2)}, u32[]{:S(2)}) collective-permute-start(bf16[128,4096]{1,0:T(8,128)(2,1)S(1)} %bitcast.42), channel_id=1, source_target_pairs={{0,4},{1,5},{2,6},{3,7},{4,8},{5,9},{6,10},{7,11},{8,12},{9,13},{1... | collective-permute-start | bytes 3145736 | tf_op jit(solution)/shard_map/ppermute | solution.py:120
  61.6 22.2 %all-to-all-start.2 = ((bf16[16,8,32,128]{3,2,1,0:T(8,128)(2,1)}), bf16[16,8,32,128]{3,2,1,0:T(8,128)(2,1)}, u32[]{:S(2)}, u32[]{:S(2)}) async-start(bf16[16,8,32,128]{3,2,1,0:T(8,128)(2,1)} %front.1), calls=%async_computation.2 | async-start | bytes 2097152 | tf_op jit(solution)/shard_map/all_to_all | solution.py:168
  70.3 17.8 %collective-permute-start.9 = (bf16[64,4096]{1,0:T(8,128)(2,1)}, bf16[64,4096]{1,0:T(8,128)(2,1)}, u32[]{:S(2)}, u32[]{:S(2)}) collective-permute-start(bf16[64,4096]{1,0:T(8,128)(2,1)} %slice.29), channel_id=1, source_target_pairs={{0,12},{1,13},{2,14},{3,15},{4,0},{5,1},{6,2},{7,3},{8,4},{9,5},{1... | collective-permute-start | bytes 1572872 | tf_op jit(solution)/shard_map/ppermute | solution.py:120
  76.9 12.6 %collective-permute-start.8 = (bf16[64,4096]{1,0:T(8,128)(2,1)}, bf16[64,4096]{1,0:T(8,128)(2,1)}, u32[]{:S(2)}, u32[]{:S(2)}) collective-permute-start(bf16[64,4096]{1,0:T(8,128)(2,1)} %slice.28), channel_id=1, source_target_pairs={{0,4},{1,5},{2,6},{3,7},{4,8},{5,9},{6,10},{7,11},{8,12},{9,13},{1... | collective-permute-start | bytes 1572872 | tf_op jit(solution)/shard_map/ppermute | solution.py:120
  86.1 16.9 %copy-start = (bf16[512,512]{1,0:T(8,128)(2,1)S(1)}, bf16[512,512]{1,0:T(8,128)(2,1)}, u32[]{:S(2)}) copy-start(bf16[512,512]{1,0:T(8,128)(2,1)} %fusion.8) | copy-start | bytes 1572868
  86.1 9.9 %collective-permute-start.5 = (bf16[256,512]{1,0:T(8,128)(2,1)S(1)}, bf16[256,512]{1,0:T(8,128)(2,1)S(1)}, u32[]{:S(2)}, u32[]{:S(2)}) collective-permute-start(bf16[256,512]{1,0:T(8,128)(2,1)S(1)} %fusion.9), channel_id=1, source_target_pairs={{0,20},{1,21},{2,22},{3,23},{4,16},{5,17},{6,18},{7,19},{8,28},{9,... | collective-permute-start | bytes 786440 | tf_op jit(solution)/shard_map/ppermute | solution.py:120
  88.1 12.7 %collective-permute-start.4 = (bf16[256,512]{1,0:T(8,128)(2,1)S(1)}, bf16[256,512]{1,0:T(8,128)(2,1)S(1)}, u32[]{:S(2)}, u32[]{:S(2)}) collective-permute-start(bf16[256,512]{1,0:T(8,128)(2,1)S(1)} %fusion.9), channel_id=1, source_target_pairs={{0,16},{1,17},{2,18},{3,19},{4,20},{5,21},{6,22},{7,23},{8,24},{9,... | collective-permute-start | bytes 786440 | tf_op jit(solution)/shard_map/ppermute | solution.py:120
  100.8 11.1 %collective-permute-start.10 = (bf16[512,512]{1,0:T(8,128)(2,1)S(1)}, bf16[512,512]{1,0:T(8,128)(2,1)S(1)}, u32[]{:S(2)}, u32[]{:S(2)}) collective-permute-start(bf16[512,512]{1,0:T(8,128)(2,1)S(1)} %back.2), channel_id=1, source_target_pairs={{0,1},{1,0},{2,3},{3,2},{4,5},{5,4},{6,7},{7,6},{8,9},{9,8},{10,11... | collective-permute-start | bytes 1572872 | tf_op jit(solution)/shard_map/ppermute | solution.py:120

commit v10 on v9

--- a/solution.py
+++ b/solution.py
@@ -140,8 +140,12 @@
     cols = jnp.where(odd, quarters[:, None], quarters[None]).reshape(16, 4, 32, 128)
     offsets = (row + jnp.array([0, 3, 1, 2], jnp.int32)) % LINE * 128
     right = lax.dynamic_slice_in_dim(right_env[0], column % 2 * 256, 256, 1).reshape(2048, chi)
-    pair, blocks[3], local, two_site, cols, offsets, right = lax.optimization_barrier(
-        (pair, blocks[3], local, two_site, cols, offsets, right)
+    i = lax.broadcasted_iota(jnp.int32, (chi, chi), 0)
+    j = lax.broadcasted_iota(jnp.int32, (chi, chi), 1)
+    place = jnp.where(odd, i, i // 32 % 4 * 128 + i // 128 * 32 + i % 32)
+    place = (place == j).astype(BF)
+    pair, blocks[3], local, two_site, cols, offsets, right, place = lax.optimization_barrier(
+        (pair, blocks[3], local, two_site, cols, offsets, right, place)
     )
     up = moved(pair, along_column(1))
     down = moved(pair, along_column(-1))
@@ -170,11 +174,6 @@
     fresh = [fresh[i].astype(F32) for i in range(4)]
     fresh = ((fresh[0] + fresh[1]) + (fresh[2] + fresh[3])).astype(BF)
     source = fresh.transpose(2, 1, 0, 3).reshape(256, chi)
-    i = lax.broadcasted_iota(jnp.int32, (chi, chi), 0)
-    j = lax.broadcasted_iota(jnp.int32, (chi, chi), 1)
-    place = jnp.where(odd, i, i // 32 % 4 * 128 + i // 128 * 32 + i % 32)
-    place = (place == j).astype(BF)
-    source, place = lax.optimization_barrier((source, place))
     new_left = jnp.dot(source, place, preferred_element_type=F32).astype(BF).reshape(32, 8, chi)
     other = moved(source, lambda b: b ^ 1, 1)
     source = moved(source, lambda b: b, 1)

time: 114 us -> 118 us (1.035)
  the two profiles are of different devices: /device:TPU:2 before, /device:TPU:28 now
where the time goes in v10:
time: 118 us; the launch traced here: 117 us
  starting transfers between devices  51.2 us (43%)
  waiting for transfers between devices  26.7 us (23%)
  Pallas kernels  14.6 us (12%)
  local copies, waits for them, and re-layouts  14.2 us (12%)
  other arithmetic  7.12 us (6%)
  matrix products  2.18 us (2%)
    ppermute x11, starting transfers between devices, moved(): return lax.ppermute(block, ('sec', 'bond'), routed(sections, step, ahead))  29.6 us
    ppermute x11, waiting for transfers between devices, moved(): return lax.ppermute(block, ('sec', 'bond'), routed(sections, step, ahead))  22.3 us
    pallas_call x2, Pallas kernels, applied(): pl.pallas_call(back, out_shape=jax.ShapeDtypeStruct((512, 512), BF), in_s...  9.67 us
    all_to_all x1, starting transfers between devices, shards(): lax.all_to_all(fresh, 'bond', 0, 0, tiled=True).reshape(4, 4, 8, 32, 128)  9.26 us
    all_to_all x1, starting transfers between devices, shards(): cols = lax.all_to_all(cols, 'bond', 0, 0, tiled=True)  7.54 us
    pallas_call x1, Pallas kernels, shards(): pl.pallas_call(front, out_shape=jax.ShapeDtypeStruct((16, 8, 32, 128), BF...  4.95 us
    all_to_all x1, starting transfers between devices, shards(): lax.all_to_all(send, ('sec', 'bond'), 0, 0, axis_index_groups=lines, tile...  4.8 us
    all_to_all x1, waiting for transfers between devices, shards(): lax.all_to_all(send, ('sec', 'bond'), 0, 0, axis_index_groups=lines, tile...  3.32 us
  transfers between devices with their start and end apart: 14, of which 8 were waited for; matrix products, arithmetic and copies ran while one was open for 17% of the time, Pallas kernels for 13%

profile of v10, /device:TPU:28, one launch (start us, length us, event | category | flops | bytes accessed | tf_op | source)
XLA Modules:
  0.0 116.9 jit_solution(7175899276892428382)
XLA Ops:
  1.6 1.7 %pad_maximum_fusion.own = bf16[384,512]{1,0:T(8,128)(2,1)} fusion(bf16[128,512]{1,0:T(8,128)(2,1)S(1)} %reshape_squeeze.10, bf16[256,512]{1,0:T(8,128)(2,1)} %bitcast.50), kind=kLoop, calls=%fused_computation.22 | loop fusion | flops 786432 | bytes 786432 | tf_op jit(solution)/shard_map/concatenate | solution.py:127
  3.3 2.4 %collective-permute-start.3 = (bf16[384,512]{1,0:T(8,128)(2,1)}, bf16[384,512]{1,0:T(8,128)(2,1)}, u32[]{:S(2)}, u32[]{:S(2)}) collective-permute-start(bf16[384,512]{1,0:T(8,128)(2,1)} %pad_maximum_fusion.own), channel_id=1, source_target_pairs={{0,2},{1,3},{2,0},{3,1},{4,6},{5,7},{6,4},{7,5},{8,10},{9,11},{10,... | collective-permute-start | bytes 1179656 | tf_op jit(solution)/shard_map/ppermute | solution.py:120
  5.7 4.1 %collective-permute-start.2 = (bf16[384,512]{1,0:T(8,128)(2,1)}, bf16[384,512]{1,0:T(8,128)(2,1)S(1)}, u32[]{:S(2)}, u32[]{:S(2)}) collective-permute-start(bf16[384,512]{1,0:T(8,128)(2,1)} %pad_maximum_fusion.own), channel_id=1, source_target_pairs={{0,3},{1,0},{2,1},{3,2},{4,7},{5,4},{6,5},{7,6},{8,11},{9,8},{10,9... | collective-permute-start | bytes 1179656 | tf_op jit(solution)/shard_map/ppermute | solution.py:120
  9.8 1.9 %collective-permute-start.1 = (bf16[384,512]{1,0:T(8,128)(2,1)}, bf16[384,512]{1,0:T(8,128)(2,1)S(1)}, u32[]{:S(2)}, u32[]{:S(2)}) collective-permute-start(bf16[384,512]{1,0:T(8,128)(2,1)} %pad_maximum_fusion.own), channel_id=1, source_target_pairs={{0,1},{1,2},{2,3},{3,0},{4,5},{5,6},{6,7},{7,4},{8,9},{9,10},{10,1... | collective-permute-start | bytes 1179656 | tf_op jit(solution)/shard_map/ppermute | solution.py:120
  13.5 1.2 %reshape_squeeze.11 = bf16[32,4,4,4,32]{4,3,2,1,0:T(4,128)(2,1)S(1)} reshape(bf16[1,32,4,512]{3,2,1,0:T(4,128)(2,1)} %param.7) | data formatting | bytes 262144 | tf_op jit(solution)/shard_map/reshape;squeeze | solution.py:137
  16.3 1.2 %fusion = bf16[8,4,4,4,4,8]{5,0,1,3,2,4:T(8,128)(2,1)S(1)} fusion(bf16[8,8,4,4,1,1]{1,3,2,0,5,4:T(4,128)(2,1)} %bitcast.49), kind=kOutput, calls=%fused_computation.6 | convolution fusion | flops 278528 | bytes 34816 | tf_op jit(solution)/shard_map/mnsu,nkvw->kuwsvm/dot_general | solution.py:135
  19.7 9.0 %collective-permute-done = bf16[32,4,4,512]{3,2,1,0:T(4,128)(2,1)S(1)} collective-permute-done((bf16[32,4,4,512]{3,2,1,0:T(4,128)(2,1)}, bf16[32,4,4,512]{3,2,1,0:T(4,128)(2,1)S(1)}, u32[]{:S(2)}, u32[]{:S(2)}) %collective-permute-start) | collective-permute-done | bytes 524320 | tf_op jit(solution)/shard_map/ppermute | solution.py:120
  29.2 1.1 broadcast_in_dim.26
  30.3 4.8 %all-to-all-start = ((bf16[4,32,4096]{2,1,0:T(8,128)(2,1)}), bf16[4,32,4096]{2,1,0:T(8,128)(2,1)S(1)}, u32[]{:S(2)}, u32[]{:S(2)}) async-start(bf16[4,32,4096]{2,1,0:T(8,128)(2,1)} %bitcast.3), calls=%async_computation | async-start | bytes 2097152 | tf_op jit(solution)/shard_map/all_to_all | solution.py:133
  35.1 1.7 %constant_dynamic-slice_fusion = bf16[1,8,256,512]{3,2,1,0:T(8,128)(2,1)S(1)} fusion(bf16[1,8,512,512]{3,2,1,0:T(8,128)(2,1)} %param.9, s32[]{:T(128)S(6)} %select_n.105), kind=kLoop, calls=%fused_computation.48 | loop fusion | bytes 4194308 | tf_op jit(solution)/shard_map/dynamic_slice | solution.py:142
  37.7 2.0 %fusion.8 = bf16[512,512]{1,0:T(8,128)(2,1)} fusion(s32[512]{0:T(512)S(1)} %get-tuple-element.30, s32[512]{0:T(512)S(1)} %get-tuple-element.31, s32[512]{0:T(512)S(1)} %get-tuple-element.28, s32[512]{0:T(512)S(1)} %get-tuple-element.34, s32[512]{0:T(512)S(1)} %get-tuple-element.29, s32[512]{0:T(512)S(1)} %get-tuple-element.35, ...), kind=kLoop, calls=%fused_computation.17 | loop fusion | flops 5505024 | bytes 538113 | tf_op jit(solution)/shard_map/convert_element_type | solution.py:146
  39.7 3.3 %all-to-all-done = bf16[4,32,4096]{2,1,0:T(8,128)(2,1)S(1)} async-done(((bf16[4,32,4096]{2,1,0:T(8,128)(2,1)}), bf16[4,32,4096]{2,1,0:T(8,128)(2,1)S(1)}, u32[]{:S(2)}, u32[]{:S(2)}) %all-to-all-start) | async-done | bytes 1048608 | tf_op jit(solution)/shard_map/all_to_all | solution.py:133
  43.1 7.5 %all-to-all-start.1 = ((bf16[16,4,32,128]{3,2,1,0:T(8,128)(2,1)}), bf16[16,4,32,128]{3,2,1,0:T(8,128)(2,1)}, u32[]{:S(2)}, u32[]{:S(2)}) async-start(bf16[16,4,32,128]{3,2,1,0:T(8,128)(2,1)} %bitcast.46), calls=%async_computation.1 | async-start | bytes 1048576 | tf_op jit(solution)/shard_map/all_to_all | solution.py:155
  50.6 2.8 %collective-permute-start.7 = (bf16[128,4096]{1,0:T(8,128)(2,1)S(1)}, bf16[128,4096]{1,0:T(8,128)(2,1)}, u32[]{:S(2)}, u32[]{:S(2)}) collective-permute-start(bf16[128,4096]{1,0:T(8,128)(2,1)S(1)} %bitcast.41), channel_id=1, source_target_pairs={{0,12},{1,13},{2,14},{3,15},{4,0},{5,1},{6,2},{7,3},{8,4},{9,5},{1... | collective-permute-start | bytes 3145736 | tf_op jit(solution)/shard_map/ppermute | solution.py:120
  53.4 4.3 %collective-permute-start.6 = (bf16[128,4096]{1,0:T(8,128)(2,1)S(1)}, bf16[128,4096]{1,0:T(8,128)(2,1)}, u32[]{:S(2)}, u32[]{:S(2)}) collective-permute-start(bf16[128,4096]{1,0:T(8,128)(2,1)S(1)} %bitcast.42), channel_id=1, source_target_pairs={{0,4},{1,5},{2,6},{3,7},{4,8},{5,9},{6,10},{7,11},{8,12},{9,13},{1... | collective-permute-start | bytes 3145736 | tf_op jit(solution)/shard_map/ppermute | solution.py:120
  57.7 1.0 all-to-all-done.1.cols
  58.7 5.0 %front.1 = bf16[16,8,32,128]{3,2,1,0:T(8,128)(2,1)} custom-call(bf16[384,512]{1,0:T(8,128)(2,1)} %pad_maximum_fusion.own, bf16[384,512]{1,0:T(8,128)(2,1)} %copy-done.2, bf16[384,512]{1,0:T(8,128)(2,1)} %copy-done.1, bf16[384,512]{1,0:T(8,128)(2,1)} %collective-permute-done.3.far, bf16[16,4,32,128]{3,2,1,0:T(8,128)(2,1)} %all-to-all-done.1.cols, ...), custom_call_target="tpu_custom_call" | custom-call | flops 2000000000 | bytes 4000000 | tf_op jit(solution)/shard_map/front/pallas_call | solution.py:156
  63.7 9.3 %all-to-all-start.2 = ((bf16[16,8,32,128]{3,2,1,0:T(8,128)(2,1)}), bf16[16,8,32,128]{3,2,1,0:T(8,128)(2,1)}, u32[]{:S(2)}, u32[]{:S(2)}) async-start(bf16[16,8,32,128]{3,2,1,0:T(8,128)(2,1)} %front.1), calls=%async_computation.2 | async-start | bytes 2097152 | tf_op jit(solution)/shard_map/all_to_all | solution.py:172
  72.9 1.9 %collective-permute-done.7.down = bf16[128,4096]{1,0:T(8,128)(2,1)} collective-permute-done((bf16[128,4096]{1,0:T(8,128)(2,1)S(1)}, bf16[128,4096]{1,0:T(8,128)(2,1)}, u32[]{:S(2)}, u32[]{:S(2)}) %collective-permute-start.7) | collective-permute-done | bytes 1048608 | tf_op jit(solution)/shard_map/ppermute | solution.py:120
  74.8 1.9 %slice.29 = bf16[64,4096]{1,0:T(8,128)(2,1)} slice(bf16[128,4096]{1,0:T(8,128)(2,1)} %collective-permute-done.7.down), slice={[64:128], [0:4096]} | slice | bytes 1048576 | tf_op jit(solution)/shard_map/slice | solution.py:153
  76.7 2.3 %collective-permute-start.9 = (bf16[64,4096]{1,0:T(8,128)(2,1)}, bf16[64,4096]{1,0:T(8,128)(2,1)}, u32[]{:S(2)}, u32[]{:S(2)}) collective-permute-start(bf16[64,4096]{1,0:T(8,128)(2,1)} %slice.29), channel_id=1, source_target_pairs={{0,12},{1,13},{2,14},{3,15},{4,0},{5,1},{6,2},{7,3},{8,4},{9,5},{1... | collective-permute-start | bytes 1572872 | tf_op jit(solution)/shard_map/ppermute | solution.py:120
  79.1 1.9 %slice.28 = bf16[64,4096]{1,0:T(8,128)(2,1)} slice(bf16[128,4096]{1,0:T(8,128)(2,1)} %collective-permute-done.6.up), slice={[0:64], [0:4096]} | slice | bytes 1048576 | tf_op jit(solution)/shard_map/slice | solution.py:152
  80.9 6.8 %collective-permute-start.8 = (bf16[64,4096]{1,0:T(8,128)(2,1)}, bf16[64,4096]{1,0:T(8,128)(2,1)}, u32[]{:S(2)}, u32[]{:S(2)}) collective-permute-start(bf16[64,4096]{1,0:T(8,128)(2,1)} %slice.28), channel_id=1, source_target_pairs={{0,4},{1,5},{2,6},{3,7},{4,8},{5,9},{6,10},{7,11},{8,12},{9,13},{1... | collective-permute-start | bytes 1572872 | tf_op jit(solution)/shard_map/ppermute | solution.py:120
  87.7 2.1 %bitcast_select_fusion = bf16[4,4,8,32,128]{4,2,1,3,0:T(8,128)(2,1)S(1)} fusion(bf16[4,4,8,32,128]{4,3,2,1,0:T(8,128)(2,1)} %bitcast.13, pred[]{:T(512)S(6)} %eq.16), kind=kLoop, calls=%fused_computation.15 | loop fusion | flops 524288 | bytes 2097153 | tf_op jit(solution)/shard_map/jit(_where)/select_n | solution.py:173
  90.0 2.1 %collective-permute-start.5 = (bf16[256,512]{1,0:T(8,128)(2,1)S(1)}, bf16[256,512]{1,0:T(8,128)(2,1)S(1)}, u32[]{:S(2)}, u32[]{:S(2)}) collective-permute-start(bf16[256,512]{1,0:T(8,128)(2,1)S(1)} %fusion.9), channel_id=1, source_target_pairs={{0,20},{1,21},{2,22},{3,23},{4,16},{5,17},{6,18},{7,19},{8,28},{9,... | collective-permute-start | bytes 786440 | tf_op jit(solution)/shard_map/ppermute | solution.py:120
  92.1 2.6 %collective-permute-done.8.far_a = bf16[64,4096]{1,0:T(8,128)(2,1)} collective-permute-done((bf16[64,4096]{1,0:T(8,128)(2,1)}, bf16[64,4096]{1,0:T(8,128)(2,1)}, u32[]{:S(2)}, u32[]{:S(2)}) %collective-permute-start.8) | collective-permute-done | bytes 524320 | tf_op jit(solution)/shard_map/ppermute | solution.py:120
  94.7 5.2 %collective-permute-done.5.left = bf16[256,512]{1,0:T(8,128)(2,1)S(1)} collective-permute-done((bf16[256,512]{1,0:T(8,128)(2,1)S(1)}, bf16[256,512]{1,0:T(8,128)(2,1)S(1)}, u32[]{:S(2)}, u32[]{:S(2)}) %collective-permute-start.5) | collective-permute-done | bytes 262176 | tf_op jit(solution)/shard_map/ppermute | solution.py:120
  99.9 4.8 %back.2 = bf16[512,512]{1,0:T(8,128)(2,1)S(1)} custom-call(s32[4]{0:T(128)S(1)} %fusion.22.offsets, bf16[256,512]{1,0:T(8,128)(2,1)S(1)} %collective-permute-done.5.left, bf16[128,4096]{1,0:T(8,128)(2,1)S(1)} %bitcast.43, bf16[128,4096]{1,0:T(8,128)(2,1)} %collective-permute-done.6.up, bf16[128,4096]{1,0:T(8,128)(2,1)} %collective-permute-done.7.down, ...), custom_call_target="tpu_custom_call" | custom-call | flops 2500000000 | bytes 8000000 | tf_op jit(solution)/shard_map/back/pallas_call | solution.py:99
  104.8 2.2 %collective-permute-start.10 = (bf16[512,512]{1,0:T(8,128)(2,1)S(1)}, bf16[512,512]{1,0:T(8,128)(2,1)S(1)}, u32[]{:S(2)}, u32[]{:S(2)}) collective-permute-start(bf16[512,512]{1,0:T(8,128)(2,1)S(1)} %back.2), channel_id=1, source_target_pairs={{0,1},{1,0},{2,3},{3,2},{4,5},{5,4},{6,7},{7,6},{8,9},{9,8},{10,11... | collective-permute-start | bytes 1572872 | tf_op jit(solution)/shard_map/ppermute | solution.py:120
  107.0 1.0 fusion.1
  108.0 4.8 %back.3 = bf16[512,512]{1,0:T(8,128)(2,1)S(1)} custom-call(s32[4]{0:T(128)S(1)} %fusion.22.offsets, bf16[256,512]{1,0:T(8,128)(2,1)S(1)} %collective-permute-done.4.left, bf16[128,4096]{1,0:T(8,128)(2,1)S(1)} %bitcast.44, bf16[128,4096]{1,0:T(8,128)(2,1)} %collective-permute-done.6.up, bf16[128,4096]{1,0:T(8,128)(2,1)} %collective-permute-done.7.down, ...), custom_call_target="tpu_custom_call" | custom-call | flops 2500000000 | bytes 8000000 | tf_op jit(solution)/shard_map/back/pallas_call | solution.py:99
  112.9 3.0 %collective-permute-done.10 = bf16[512,512]{1,0:T(8,128)(2,1)S(1)} collective-permute-done((bf16[512,512]{1,0:T(8,128)(2,1)S(1)}, bf16[512,512]{1,0:T(8,128)(2,1)S(1)}, u32[]{:S(2)}, u32[]{:S(2)}) %collective-permute-start.10) | collective-permute-done | bytes 524320 | tf_op jit(solution)/shard_map/ppermute | solution.py:120
  (40 shorter events, 8.9 us)
Async XLA Ops:
  0.6 18.5 %copy-start.3 = (s32[4]{0:T(128)S(1)}, s32[4]{0:T(128)}, u32[]{:S(2)}) copy-start(s32[4]{0:T(128)} %constant.118.clone) | copy-start | bytes 52
  3.3 36.4 %collective-permute-start.3 = (bf16[384,512]{1,0:T(8,128)(2,1)}, bf16[384,512]{1,0:T(8,128)(2,1)}, u32[]{:S(2)}, u32[]{:S(2)}) collective-permute-start(bf16[384,512]{1,0:T(8,128)(2,1)} %pad_maximum_fusion.own), channel_id=1, source_target_pairs={{0,2},{1,3},{2,0},{3,1},{4,6},{5,7},{6,4},{7,5},{8,10},{9,11},{10,... | collective-permute-start | bytes 1179656 | tf_op jit(solution)/shard_map/ppermute | solution.py:120
  5.7 13.4 %collective-permute-start.2 = (bf16[384,512]{1,0:T(8,128)(2,1)}, bf16[384,512]{1,0:T(8,128)(2,1)S(1)}, u32[]{:S(2)}, u32[]{:S(2)}) collective-permute-start(bf16[384,512]{1,0:T(8,128)(2,1)} %pad_maximum_fusion.own), channel_id=1, source_target_pairs={{0,3},{1,0},{2,1},{3,2},{4,7},{5,4},{6,5},{7,6},{8,11},{9,8},{10,9... | collective-permute-start | bytes 1179656 | tf_op jit(solution)/shard_map/ppermute | solution.py:120
  9.8 9.9 %collective-permute-start.1 = (bf16[384,512]{1,0:T(8,128)(2,1)}, bf16[384,512]{1,0:T(8,128)(2,1)S(1)}, u32[]{:S(2)}, u32[]{:S(2)}) collective-permute-start(bf16[384,512]{1,0:T(8,128)(2,1)} %pad_maximum_fusion.own), channel_id=1, source_target_pairs={{0,1},{1,2},{2,3},{3,0},{4,5},{5,6},{6,7},{7,4},{8,9},{9,10},{10,1... | collective-permute-start | bytes 1179656 | tf_op jit(solution)/shard_map/ppermute | solution.py:120
  11.7 17.0 %collective-permute-start = (bf16[32,4,4,512]{3,2,1,0:T(4,128)(2,1)}, bf16[32,4,4,512]{3,2,1,0:T(4,128)(2,1)S(1)}, u32[]{:S(2)}, u32[]{:S(2)}) collective-permute-start(bf16[32,4,4,512]{3,2,1,0:T(4,128)(2,1)} %bitcast.51), channel_id=1, source_target_pairs={{0,16},{1,17},{2,18},{3,19},{4,20},{5,21},{6,22},{7,23},{8,24},{9,... | collective-permute-start | bytes 1572872 | tf_op jit(solution)/shard_map/ppermute | solution.py:120
  19.1 11.2 %copy-start.1 = (bf16[384,512]{1,0:T(8,128)(2,1)}, bf16[384,512]{1,0:T(8,128)(2,1)S(1)}, u32[]{:S(2)}) copy-start(bf16[384,512]{1,0:T(8,128)(2,1)S(1)} %collective-permute-done.2.back_) | copy-start | bytes 1179652
  19.7 10.7 %copy-start.2 = (bf16[384,512]{1,0:T(8,128)(2,1)}, bf16[384,512]{1,0:T(8,128)(2,1)S(1)}, u32[]{:S(2)}) copy-start(bf16[384,512]{1,0:T(8,128)(2,1)S(1)} %collective-permute-done.1.near) | copy-start | bytes 1179652
  30.3 12.7 %all-to-all-start = ((bf16[4,32,4096]{2,1,0:T(8,128)(2,1)}), bf16[4,32,4096]{2,1,0:T(8,128)(2,1)S(1)}, u32[]{:S(2)}, u32[]{:S(2)}) async-start(bf16[4,32,4096]{2,1,0:T(8,128)(2,1)} %bitcast.3), calls=%async_computation | async-start | bytes 2097152 | tf_op jit(solution)/shard_map/all_to_all | solution.py:133
  43.1 15.6 %all-to-all-start.1 = ((bf16[16,4,32,128]{3,2,1,0:T(8,128)(2,1)}), bf16[16,4,32,128]{3,2,1,0:T(8,128)(2,1)}, u32[]{:S(2)}, u32[]{:S(2)}) async-start(bf16[16,4,32,128]{3,2,1,0:T(8,128)(2,1)} %bitcast.46), calls=%async_computation.1 | async-start | bytes 1048576 | tf_op jit(solution)/shard_map/all_to_all | solution.py:155
  50.6 24.2 %collective-permute-start.7 = (bf16[128,4096]{1,0:T(8,128)(2,1)S(1)}, bf16[128,4096]{1,0:T(8,128)(2,1)}, u32[]{:S(2)}, u32[]{:S(2)}) collective-permute-start(bf16[128,4096]{1,0:T(8,128)(2,1)S(1)} %bitcast.41), channel_id=1, source_target_pairs={{0,12},{1,13},{2,14},{3,15},{4,0},{5,1},{6,2},{7,3},{8,4},{9,5},{1... | collective-permute-start | bytes 3145736 | tf_op jit(solution)/shard_map/ppermute | solution.py:120
  53.4 25.7 %collective-permute-start.6 = (bf16[128,4096]{1,0:T(8,128)(2,1)S(1)}, bf16[128,4096]{1,0:T(8,128)(2,1)}, u32[]{:S(2)}, u32[]{:S(2)}) collective-permute-start(bf16[128,4096]{1,0:T(8,128)(2,1)S(1)} %bitcast.42), channel_id=1, source_target_pairs={{0,4},{1,5},{2,6},{3,7},{4,8},{5,9},{6,10},{7,11},{8,12},{9,13},{1... | collective-permute-start | bytes 3145736 | tf_op jit(solution)/shard_map/ppermute | solution.py:120
  63.7 24.0 %all-to-all-start.2 = ((bf16[16,8,32,128]{3,2,1,0:T(8,128)(2,1)}), bf16[16,8,32,128]{3,2,1,0:T(8,128)(2,1)}, u32[]{:S(2)}, u32[]{:S(2)}) async-start(bf16[16,8,32,128]{3,2,1,0:T(8,128)(2,1)} %front.1), calls=%async_computation.2 | async-start | bytes 2097152 | tf_op jit(solution)/shard_map/all_to_all | solution.py:172
  76.7 15.4 %collective-permute-start.9 = (bf16[64,4096]{1,0:T(8,128)(2,1)}, bf16[64,4096]{1,0:T(8,128)(2,1)}, u32[]{:S(2)}, u32[]{:S(2)}) collective-permute-start(bf16[64,4096]{1,0:T(8,128)(2,1)} %slice.29), channel_id=1, source_target_pairs={{0,12},{1,13},{2,14},{3,15},{4,0},{5,1},{6,2},{7,3},{8,4},{9,5},{1... | collective-permute-start | bytes 1572872 | tf_op jit(solution)/shard_map/ppermute | solution.py:120
  80.9 13.8 %collective-permute-start.8 = (bf16[64,4096]{1,0:T(8,128)(2,1)}, bf16[64,4096]{1,0:T(8,128)(2,1)}, u32[]{:S(2)}, u32[]{:S(2)}) collective-permute-start(bf16[64,4096]{1,0:T(8,128)(2,1)} %slice.28), channel_id=1, source_target_pairs={{0,4},{1,5},{2,6},{3,7},{4,8},{5,9},{6,10},{7,11},{8,12},{9,13},{1... | collective-permute-start | bytes 1572872 | tf_op jit(solution)/shard_map/ppermute | solution.py:120
  90.0 17.0 %copy-start = (bf16[512,512]{1,0:T(8,128)(2,1)S(1)}, bf16[512,512]{1,0:T(8,128)(2,1)}, u32[]{:S(2)}) copy-start(bf16[512,512]{1,0:T(8,128)(2,1)} %fusion.8) | copy-start | bytes 1572868
  90.0 9.9 %collective-permute-start.5 = (bf16[256,512]{1,0:T(8,128)(2,1)S(1)}, bf16[256,512]{1,0:T(8,128)(2,1)S(1)}, u32[]{:S(2)}, u32[]{:S(2)}) collective-permute-start(bf16[256,512]{1,0:T(8,128)(2,1)S(1)} %fusion.9), channel_id=1, source_target_pairs={{0,20},{1,21},{2,22},{3,23},{4,16},{5,17},{6,18},{7,19},{8,28},{9,... | collective-permute-start | bytes 786440 | tf_op jit(solution)/shard_map/ppermute | solution.py:120
  92.1 12.7 %collective-permute-start.4 = (bf16[256,512]{1,0:T(8,128)(2,1)S(1)}, bf16[256,512]{1,0:T(8,128)(2,1)S(1)}, u32[]{:S(2)}, u32[]{:S(2)}) collective-permute-start(bf16[256,512]{1,0:T(8,128)(2,1)S(1)} %fusion.9), channel_id=1, source_target_pairs={{0,16},{1,17},{2,18},{3,19},{4,20},{5,21},{6,22},{7,23},{8,24},{9,... | collective-permute-start | bytes 786440 | tf_op jit(solution)/shard_map/ppermute | solution.py:120
  104.8 11.1 %collective-permute-start.10 = (bf16[512,512]{1,0:T(8,128)(2,1)S(1)}, bf16[512,512]{1,0:T(8,128)(2,1)S(1)}, u32[]{:S(2)}, u32[]{:S(2)}) collective-permute-start(bf16[512,512]{1,0:T(8,128)(2,1)S(1)} %back.2), channel_id=1, source_target_pairs={{0,1},{1,0},{2,3},{3,2},{4,5},{5,4},{6,7},{7,6},{8,9},{9,8},{10,11... | collective-permute-start | bytes 1572872 | tf_op jit(solution)/shard_map/ppermute | solution.py:120
